TPU v7x, 32 devices: a whole 2x2x4 slice. The times are simulated.
32 devices in a mesh: groups: 2 (over y), state: 4 (over z), type: 4 (over x, core).
Axes of the slice: x: 2, y: 2, z: 4, core: 2. Of those that a mesh axis runs over, the one named last changes fastest.
Arguments:
- value_in: bfloat16 [16384, 2048], P(('groups', 'state'), 'type'), parts along dimension 0, may hold values from -7.5 to 7.5
- cotangent: bfloat16 [16384, 2048], P(('groups', 'state'), 'type'), parts along dimension 0, may hold values from -100 to 100
- state_util: float32 [2, 16384], P(None, ('groups', 'state')), parts along dimension 1, may hold values from -300 to 300
- taste: float32 [2, 4096], P(None, ('groups', 'type')), parts along dimension 1, may hold values from -6 to 6
- tiles: bfloat16 [128, 2, 6, 128, 128], P(('groups', 'state')), parts along dimension 0, may hold values from 0 to 0.0051879883
- dest_block: int32 [128, 2, 6], P(('groups', 'state')), parts along dimension 0, may hold values from 0 to 63, as said below
- counts: int32 [128, 2], P(('groups', 'state')), parts along dimension 0, may hold values from 1 to 6
Outputs:
- value_out: float32 [16384, 2048], P(('groups', 'state'), 'type'), parts along dimension 0
- adjoint: float32 [16384, 2048], P(('groups', 'state'), 'type'), parts along dimension 0
- grad_util: float32 [2, 16384], P(None, ('groups', 'state')), parts along dimension 1
- grad_taste: float32 [2, 4096], P(None, ('groups', 'type')), parts along dimension 1
There are 2 independent parts, one for each index of `groups`. A program takes and returns all parts, laid end to end along the dimension named above; each array names one. Nothing has to cross between parts.
Inputs may be any that keep to these rules, and one draw needn't show every extreme that they name: `dest_block`: entries at or beyond a list's count name blocks of the list's own run of 16 blocks. In each run of 16 blocks exactly 16 used entries name blocks outside the run, at most 6 of them in any one other run, and exactly 6 in some other run.
All inputs are finite; a program needn't handle non-finite values.
Results may differ from a plain program's by a relative error of at most 0.0012.
Values may be sent and summed in bfloat16 or wider, within the bound.
No kernel may reach another device: no remote copies, remote signals or barrier semaphores. Data moves between devices by JAX's collectives and lax.ppermute only.
A program may use at most 192 MiB of HBM per device.

v0:
```python
import jax
import jax.numpy as jnp
from jax import lax
from jax.sharding import PartitionSpec as P


def local(value_in, cotangent, state_util, taste, tiles, dest_block, counts):
    block_count, action_count, entry_count, tile_rows, _ = tiles.shape
    type_width = value_in.shape[1]
    device_count = lax.axis_size("state")
    my_index = lax.axis_index("state")
    capacity = max(2, (block_count + device_count - 2) // (device_count - 1))
    entry_total = block_count * action_count * entry_count
    value_blocks = value_in.reshape(block_count, tile_rows, type_width)
    flat_dest = dest_block.reshape(entry_total)
    owner = flat_dest // block_count
    local_block = flat_dest % block_count
    used = (jnp.arange(entry_count, dtype=jnp.int32)[None, None, :] < counts[:, :, None]).reshape(
        entry_total
    )
    remote = used & (owner != my_index)
    local_used = used & (owner == my_index)
    peer_ids = jnp.arange(device_count, dtype=jnp.int32)
    owner_hits = (remote[:, None] & (owner[:, None] == peer_ids[None, :])).astype(jnp.int32)
    earlier = jnp.cumsum(owner_hits, axis=0) - owner_hits
    slot_of = jnp.sum(earlier * owner_hits, axis=1)
    target = jnp.where(remote, owner * capacity + slot_of, device_count * capacity)
    request = (
        jnp.full((device_count * capacity,), -1, jnp.int32).at[target].set(local_block, mode="drop")
    )
    source_entry = (
        jnp.full((device_count * capacity,), -1, jnp.int32)
        .at[target]
        .set(jnp.arange(entry_total, dtype=jnp.int32), mode="drop")
    )
    wanted = lax.all_to_all(
        request.reshape(device_count, capacity), "state", split_axis=0, concat_axis=0, tiled=True
    )
    outgoing = jnp.take(value_blocks, jnp.clip(wanted.reshape(-1), 0, block_count - 1), axis=0)
    incoming = lax.all_to_all(
        outgoing.reshape(device_count, capacity, tile_rows, type_width),
        "state",
        split_axis=0,
        concat_axis=0,
        tiled=True,
    )
    table = jnp.concatenate(
        [value_blocks, incoming.reshape(device_count * capacity, tile_rows, type_width)], axis=0
    )
    lookup = jnp.where(remote, block_count + target, local_block)
    picked = jnp.take(table, lookup, axis=0)
    picked = jnp.where(used[:, None, None], picked, jnp.zeros_like(picked))
    picked = picked.reshape(block_count, action_count, entry_count, tile_rows, type_width)
    cont = jnp.einsum("bamij,bamjk->baik", tiles, picked, preferred_element_type=jnp.float32)
    util_grid = state_util.reshape(action_count, block_count, tile_rows).transpose(1, 0, 2)[
        :, :, :, None
    ]
    scores = util_grid + taste[None, :, None, :] + 0.95 * cont
    largest = jnp.max(scores, axis=1)
    value = largest + jnp.log(jnp.sum(jnp.exp(scores - largest[:, None]), axis=1))
    prob = jnp.exp(scores - value[:, None])
    grad_q = cotangent.reshape(block_count, 1, tile_rows, type_width).astype(jnp.float32) * prob
    util_part = (
        jnp.sum(grad_q, axis=3).transpose(1, 0, 2).reshape(action_count, block_count * tile_rows)
    )
    util_total = lax.psum(util_part, "type") / (type_width * lax.axis_size("type"))
    taste_total = lax.psum(jnp.sum(grad_q, axis=(0, 2)), "state") / (
        block_count * tile_rows * device_count
    )
    scaled = (0.95 * grad_q).astype(jnp.bfloat16)
    slot_valid = source_entry >= 0
    safe_entry = jnp.clip(source_entry, 0, entry_total - 1)
    contrib = jnp.einsum(
        "bamij,baik->bamjk", tiles, scaled, preferred_element_type=jnp.float32
    ).reshape(entry_total, tile_rows, type_width)
    outbound = jnp.where(
        slot_valid[:, None, None], jnp.take(contrib, safe_entry, axis=0), 0.0
    ).astype(jnp.bfloat16)
    returned = lax.all_to_all(
        outbound.reshape(device_count, capacity, tile_rows, type_width),
        "state",
        split_axis=0,
        concat_axis=0,
        tiled=True,
    )
    block_ids = jnp.arange(block_count, dtype=jnp.int32)
    local_select = (local_used[:, None] & (local_block[:, None] == block_ids[None, :])).astype(
        jnp.float32
    )
    own_terms = jnp.einsum("rd,rjk->djk", local_select, contrib, precision=lax.Precision.HIGHEST)
    arrive_select = (wanted.reshape(-1)[None, :] == block_ids[:, None]).astype(jnp.bfloat16)
    arrived = jnp.dot(
        arrive_select,
        returned.reshape(device_count * capacity, tile_rows * type_width),
        preferred_element_type=jnp.float32,
    )
    adjoint = own_terms + arrived.reshape(block_count, tile_rows, type_width)
    value_out = value.reshape(block_count * tile_rows, type_width)
    return (
        value_out,
        adjoint.reshape(block_count * tile_rows, type_width),
        util_total,
        taste_total,
    )


def solution(mesh):
    return jax.shard_map(
        local,
        mesh=mesh,
        in_specs=(
            P(("groups", "state"), "type"),
            P(("groups", "state"), "type"),
            P(None, ("groups", "state")),
            P(None, ("groups", "type")),
            P(("groups", "state"), None, None, None, None),
            P(("groups", "state"), None, None),
            P(("groups", "state"), None),
        ),
        out_specs=(
            P(("groups", "state"), "type"),
            P(("groups", "state"), "type"),
            P(None, ("groups", "state")),
            P(None, ("groups", "type")),
        ),
        check_vma=False,
    )
```

profile of v0, /device:TPU:0, one launch (start us, length us, event | category | flops | bytes accessed | tf_op | source)
XLA Modules:
  0.0 337.8 jit_solution(11441029719686296648)
XLA Ops:
  0.6 0.8 copy.37
  1.4 0.1 iota_compare_fusion.1
  1.5 0.1 lt.106
  1.6 0.1 lt.109
  1.7 0.8 copy.38
  2.5 0.1 reshape.392
  2.6 0.1 reshape.396
  2.8 1.2 reduce-window.6
  4.1 0.1 copy.43
  4.3 0.1 copy.44
  4.5 1.2 scatter_custom_fusion
  5.7 0.1 all_to_all.12
  5.8 11.7 %all_to_all.19 = s32[4,1,6]{2,1,0:T(1,128)S(1)} all-to-all(s32[4,1,6]{2,1,0:T(1,128)S(1)} %bitcast.86), channel_id=1, replica_groups=mesh['groups'=2,'state'=4,'type'=4] {'state'}, dimensions={0} | all-to-all | bytes 192 | tf_op jit(solution)/shard_map/all_to_all | solution.py:36
  17.4 0.5 broadcast.505
  18.0 0.7 fusion.47
  18.6 0.1 min.24
  18.7 2.3 gather_fusion
  21.1 2.0 broadcast_select_fusion
  23.1 4.8 %all-to-all-start.1 = ((bf16[4,6,128,512]{3,2,1,0:T(8,128)(2,1)}), bf16[4,6,128,512]{3,2,1,0:T(8,128)(2,1)}, u32[]{:S(2)}, u32[]{:S(2)}) async-start(bf16[4,6,128,512]{3,2,1,0:T(8,128)(2,1)} %broadcast_select_fusion), calls=%async_computation.1 | async-start | bytes 6291456 | tf_op jit(solution)/shard_map/all_to_all | solution.py:40
  27.9 0.1 reduce_sum.41
  28.0 1.4 scatter_custom_fusion.1
  29.4 0.1 broadcast_in_dim.91
  29.5 0.1 broadcast_in_dim.89
  29.6 4.1 %copy.49 = f32[16,128,512]{1,2,0:T(8,128)} copy(bf16[16,128,512]{2,1,0:T(8,128)(2,1)} %bitcast.81) | data formatting | bytes 6291456 | tf_op jit(solution)/shard_map/convert_element_type | solution.py:62
  33.7 0.1 compare_and_fusion
  33.8 63.7 %all-to-all-done.1 = bf16[4,6,128,512]{3,2,1,0:T(8,128)(2,1)} async-done(((bf16[4,6,128,512]{3,2,1,0:T(8,128)(2,1)}), bf16[4,6,128,512]{3,2,1,0:T(8,128)(2,1)}, u32[]{:S(2)}, u32[]{:S(2)}) %all-to-all-start.1) | async-done | bytes 3145760 | tf_op jit(solution)/shard_map/all_to_all | solution.py:40
  97.5 4.7 %pad_maximum_fusion = bf16[40,128,512]{2,1,0:T(8,128)(2,1)} fusion(bf16[24,128,512]{2,1,0:T(8,128)(2,1)} %bitcast.11, bf16[16,128,512]{2,1,0:T(8,128)(2,1)S(1)} %bitcast.75), kind=kLoop, calls=%fused_computation.20 | loop fusion | flops 2621440 | bytes 10485760 | tf_op jit(solution)/shard_map/concatenate | solution.py:47
  102.2 13.5 %gather_fusion.1 = bf16[192,128,512]{2,1,0:T(8,128)(2,1)} fusion(bf16[40,128,512]{2,1,0:T(8,128)(2,1)} %pad_maximum_fusion, s32[1024]{0:T(1024)S(1)} %pad_clamp_fusion.1), kind=kCustom, calls=%fused_computation.1 | custom fusion | bytes 50332416 | tf_op jit(solution)/shard_map/jit(_take)/gather | solution.py:51
  115.8 32.6 %copy.47 = bf16[16,2,6,128,512]{3,4,2,1,0:T(8,128)(2,1)} copy(bf16[16,2,6,128,512]{4,3,2,1,0:T(8,128)(2,1)} %bitcast.73) | data formatting | bytes 50331648 | tf_op jit(solution)/shard_map/jit(_take)/gather | solution.py:51
  148.3 15.0 %fusion.48 = (f32[16,128,512]{1,2,0:T(8,128)}, f32[16,2,128,512]{2,3,1,0:T(8,128)S(1)}) fusion(bf16[16,2,6,128,128]{4,3,2,1,0:T(8,128)(2,1)} %param.11, bf16[16,2,6,128,512]{3,4,2,1,0:T(8,128)(2,1)} %copy.47, pred[16,2,6]{2,1,0:T(4,128)(4,1)S(1)} %compare_and_fusion, pred[16,2,6]{2,1,0:T(4,128)(4,1)S(1)} %iota_compare_fusion.1, ...), kind=kOutput, calls=%fused_computation.102 | convolution fusion | flops 3253731328 | bytes 44061056 | tf_op jit(solution)/shard_map/bamij,bamjk->baik/dot_general | solution.py:54
  163.3 9.7 %exponential_reduce_fusion = f32[16,128,512]{1,2,0:T(8,128)} fusion(f32[16,2,128,512]{2,3,1,0:T(8,128)S(1)} %get-tuple-element.17, f32[16,128,512]{1,2,0:T(8,128)} %get-tuple-element.16), kind=kLoop, calls=%fused_computation.16 | loop fusion | flops 3145728 | bytes 16777216 | tf_op jit(solution)/shard_map/reduce_sum | solution.py:60
  173.0 6.0 %log_add_fusion = f32[16,128,512]{1,2,0:T(8,128)} fusion(f32[16,128,512]{1,2,0:T(8,128)} %get-tuple-element.16, f32[16,128,512]{1,2,0:T(8,128)} %exponential_reduce_fusion), kind=kLoop, calls=%fused_computation.26 | loop fusion | flops 1048576 | bytes 12582912 | tf_op jit(solution)/shard_map/add | solution.py:60
  179.0 24.5 %fusion.10 = f32[16,2,512,6,128]{4,2,3,1,0:T(8,128)} fusion(bf16[16,2,6,128,128]{4,3,2,1,0:T(8,128)(2,1)} %param.11, f32[16,2,128,512]{2,3,1,0:T(8,128)} %copy-done, f32[16,128,512]{1,2,0:T(8,128)} %log_add_fusion, f32[16,128,512]{1,2,0:T(8,128)} %copy.49), kind=kOutput, calls=%fused_computation.22 | convolution fusion | flops 3229614080 | bytes 73400320 | tf_op jit(solution)/shard_map/bamij,baik->bamjk/dot_general | solution.py:73
  203.5 4.4 %gather_fusion.2 = bf16[24,128,512]{1,2,0:T(8,128)(2,1)S(1)} fusion(f32[192,128,512]{1,2,0:T(8,128)} %bitcast.71, s32[1024]{0:T(1024)S(1)} %pad_clamp_fusion), kind=kCustom, calls=%fused_computation.2 | custom fusion | bytes 6291552 | tf_op jit(solution)/shard_map/jit(_take)/gather | solution.py:77
  207.9 2.8 copy.51
  210.7 5.0 %select_convert_fusion = bf16[4,6,128,512]{3,2,1,0:T(8,128)(2,1)} fusion(bf16[4,6,128,512]{3,2,1,0:T(8,128)(2,1)} %bitcast.78, pred[4,6]{1,0:T(4,128)(4,1)S(1)} %broadcast_in_dim.91, pred[4,6]{1,0:T(4,128)(4,1)S(1)} %broadcast_in_dim.89), kind=kLoop, calls=%fused_computation.17 | loop fusion | flops 3145728 | bytes 6291504 | tf_op jit(solution)/shard_map/convert_element_type | solution.py:78
  215.7 3.7 %all-to-all-start.2 = ((bf16[4,6,128,512]{3,2,1,0:T(8,128)(2,1)}), bf16[4,6,128,512]{3,2,1,0:T(8,128)(2,1)S(1)}, u32[]{:S(2)}, u32[]{:S(2)}) async-start(bf16[4,6,128,512]{3,2,1,0:T(8,128)(2,1)} %select_convert_fusion), calls=%async_computation.2 | async-start | bytes 6291456 | tf_op jit(solution)/shard_map/all_to_all | solution.py:79
  219.4 0.1 reshape.399
  219.5 5.3 %copy.48 = f32[16,128,512]{2,1,0:T(8,128)} copy(f32[16,128,512]{1,2,0:T(8,128)} %log_add_fusion) | data formatting | bytes 8388608 | tf_op jit(solution)/shard_map/add | solution.py:60
  224.8 49.2 %copy.50 = f32[192,128,512]{2,0,1:T(8,128)} copy(f32[192,128,512]{1,2,0:T(8,128)} %bitcast.72) | data formatting | bytes 100663296 | tf_op jit(solution)/shard_map/reshape | solution.py:75
  274.0 7.5 %fusion.7 = (f32[2,512]{1,0:T(2,128)S(1)}, f32[16,2,128]{2,1,0:T(2,128)S(1)}) fusion(f32[16,2,128,512]{2,3,1,0:T(8,128)} %copy-done, f32[16,128,512]{1,2,0:T(8,128)} %log_add_fusion, f32[16,128,512]{1,2,0:T(8,128)} %copy.49), kind=kLoop, calls=%fused_computation.18 | loop fusion | flops 8383488 | bytes 16797696 | tf_op jit(solution)/shard_map/reduce_sum | solution.py:67
  281.5 12.2 %psum.15 = f32[2,512]{1,0:T(2,128)S(1)} all-reduce(f32[2,512]{1,0:T(2,128)S(1)} %get-tuple-element.4), channel_id=1, replica_groups=mesh['groups'=2,'state'=4,'type'=4] {'state'}, use_global_device_ids=true, to_apply=%region_10.11 | all-reduce | flops 1024 | bytes 8192 | tf_op jit(solution)/shard_map/psum | solution.py:67
  293.7 10.1 %psum.14 = f32[2,2048]{1,0:T(2,128)S(1)} all-reduce(f32[2,2048]{1,0:T(2,128)S(1)} %bitcast.82), channel_id=1, replica_groups=mesh['groups'=2,'state'=4,'type'=4] {'type'}, use_global_device_ids=true, to_apply=%region_8.9 | all-reduce | flops 4096 | bytes 32768 | tf_op jit(solution)/shard_map/psum | solution.py:66
  303.8 0.6 broadcast_multiply_fusion.1
  304.4 0.6 broadcast_multiply_fusion
  305.0 23.2 %fusion.26 = f32[16,128,512]{2,0,1:T(8,128)} fusion(f32[192,128,512]{2,0,1:T(8,128)} %copy.50, s32[192]{0:T(256)S(1)} %and_select_fusion.4, pred[192]{0:T(512)(128)(4,1)S(1)} %get-tuple-element.10), kind=kOutput, calls=%fused_computation.45 | convolution fusion | flops 2415925248 | bytes 54526912 | tf_op jit(solution)/shard_map/rd,rjk->djk/dot_general | solution.py:90
  328.2 5.1 %fusion.20 = f32[16,128,512]{2,0,1:T(8,128)S(1)} fusion(f32[16,128,512]{2,0,1:T(8,128)} %fusion.26, s32[24]{0:T(128)S(1)} %reshape.399, bf16[3,8,128,512]{3,2,1,0:T(8,128)(2,1)S(1)} %bitcast.77), kind=kOutput, calls=%fused_computation.31 | convolution fusion | flops 51380608 | bytes 11534432 | tf_op jit(solution)/shard_map/dot_general | solution.py:92
  333.3 4.4 %copy.53 = f32[16,128,512]{2,1,0:T(8,128)} copy(f32[16,128,512]{2,0,1:T(8,128)S(1)} %fusion.20) | data formatting | bytes 8388608 | tf_op jit(solution)/shard_map/add | solution.py:97
  (30 shorter events, 0.4 us)
Async XLA Ops:
  23.1 74.4 %copy-start.1 = (bf16[2048,512]{1,0:T(8,128)(2,1)S(1)}, bf16[2048,512]{1,0:T(8,128)(2,1)}, u32[]{:S(2)}) copy-start(bf16[2048,512]{1,0:T(8,128)(2,1)} %param.7) | copy-start | bytes 6291460
  23.1 74.4 %all-to-all-start.1 = ((bf16[4,6,128,512]{3,2,1,0:T(8,128)(2,1)}), bf16[4,6,128,512]{3,2,1,0:T(8,128)(2,1)}, u32[]{:S(2)}, u32[]{:S(2)}) async-start(bf16[4,6,128,512]{3,2,1,0:T(8,128)(2,1)} %broadcast_select_fusion), calls=%async_computation.1 | async-start | bytes 6291456 | tf_op jit(solution)/shard_map/all_to_all | solution.py:40
  115.8 32.6 %copy-start.2 = (f32[2,2048]{1,0:T(2,128)S(1)}, f32[2,2048]{1,0:T(2,128)}, u32[]{:S(2)}) copy-start(f32[2,2048]{1,0:T(2,128)} %param.9) | copy-start | bytes 49156
  115.8 32.6 %copy-start.3 = (f32[2,512]{1,0:T(2,128)S(1)}, f32[2,512]{1,0:T(2,128)}, u32[]{:S(2)}) copy-start(f32[2,512]{1,0:T(2,128)} %param.10) | copy-start | bytes 12292
  163.3 9.7 %copy-start = (f32[16,2,128,512]{2,3,1,0:T(8,128)}, f32[16,2,128,512]{2,3,1,0:T(8,128)S(1)}, u32[]{:S(2)}) copy-start(f32[16,2,128,512]{2,3,1,0:T(8,128)S(1)} %get-tuple-element.17) | copy-start | bytes 25165828
  215.7 112.5 %all-to-all-start.2 = ((bf16[4,6,128,512]{3,2,1,0:T(8,128)(2,1)}), bf16[4,6,128,512]{3,2,1,0:T(8,128)(2,1)S(1)}, u32[]{:S(2)}, u32[]{:S(2)}) async-start(bf16[4,6,128,512]{3,2,1,0:T(8,128)(2,1)} %select_convert_fusion), calls=%async_computation.2 | async-start | bytes 6291456 | tf_op jit(solution)/shard_map/all_to_all | solution.py:79
where the time goes:
time: 340 us; the launch traced here: 338 us
  local copies, waits for them, and re-layouts  125 us (37%)
  matrix products  67.8 us (20%)
  waiting for transfers between devices  63.7 us (19%)
  other arithmetic  38.5 us (11%)
  blocking collectives  33.9 us (10%)
  starting transfers between devices  8.47 us (2%)
    all_to_all x1, waiting for transfers between devices, local(): lax.all_to_all(outgoing.reshape(device_count, capacity, tile_rows, type_w...  63.7 us
    reshape x1, local copies, waits for them, and re-layouts, local(): contrib = jnp.einsum('bamij,baik->bamjk', tiles, scaled, preferred_elemen...  49.2 us
    gather x2, local copies, waits for them, and re-layouts, local(): picked = jnp.take(table, lookup, axis=0)  46.1 us
    dot_general x1, matrix products, local(): jnp.einsum('bamij,baik->bamjk', tiles, scaled, preferred_element_type=jnp...  24.5 us
    dot_general x1, matrix products, local(): jnp.einsum('rd,rjk->djk', local_select, contrib, precision=lax.Precision....  23.2 us
    dot_general x1, matrix products, local(): jnp.einsum('bamij,bamjk->baik', tiles, picked, preferred_element_type=jnp...  15 us
    psum x1, blocking collectives, local(): lax.psum(jnp.sum(grad_q, axis=(0, 2)), 'state')  12.2 us
    all_to_all x1, blocking collectives, local(): lax.all_to_all(request.reshape(device_count, capacity), 'state', split_ax...  11.7 us
  transfers between devices with their start and end apart: 2, of which 1 were waited for; matrix products, arithmetic and copies ran while one was open for 27% of the time, Pallas kernels for 0%

commit v1 on v0

v1 whole, which is shorter than its diff:
```python
import functools

import jax
import jax.numpy as jnp
from jax import lax
from jax.experimental import pallas as pl
from jax.experimental.pallas import tpu as pltpu
from jax.sharding import PartitionSpec as P

DISCOUNT = 0.95
VMEM_LIMIT = 40 * 1024 * 1024

SMEM_SPEC = pl.BlockSpec(memory_space=pltpu.SMEM)
ANY_SPEC = pl.BlockSpec(memory_space=pl.ANY)


def plan_kernel(device_count, capacity, me_ref, dest_ref, counts_ref, req_ref, src_ref, loc_ref, fill_ref):
    block_count, action_count, entry_count = dest_ref.shape
    me = me_ref[0]
    base = me * block_count
    for k in range((device_count - 1) * capacity):
        req_ref[k] = -1
        src_ref[k] = 0
    for k in range(device_count):
        fill_ref[k] = 0

    def one_list(block, action):
        def one_entry(n, carry):
            dest = dest_ref[block, action, n]
            rel = dest - base
            entry = (block * action_count + action) * entry_count + n
            loc_ref[entry] = -1

            @pl.when((rel < 0) | (rel >= block_count))
            def _():
                owner = dest // block_count
                offset = lax.rem(owner - me + device_count, device_count)
                place = fill_ref[offset]
                fill_ref[offset] = place + 1
                slot = (offset - 1) * capacity + place
                req_ref[slot] = dest - owner * block_count
                src_ref[slot] = entry
                loc_ref[entry] = slot

            return carry

        lax.fori_loop(0, counts_ref[block, action], one_entry, 0)

    def one_block(block, carry):
        for action in range(action_count):
            one_list(block, action)
        return carry

    lax.fori_loop(0, block_count, one_block, 0)


def make_plan(me, dest_block, counts, device_count, capacity):
    slots = (device_count - 1) * capacity
    return pl.pallas_call(
        functools.partial(plan_kernel, device_count, capacity),
        out_shape=(
            jax.ShapeDtypeStruct((slots,), jnp.int32),
            jax.ShapeDtypeStruct((slots,), jnp.int32),
            jax.ShapeDtypeStruct((dest_block.size,), jnp.int32),
        ),
        in_specs=[SMEM_SPEC] * 3,
        out_specs=(SMEM_SPEC,) * 3,
        scratch_shapes=[pltpu.SMEM((device_count,), jnp.int32)],
        name="plan",
    )(me, dest_block, counts)


def gather_kernel(wanted_ref, value_ref, out_ref, sems):
    slots = out_ref.shape[0]
    copies = [
        pltpu.make_async_copy(value_ref.at[jnp.maximum(wanted_ref[k], 0)], out_ref.at[k], sems.at[k])
        for k in range(slots)
    ]
    for copy in copies:
        copy.start()
    for copy in copies:
        copy.wait()


def gather_blocks(wanted, value_blocks):
    slots = wanted.shape[0]
    return pl.pallas_call(
        gather_kernel,
        out_shape=jax.ShapeDtypeStruct((slots,) + value_blocks.shape[1:], value_blocks.dtype),
        in_specs=[SMEM_SPEC, ANY_SPEC],
        out_specs=ANY_SPEC,
        scratch_shapes=[pltpu.SemaphoreType.DMA((slots,))],
        cost_estimate=pl.CostEstimate(flops=0, bytes_accessed=1 << 20, transcendentals=0),
        name="gather",
    )(wanted, value_blocks)


def local_forward_kernel(me_ref, dest_ref, counts_ref, value_ref, tiles_ref, util_ref, taste_ref, sent_ref, out_ref, acc_ref):
    del sent_ref
    block = pl.program_id(0)
    _, action_count, entry_count, tile_rows, _ = tiles_ref.shape
    block_count, _, width = value_ref.shape
    base = me_ref[0] * block_count
    for action in range(action_count):
        acc_ref[...] = jnp.zeros_like(acc_ref)
        for n in range(entry_count):
            rel = dest_ref[block, action, n] - base

            @pl.when((n < counts_ref[block, action]) & (rel >= 0) & (rel < block_count))
            def _():
                acc_ref[...] += jnp.dot(
                    tiles_ref[0, action, n], value_ref[rel], preferred_element_type=jnp.float32
                )

        util = jnp.broadcast_to(util_ref[action : action + 1, :], (tile_rows, tile_rows)).T
        taste = taste_ref[action : action + 1, :]
        for c in range(0, width, tile_rows):
            cols = slice(c, c + tile_rows)
            out_ref[0, action, :, cols] = (util + taste[:, cols]) + DISCOUNT * acc_ref[:, cols]


def local_forward(me, dest_block, counts, value_blocks, tiles, state_util, taste, sent):
    block_count, action_count, entry_count, tile_rows, _ = tiles.shape
    width = value_blocks.shape[2]
    return pl.pallas_call(
        local_forward_kernel,
        out_shape=jax.ShapeDtypeStruct((block_count, action_count, tile_rows, width), jnp.float32),
        grid_spec=pltpu.PrefetchScalarGridSpec(
            num_scalar_prefetch=3,
            grid=(block_count,),
            in_specs=[
                pl.BlockSpec(value_blocks.shape, lambda i, *_: (0, 0, 0)),
                pl.BlockSpec((1,) + tiles.shape[1:], lambda i, *_: (i, 0, 0, 0, 0)),
                pl.BlockSpec((action_count, tile_rows), lambda i, *_: (0, i)),
                pl.BlockSpec(taste.shape, lambda i, *_: (0, 0)),
                ANY_SPEC,
            ],
            out_specs=pl.BlockSpec((1, action_count, tile_rows, width), lambda i, *_: (i, 0, 0, 0)),
            scratch_shapes=[pltpu.VMEM((tile_rows, width), jnp.float32)],
        ),
        compiler_params=pltpu.CompilerParams(vmem_limit_bytes=VMEM_LIMIT),
        cost_estimate=pl.CostEstimate(flops=4 * 10**9, bytes_accessed=16 << 20, transcendentals=0),
        name="local_forward",
    )(me, dest_block, counts, value_blocks, tiles, state_util, taste, sent)


def add_remote(block, loc_ref, counts_ref, tiles_ref, incoming_refs, part_ref, scores_ref):
    _, action_count, entry_count, _, _ = tiles_ref.shape
    capacity = incoming_refs[0].shape[0]
    for action in range(action_count):
        scores_ref[action] = part_ref[0, action]
    for action in range(action_count):
        for n in range(entry_count):
            slot = loc_ref[(block * action_count + action) * entry_count + n]
            used = n < counts_ref[block, action]
            for row, incoming_ref in enumerate(incoming_refs):
                place = slot - row * capacity

                @pl.when(used & (place >= 0) & (place < capacity))
                def _():
                    scores_ref[action] += DISCOUNT * jnp.dot(
                        tiles_ref[0, action, n], incoming_ref[place], preferred_element_type=jnp.float32
                    )


def transposed_dot(tile, rows):
    return lax.dot_general(tile, rows, (((0,), (0,)), ((), ())), preferred_element_type=jnp.float32)


def remote_terms_kernel(row_count, src_ref, loc_ref, counts_ref, *refs):
    incoming_refs = refs[:row_count]
    part_ref, tiles_ref, cot_ref, out_ref, scores_ref = refs[row_count:]
    _, action_count, entry_count, _, _ = tiles_ref.shape
    entry = src_ref[pl.program_id(0)]
    one_list = entry // entry_count
    block = one_list // action_count
    action = one_list - block * action_count
    n = entry - one_list * entry_count
    add_remote(block, loc_ref, counts_ref, tiles_ref, incoming_refs, part_ref, scores_ref)
    largest = scores_ref[0]
    for other in range(1, action_count):
        largest = jnp.maximum(largest, scores_ref[other])
    total = jnp.exp(scores_ref[0] - largest)
    for other in range(1, action_count):
        total = total + jnp.exp(scores_ref[other] - largest)
    prob = jnp.exp(scores_ref[action] - largest) / total
    scaled = (DISCOUNT * (cot_ref[0].astype(jnp.float32) * prob)).astype(jnp.bfloat16)
    out_ref[0] = transposed_dot(tiles_ref[0, action, n], scaled).astype(jnp.bfloat16)


def remote_terms(src, loc, counts, incoming, part, tiles, cot_blocks):
    block_count, action_count, entry_count, tile_rows, _ = tiles.shape
    width = cot_blocks.shape[2]
    per_block = action_count * entry_count
    return pl.pallas_call(
        functools.partial(remote_terms_kernel, len(incoming)),
        out_shape=jax.ShapeDtypeStruct((src.shape[0], tile_rows, width), jnp.bfloat16),
        grid_spec=pltpu.PrefetchScalarGridSpec(
            num_scalar_prefetch=3,
            grid=(src.shape[0],),
            in_specs=[pl.BlockSpec(x.shape, lambda r, *_: (0, 0, 0)) for x in incoming]
            + [
                pl.BlockSpec((1,) + part.shape[1:], lambda r, src, *_: (src[r] // per_block, 0, 0, 0)),
                pl.BlockSpec((1,) + tiles.shape[1:], lambda r, src, *_: (src[r] // per_block, 0, 0, 0, 0)),
                pl.BlockSpec((1, tile_rows, width), lambda r, src, *_: (src[r] // per_block, 0, 0)),
            ],
            out_specs=pl.BlockSpec((1, tile_rows, width), lambda r, *_: (r, 0, 0)),
            scratch_shapes=[pltpu.VMEM((action_count, tile_rows, width), jnp.float32)],
        ),
        compiler_params=pltpu.CompilerParams(vmem_limit_bytes=VMEM_LIMIT),
        cost_estimate=pl.CostEstimate(flops=10**8, bytes_accessed=4 << 20, transcendentals=10**5),
        name="remote_terms",
    )(src, loc, counts, *incoming, part, tiles, cot_blocks)


def finish_kernel(row_count, sent_count, util_scale, taste_scale, me_ref, dest_ref, loc_ref, counts_ref, *refs):
    incoming_refs = refs[:row_count]
    part_ref, tiles_ref, cot_ref = refs[row_count : row_count + 3]
    value_ref, adjoint_ref, util_ref, taste_ref, scores_ref, scaled_ref = refs[row_count + 3 + sent_count :]
    block = pl.program_id(0)
    _, action_count, entry_count, tile_rows, _ = tiles_ref.shape
    block_count = adjoint_ref.shape[0]
    width = value_ref.shape[1]
    base = me_ref[0] * block_count

    @pl.when(block == 0)
    def _():
        adjoint_ref[...] = jnp.zeros_like(adjoint_ref)
        taste_ref[...] = jnp.zeros_like(taste_ref)

    add_remote(block, loc_ref, counts_ref, tiles_ref, incoming_refs, part_ref, scores_ref)
    sums = [jnp.zeros((tile_rows, tile_rows), jnp.float32) for _ in range(action_count)]
    for c in range(0, width, tile_rows):
        cols = slice(c, c + tile_rows)
        scores = [scores_ref[action, :, cols] for action in range(action_count)]
        largest = functools.reduce(jnp.maximum, scores)
        powers = [jnp.exp(x - largest) for x in scores]
        total = functools.reduce(jnp.add, powers)
        value_ref[:, cols] = largest + jnp.log(total)
        ratio = cot_ref[0, :, cols].astype(jnp.float32) / total
        for action in range(action_count):
            grad = ratio * powers[action]
            scaled_ref[action, :, cols] = (DISCOUNT * grad).astype(jnp.bfloat16)
            sums[action] = sums[action] + grad
            taste_ref[action : action + 1, cols] += taste_scale * jnp.sum(grad, axis=0, keepdims=True)
    for action in range(action_count):
        util_ref[action : action + 1, :] = util_scale * jnp.sum(sums[action].T, axis=0, keepdims=True)
    for action in range(action_count):
        for n in range(entry_count):
            rel = dest_ref[block, action, n] - base

            @pl.when((n < counts_ref[block, action]) & (rel >= 0) & (rel < block_count))
            def _():
                adjoint_ref[rel] += transposed_dot(tiles_ref[0, action, n], scaled_ref[action])


def finish(me, dest_block, loc, counts, incoming, part, tiles, cot_blocks, sent, util_scale, taste_scale):
    block_count, action_count, entry_count, tile_rows, _ = tiles.shape
    width = cot_blocks.shape[2]
    states = block_count * tile_rows
    return pl.pallas_call(
        functools.partial(finish_kernel, len(incoming), len(sent), util_scale, taste_scale),
        out_shape=(
            jax.ShapeDtypeStruct((states, width), jnp.float32),
            jax.ShapeDtypeStruct((block_count, tile_rows, width), jnp.float32),
            jax.ShapeDtypeStruct((action_count, states), jnp.float32),
            jax.ShapeDtypeStruct((action_count, width), jnp.float32),
        ),
        grid_spec=pltpu.PrefetchScalarGridSpec(
            num_scalar_prefetch=4,
            grid=(block_count,),
            in_specs=[pl.BlockSpec(x.shape, lambda i, *_: (0, 0, 0)) for x in incoming]
            + [
                pl.BlockSpec((1,) + part.shape[1:], lambda i, *_: (i, 0, 0, 0)),
                pl.BlockSpec((1,) + tiles.shape[1:], lambda i, *_: (i, 0, 0, 0, 0)),
                pl.BlockSpec((1, tile_rows, width), lambda i, *_: (i, 0, 0)),
            ]
            + [ANY_SPEC] * len(sent),
            out_specs=(
                pl.BlockSpec((tile_rows, width), lambda i, *_: (i, 0)),
                pl.BlockSpec((block_count, tile_rows, width), lambda i, *_: (0, 0, 0)),
                pl.BlockSpec((action_count, tile_rows), lambda i, *_: (0, i)),
                pl.BlockSpec((action_count, width), lambda i, *_: (0, 0)),
            ),
            scratch_shapes=[
                pltpu.VMEM((action_count, tile_rows, width), jnp.float32),
                pltpu.VMEM((action_count, tile_rows, width), jnp.bfloat16),
            ],
        ),
        compiler_params=pltpu.CompilerParams(vmem_limit_bytes=VMEM_LIMIT),
        cost_estimate=pl.CostEstimate(flops=4 * 10**9, bytes_accessed=24 << 20, transcendentals=4 * 10**6),
        name="finish",
    )(me, dest_block, loc, counts, *incoming, part, tiles, cot_blocks, *sent)


def add_arrivals_kernel(wanted_ref, arrived_ref, base_ref, out_ref, held_ref, in_sems, out_sems):
    slots = arrived_ref.shape[0]
    target = [wanted_ref[k] for k in range(slots)]
    lead = []
    for k in range(slots):
        first = target[k] >= 0
        for other in range(k):
            first = first & (target[other] != target[k])
        lead.append(first)
    place = [jnp.maximum(t, 0) for t in target]
    fetch = [pltpu.make_async_copy(out_ref.at[place[k]], held_ref.at[k], in_sems.at[k]) for k in range(slots)]
    store = [pltpu.make_async_copy(held_ref.at[k], out_ref.at[place[k]], out_sems.at[k]) for k in range(slots)]
    for k in range(slots):

        @pl.when(lead[k])
        def _():
            fetch[k].start()

    for k in range(slots):

        @pl.when(lead[k])
        def _():
            fetch[k].wait()
            held_ref[k] += arrived_ref[k].astype(jnp.float32)
            for other in range(k + 1, slots):

                @pl.when(target[other] == target[k])
                def _():
                    held_ref[k] += arrived_ref[other].astype(jnp.float32)

            store[k].start()

    for k in range(slots):

        @pl.when(lead[k])
        def _():
            store[k].wait()


def add_arrivals(wanted, arrived, adjoint):
    slots = arrived.shape[0]
    return pl.pallas_call(
        add_arrivals_kernel,
        out_shape=jax.ShapeDtypeStruct(adjoint.shape, adjoint.dtype),
        in_specs=[SMEM_SPEC, pl.BlockSpec(memory_space=pltpu.VMEM), ANY_SPEC],
        out_specs=ANY_SPEC,
        scratch_shapes=[
            pltpu.VMEM(arrived.shape, jnp.float32),
            pltpu.SemaphoreType.DMA((slots,)),
            pltpu.SemaphoreType.DMA((slots,)),
        ],
        input_output_aliases={2: 0},
        compiler_params=pltpu.CompilerParams(vmem_limit_bytes=VMEM_LIMIT),
        cost_estimate=pl.CostEstimate(flops=10**6, bytes_accessed=4 << 20, transcendentals=0),
        name="add_arrivals",
    )(wanted, arrived, adjoint)


def local(value_in, cotangent, state_util, taste, tiles, dest_block, counts):
    block_count, action_count, entry_count, tile_rows, _ = tiles.shape
    width = value_in.shape[1]
    device_count = lax.axis_size("state")
    me = lax.axis_index("state").astype(jnp.int32).reshape(1)
    capacity = max(2, (block_count + device_count - 2) // (device_count - 1))
    value_blocks = value_in.reshape(block_count, tile_rows, width)
    cot_blocks = cotangent.reshape(block_count, tile_rows, width)
    offsets = range(1, device_count)
    order = sorted(offsets, key=lambda d: -min(d, device_count - d))

    def shift(x, offset):
        return lax.ppermute(x, "state", [(s, (s + offset) % device_count) for s in range(device_count)])

    def row(x, offset):
        return lax.slice(x, ((offset - 1) * capacity,), (offset * capacity,))

    request, source, loc = make_plan(me, dest_block, counts, device_count, capacity)
    wanted = {d: shift(row(request, d), d) for d in order}
    outgoing = {d: gather_blocks(wanted[d], value_blocks) for d in order}
    incoming = {d: shift(outgoing[d], -d) for d in order}
    part = local_forward(me, dest_block, counts, value_blocks, tiles, state_util, taste, outgoing[order[-1]])
    held = [incoming[d] for d in offsets]

    returned = []
    sent = []
    for index, d in enumerate(order):
        cuts = [0, min(2, capacity), capacity] if index == 0 else [0, capacity]
        for lo, hi in zip(cuts[:-1], cuts[1:]):
            if lo < hi:
                src = row(source, d)[lo:hi]
                terms = remote_terms(src, loc, counts, held, part, tiles, cot_blocks)
                sent.append(terms)
                returned.append((wanted[d][lo:hi], shift(terms, d)))
    value_out, adjoint, util_part, taste_part = finish(
        me, dest_block, loc, counts, held, part, tiles, cot_blocks, sent,
        1.0 / (width * lax.axis_size("type")), 1.0 / (block_count * tile_rows * device_count),
    )
    util_total = lax.psum(util_part, "type")
    taste_total = lax.psum(taste_part, "state")
    for places, terms in returned:
        adjoint = add_arrivals(places, terms, adjoint)
    return value_out, adjoint.reshape(block_count * tile_rows, width), util_total, taste_total


def solution(mesh):
    return jax.shard_map(
        local,
        mesh=mesh,
        in_specs=(
            P(("groups", "state"), "type"),
            P(("groups", "state"), "type"),
            P(None, ("groups", "state")),
            P(None, ("groups", "type")),
            P(("groups", "state"), None, None, None, None),
            P(("groups", "state"), None, None),
            P(("groups", "state"), None),
        ),
        out_specs=(
            P(("groups", "state"), "type"),
            P(("groups", "state"), "type"),
            P(None, ("groups", "state")),
            P(None, ("groups", "type")),
        ),
        check_vma=False,
    )
```

time: 340 us -> 244 us (0.72)
  Pallas kernels: 0 us -> 185 us
  local copies, waits for them, and re-layouts: 125 us -> 11 us
  matrix products: 67.8 us -> 0 us
  waiting for transfers between devices: 63.7 us -> 3.89 us
  other arithmetic: 38.5 us -> 0.01 us
  blocking collectives: 33.9 us -> 23.8 us
  starting transfers between devices: 8.47 us -> 17.2 us
    pallas_call x0 -> x14, Pallas kernels: none -> 185 us  [the longest x3 77.2 us: gather_blocks(): pl.pallas_call(gather_kernel, out_shape=jax.ShapeDtypeStruct((slots,) + v...]
    dot_general x4 -> x0, matrix products: 67.8 us -> none  [the longest x1 24.5 us: local(): jnp.einsum('bamij,baik->bamjk', tiles, scaled, preferred_element_type=jnp...]
    all_to_all x2 -> x0, waiting for transfers between devices: 63.7 us -> none  [the longest x1 63.7 us: local(): lax.all_to_all(outgoing.reshape(device_count, capacity, tile_rows, type_w...]
    gather x5 -> x0, local copies, waits for them, and re-layouts: 55.6 us -> none  [the longest x2 46.1 us: local(): picked = jnp.take(table, lookup, axis=0)]
    reshape x4 -> x0, local copies, waits for them, and re-layouts: 49.5 us -> none  [the longest x1 49.2 us: local(): contrib = jnp.einsum('bamij,baik->bamjk', tiles, scaled, preferred_elemen...]
    reduce_sum x3 -> x0, other arithmetic: 17.2 us -> none  [the longest x1 9.72 us: local(): jnp.sum(jnp.exp(scores - largest[:, None]), axis=1)]
    ppermute x0 -> x10, starting transfers between devices: none -> 17.2 us  [shift(): lax.ppermute(x, 'state', [(s, (s + offset) % device_count) for s in range...]
    all_to_all x1 -> x0, blocking collectives: 11.7 us -> none  [local(): lax.all_to_all(request.reshape(device_count, capacity), 'state', split_ax...]
  transfers between devices with their start and end apart: 2 -> 10, of which waited for: 1 -> 1; matrix products, arithmetic and copies ran while one was open for 27% -> 0% of each run, Pallas kernels for 0% -> 69%
where the time goes in v1:
time: 244 us; the launch traced here: 242 us
  Pallas kernels  185 us (76%)
  blocking collectives  23.8 us (10%)
  starting transfers between devices  17.2 us (7%)
  local copies, waits for them, and re-layouts  11 us (5%)
  waiting for transfers between devices  3.89 us (2%)
    pallas_call x3, Pallas kernels, gather_blocks(): pl.pallas_call(gather_kernel, out_shape=jax.ShapeDtypeStruct((slots,) + v...  77.2 us
    pallas_call x1, Pallas kernels, finish(): pl.pallas_call(functools.partial(finish_kernel, len(incoming), len(sent),...  39.3 us
    pallas_call x4, Pallas kernels, remote_terms(): pl.pallas_call(functools.partial(remote_terms_kernel, len(incoming)), out...  27.7 us
    pallas_call x1, Pallas kernels, local_forward(): pl.pallas_call(local_forward_kernel, out_shape=jax.ShapeDtypeStruct((bloc...  23.9 us
    ppermute x10, starting transfers between devices, shift(): lax.ppermute(x, 'state', [(s, (s + offset) % device_count) for s in range...  17.2 us
    psum x1, blocking collectives, local(): taste_total = lax.psum(taste_part, 'state')  13.2 us
    pallas_call x4, Pallas kernels, add_arrivals(): pl.pallas_call(add_arrivals_kernel, out_shape=jax.ShapeDtypeStruct(adjoin...  12.2 us
    psum x1, blocking collectives, local(): util_total = lax.psum(util_part, 'type')  10.7 us
  transfers between devices with their start and end apart: 10, of which 1 were waited for; matrix products, arithmetic and copies ran while one was open for 0% of the time, Pallas kernels for 69%

profile of v1, /device:TPU:0, one launch (start us, length us, event | category | flops | bytes accessed | tf_op | source)
XLA Modules:
  0.0 241.9 jit_solution(4532413059415907235)
XLA Ops:
  0.6 1.3 copy.16.counts_ref
  2.0 1.4 copy.23.dest_ref
  3.4 4.6 %plan.1 = (s32[18]{0:T(128)}, s32[18]{0:T(128)}, s32[192]{0:T(256)}) custom-call(s32[1]{0:T(128)} %bitcast.me_ref, s32[16,2,6]{2,1,0:T(2,128)} %copy.23.dest_ref, s32[16,2]{1,0:T(8,128)} %copy.16.counts_ref), custom_call_target="tpu_custom_call" | custom-call | tf_op jit(solution)/shard_map/plan/pallas_call | solution.py:59
  8.0 0.8 fusion.1
  8.8 5.1 %collective-permute-start.4 = (s32[6]{0:T(128)S(1)}, s32[6]{0:T(128)S(1)}, u32[]{:S(2)}, u32[]{:S(2)}) collective-permute-start(s32[6]{0:T(128)S(1)} %get-tuple-element.20), channel_id=1, source_target_pairs={{0,12},{4,0},{8,4},{12,8},{1,13},{5,1},{9,5},{13,9},{2,14},{6,2},{... | collective-permute-start | bytes 80 | tf_op jit(solution)/shard_map/ppermute | solution.py:366
  13.9 0.0 collective-permute-start.2
  13.9 0.6 collective-permute-start
  14.5 3.9 %collective-permute-done.2.wanted_ref = s32[6]{0:T(128)S(1)} collective-permute-done((s32[6]{0:T(128)S(1)}, s32[6]{0:T(128)S(1)}, u32[]{:S(2)}, u32[]{:S(2)}) %collective-permute-start.2) | collective-permute-done | bytes 56 | tf_op jit(solution)/shard_map/ppermute | solution.py:366
  18.4 0.5 copy-done.13
  18.9 0.0 copy-start.8
  18.9 25.8 %gather.4 = bf16[6,128,512]{2,1,0:T(8,128)(2,1)} custom-call(s32[6]{0:T(128)} %copy-done.13, bf16[16,128,512]{2,1,0:T(8,128)(2,1)} %bitcast.12), custom_call_target="tpu_custom_call" | custom-call | bytes 1048576 | tf_op jit(solution)/shard_map/gather/pallas_call | solution.py:87
  44.7 0.1 collective-permute-start.3
  44.8 0.0 collective-permute-done.4.wanted_ref
  44.8 0.6 copy-done.9
  45.4 25.8 %gather.5.sent_ref = bf16[6,128,512]{2,1,0:T(8,128)(2,1)} custom-call(s32[6]{0:T(128)} %copy-done.9, bf16[16,128,512]{2,1,0:T(8,128)(2,1)} %bitcast.13), custom_call_target="tpu_custom_call" | custom-call | bytes 1048576 | tf_op jit(solution)/shard_map/gather/pallas_call | solution.py:87
  71.2 0.6 collective-permute-start.5
  71.8 0.0 collective-permute-done.wanted_ref
  71.8 0.5 copy-done.11
  72.3 25.6 %gather.3 = bf16[6,128,512]{2,1,0:T(8,128)(2,1)} custom-call(s32[6]{0:T(128)} %copy-done.11, bf16[16,128,512]{2,1,0:T(8,128)(2,1)} %bitcast.14), custom_call_target="tpu_custom_call" | custom-call | bytes 1048576 | tf_op jit(solution)/shard_map/gather/pallas_call | solution.py:87
  97.9 3.3 %collective-permute-start.1 = (bf16[6,128,512]{2,1,0:T(8,128)(2,1)}, bf16[6,128,512]{2,1,0:T(8,128)(2,1)S(1)}, u32[]{:S(2)}, u32[]{:S(2)}) collective-permute-start(bf16[6,128,512]{2,1,0:T(8,128)(2,1)} %gather.3), channel_id=1, source_target_pairs={{0,12},{4,0},{8,4},{12,8},{1,13},{5,1},{9,5},{13,9},{2,14},{6,2},{... | collective-permute-start | bytes 2359304 | tf_op jit(solution)/shard_map/ppermute | solution.py:366
  101.3 0.1 fusion
  101.3 0.0 copy-start
  101.4 2.8 %copy-done = bf16[16,2,6,128,128]{4,3,2,1,0:T(8,128)(2,1)S(1)} copy-done((bf16[16,2,6,128,128]{4,3,2,1,0:T(8,128)(2,1)S(1)}, bf16[16,2,6,128,128]{4,3,2,1,0:T(8,128)(2,1)}, u32[]{:S(2)}) %copy-start) | copy-done | bytes 6291480
  104.1 1.6 copy-done.2
  105.7 1.1 copy-done.3
  106.9 23.9 %local_forward.1.refs_3_ = f32[16,2,128,512]{3,2,1,0:T(8,128)} custom-call(s32[1]{0:T(128)} %bitcast.me_ref, s32[16,2,6]{2,1,0:T(2,128)S(1)} %copy-done.5, s32[16,2]{1,0:T(8,128)S(1)} %copy-done.4, bf16[16,128,512]{2,1,0:T(8,128)(2,1)S(1)} %bitcast.15, bf16[16,2,6,128,128]{4,3,2,1,0:T(8,128)(2,1)S(1)} %copy-done, f32[2,2048]{1,0:T(2,128)S(1)} %copy-done.7, ...), custom_call_target="tpu_custom_call" | custom-call | flops 4000000000 | bytes 16777216 | tf_op jit(solution)/shard_map/local_forward/pallas_call | solution.py:125
  130.7 0.0 collective-permute-done.3.refs_1_
  130.7 0.0 collective-permute-done.5.refs_2_
  130.8 9.0 %remote_terms.6.refs_8_ = bf16[6,128,512]{2,1,0:T(8,128)(2,1)} custom-call(s32[6]{0:T(128)S(1)} %get-tuple-element.19.src_ref, s32[192]{0:T(256)S(1)} %copy-done.6, s32[16,2]{1,0:T(8,128)S(1)} %copy-done.4, bf16[6,128,512]{2,1,0:T(8,128)(2,1)S(1)} %collective-permute-done.1.refs_0_, bf16[6,128,512]{2,1,0:T(8,128)(2,1)S(1)} %collective-permute-done.3.refs_1_, ...), custom_call_target="tpu_custom_call" | custom-call | flops 100000000 | bytes 4194304 | tf_op jit(solution)/shard_map/remote_terms/pallas_call | solution.py:195
  139.8 2.3 collective-permute-start.7
  142.2 8.5 %remote_terms.7.refs_9_ = bf16[6,128,512]{2,1,0:T(8,128)(2,1)} custom-call(s32[6]{0:T(128)S(1)} %get-tuple-element.18.src_ref, s32[192]{0:T(256)S(1)} %copy-done.6, s32[16,2]{1,0:T(8,128)S(1)} %copy-done.4, bf16[6,128,512]{2,1,0:T(8,128)(2,1)S(1)} %collective-permute-done.1.refs_0_, bf16[6,128,512]{2,1,0:T(8,128)(2,1)S(1)} %collective-permute-done.3.refs_1_, ...), custom_call_target="tpu_custom_call" | custom-call | flops 100000000 | bytes 4194304 | tf_op jit(solution)/shard_map/remote_terms/pallas_call | solution.py:195
  150.7 1.7 collective-permute-start.6
  152.4 0.1 slice.35.src_ref
  152.5 5.8 %remote_terms.5.refs_7_ = bf16[4,128,512]{2,1,0:T(8,128)(2,1)S(1)} custom-call(s32[4]{0:T(128)S(1)} %slice.35.src_ref, s32[192]{0:T(256)S(1)} %copy-done.6, s32[16,2]{1,0:T(8,128)S(1)} %copy-done.4, bf16[6,128,512]{2,1,0:T(8,128)(2,1)S(1)} %collective-permute-done.1.refs_0_, bf16[6,128,512]{2,1,0:T(8,128)(2,1)S(1)} %collective-permute-done.3.refs_1_, ...), custom_call_target="tpu_custom_call" | custom-call | flops 100000000 | bytes 4194304 | tf_op jit(solution)/shard_map/remote_terms/pallas_call | solution.py:195
  158.3 0.8 collective-permute-start.8
  159.1 0.1 slice.34.src_ref
  159.2 0.1 slice.38.wanted_ref
  159.2 4.4 %remote_terms.4.refs_6_ = bf16[2,128,512]{2,1,0:T(8,128)(2,1)} custom-call(s32[2]{0:T(128)S(1)} %slice.34.src_ref, s32[192]{0:T(256)S(1)} %copy-done.6, s32[16,2]{1,0:T(8,128)S(1)} %copy-done.4, bf16[6,128,512]{2,1,0:T(8,128)(2,1)S(1)} %collective-permute-done.1.refs_0_, bf16[6,128,512]{2,1,0:T(8,128)(2,1)S(1)} %collective-permute-done.3.refs_1_, ...), custom_call_target="tpu_custom_call" | custom-call | flops 100000000 | bytes 4194304 | tf_op jit(solution)/shard_map/remote_terms/pallas_call | solution.py:195
  163.6 2.7 %collective-permute-start.9 = (bf16[2,128,512]{2,1,0:T(8,128)(2,1)}, bf16[2,128,512]{2,1,0:T(8,128)(2,1)}, u32[]{:S(2)}, u32[]{:S(2)}) collective-permute-start(bf16[2,128,512]{2,1,0:T(8,128)(2,1)} %remote_terms.4.refs_6_), channel_id=1, source_target_pairs={{0,8},{4,12},{8,0},{12,4},{1,9},{5,13},{9,1},{13,5},{2,10},{6,14},... | collective-permute-start | bytes 786440 | tf_op jit(solution)/shard_map/ppermute | solution.py:366
  166.3 39.3 %finish.1 = (f32[2048,512]{1,0:T(8,128)}, f32[16,128,512]{2,1,0:T(8,128)}, f32[2,2048]{1,0:T(2,128)S(1)}, f32[2,512]{1,0:T(2,128)S(1)}) custom-call(s32[1]{0:T(128)} %bitcast.me_ref, s32[16,2,6]{2,1,0:T(2,128)S(1)} %copy-done.5, s32[192]{0:T(256)S(1)} %copy-done.6, s32[16,2]{1,0:T(8,128)S(1)} %copy-done.4, ...), custom_call_target="tpu_custom_call" | custom-call | flops 4000000000 | bytes 25165824 | tf_op jit(solution)/shard_map/finish/pallas_call | solution.py:261
  205.6 13.2 %psum.15 = f32[2,512]{1,0:T(2,128)} all-reduce(f32[2,512]{1,0:T(2,128)S(1)} %get-tuple-element.17), channel_id=1, replica_groups=mesh['groups'=2,'state'=4,'type'=4] {'state'}, use_global_device_ids=true, to_apply=%region_1.0 | all-reduce | flops 1024 | bytes 8192 | tf_op jit(solution)/shard_map/psum | solution.py:393
  218.7 10.7 %psum.14 = f32[2,2048]{1,0:T(2,128)} all-reduce(f32[2,2048]{1,0:T(2,128)S(1)} %get-tuple-element.16), channel_id=1, replica_groups=mesh['groups'=2,'state'=4,'type'=4] {'type'}, use_global_device_ids=true, to_apply=%region_0.0 | all-reduce | flops 4096 | bytes 32768 | tf_op jit(solution)/shard_map/psum | solution.py:392
  229.4 0.0 collective-permute-done.9.arrived_ref
  229.4 2.8 %add_arrivals.4.base_ref = f32[16,128,512]{2,1,0:T(8,128)} custom-call(s32[2]{0:T(128)S(1)} %bitcast.16, bf16[2,128,512]{2,1,0:T(8,128)(2,1)} %collective-permute-done.9.arrived_ref, f32[16,128,512]{2,1,0:T(8,128)} %get-tuple-element.15.base_ref), custom_call_target="tpu_custom_call", output_to_operand_aliasing={{}: (2, {})} | custom-call | flops 1000000 | bytes 4194304 | tf_op jit(solution)/shard_map/add_arrivals/pallas_call | solution.py:337
  232.2 2.9 %add_arrivals.5.base_ref = f32[16,128,512]{2,1,0:T(8,128)} custom-call(s32[4]{0:T(128)S(1)} %slice.38.wanted_ref, bf16[4,128,512]{2,1,0:T(8,128)(2,1)} %collective-permute-done.8.arrived_ref, f32[16,128,512]{2,1,0:T(8,128)} %add_arrivals.4.base_ref), custom_call_target="tpu_custom_call", output_to_operand_aliasing={{}: (2, {})} | custom-call | flops 1000000 | bytes 4194304 | tf_op jit(solution)/shard_map/add_arrivals/pallas_call | solution.py:337
  235.2 0.0 collective-permute-done.7.arrived_ref
  235.2 3.2 %add_arrivals.6.base_ref = f32[16,128,512]{2,1,0:T(8,128)} custom-call(s32[6]{0:T(128)S(1)} %copy-done.12, bf16[6,128,512]{2,1,0:T(8,128)(2,1)} %collective-permute-done.7.arrived_ref, f32[16,128,512]{2,1,0:T(8,128)} %add_arrivals.5.base_ref), custom_call_target="tpu_custom_call", output_to_operand_aliasing={{}: (2, {})} | custom-call | flops 1000000 | bytes 4194304 | tf_op jit(solution)/shard_map/add_arrivals/pallas_call | solution.py:337
  238.4 3.3 %add_arrivals.7 = f32[16,128,512]{2,1,0:T(8,128)} custom-call(s32[6]{0:T(128)S(1)} %copy-done.10, bf16[6,128,512]{2,1,0:T(8,128)(2,1)} %collective-permute-done.6.arrived_ref, f32[16,128,512]{2,1,0:T(8,128)} %add_arrivals.6.base_ref), custom_call_target="tpu_custom_call", output_to_operand_aliasing={{}: (2, {})} | custom-call | flops 1000000 | bytes 4194304 | tf_op jit(solution)/shard_map/add_arrivals/pallas_call | solution.py:337
  (32 shorter events, 0.1 us)
Async XLA Ops:
  8.8 35.9 %collective-permute-start.4 = (s32[6]{0:T(128)S(1)}, s32[6]{0:T(128)S(1)}, u32[]{:S(2)}, u32[]{:S(2)}) collective-permute-start(s32[6]{0:T(128)S(1)} %get-tuple-element.20), channel_id=1, source_target_pairs={{0,12},{4,0},{8,4},{12,8},{1,13},{5,1},{9,5},{13,9},{2,14},{6,2},{... | collective-permute-start | bytes 80 | tf_op jit(solution)/shard_map/ppermute | solution.py:366
  13.9 4.4 %collective-permute-start.2 = (s32[6]{0:T(128)S(1)}, s32[6]{0:T(128)S(1)}, u32[]{:S(2)}, u32[]{:S(2)}) collective-permute-start(s32[6]{0:T(128)S(1)} %get-tuple-element.21), channel_id=1, source_target_pairs={{0,8},{4,12},{8,0},{12,4},{1,9},{5,13},{9,1},{13,5},{2,10},{6,14},... | collective-permute-start | bytes 80 | tf_op jit(solution)/shard_map/ppermute | solution.py:366
  13.9 57.8 %collective-permute-start = (s32[6]{0:T(128)S(1)}, s32[6]{0:T(128)S(1)}, u32[]{:S(2)}, u32[]{:S(2)}) collective-permute-start(s32[6]{0:T(128)S(1)} %get-tuple-element.22), channel_id=1, source_target_pairs={{0,4},{4,8},{8,12},{12,0},{1,5},{5,9},{9,13},{13,1},{2,6},{6,10},{... | collective-permute-start | bytes 80 | tf_op jit(solution)/shard_map/ppermute | solution.py:366
  18.4 0.5 copy-start.13
  18.9 82.4 %copy-start.15 = (s32[18]{0:T(128)S(1)}, s32[18]{0:T(128)}, u32[]{:S(2)}) copy-start(s32[18]{0:T(128)} %get-tuple-element.13) | copy-start | bytes 220
  18.9 82.4 %copy-start.4 = (s32[16,2]{1,0:T(8,128)S(1)}, s32[16,2]{1,0:T(8,128)}, u32[]{:S(2)}) copy-start(s32[16,2]{1,0:T(8,128)} %copy.16.counts_ref) | copy-start | bytes 388
  18.9 82.4 %copy-start.5 = (s32[16,2,6]{2,1,0:T(2,128)S(1)}, s32[16,2,6]{2,1,0:T(2,128)}, u32[]{:S(2)}) copy-start(s32[16,2,6]{2,1,0:T(2,128)} %copy.23.dest_ref) | copy-start | bytes 2308
  18.9 82.4 %copy-start.7 = (f32[2,2048]{1,0:T(2,128)S(1)}, f32[2,2048]{1,0:T(2,128)}, u32[]{:S(2)}) copy-start(f32[2,2048]{1,0:T(2,128)} %util_ref.1) | copy-start | bytes 49156
  18.9 82.4 %copy-start.8 = (f32[2,512]{1,0:T(2,128)S(1)}, f32[2,512]{1,0:T(2,128)}, u32[]{:S(2)}) copy-start(f32[2,512]{1,0:T(2,128)} %taste_ref.1) | copy-start | bytes 12292
  44.7 86.0 %collective-permute-start.3 = (bf16[6,128,512]{2,1,0:T(8,128)(2,1)}, bf16[6,128,512]{2,1,0:T(8,128)(2,1)S(1)}, u32[]{:S(2)}, u32[]{:S(2)}) collective-permute-start(bf16[6,128,512]{2,1,0:T(8,128)(2,1)} %gather.4), channel_id=1, source_target_pairs={{0,8},{4,12},{8,0},{12,4},{1,9},{5,13},{9,1},{13,5},{2,10},{6,14},... | collective-permute-start | bytes 2359304 | tf_op jit(solution)/shard_map/ppermute | solution.py:366
  44.8 0.6 copy-start.9
  45.4 85.4 %slice-start = ((s8[6291456]{0:T(1024)(128)(4,1)}), s8[2097152]{0:T(1024)(128)(4,1)S(1)}, s32[]{:S(2)}) async-start(s8[6291456]{0:T(1024)(128)(4,1)} %bitcast.5), calls=%async_computation | async-start | bytes 4194304
  71.2 59.6 %collective-permute-start.5 = (bf16[6,128,512]{2,1,0:T(8,128)(2,1)}, bf16[6,128,512]{2,1,0:T(8,128)(2,1)}, u32[]{:S(2)}, u32[]{:S(2)}) collective-permute-start(bf16[6,128,512]{2,1,0:T(8,128)(2,1)} %gather.5.sent_ref), channel_id=1, source_target_pairs={{0,4},{4,8},{8,12},{12,0},{1,5},{5,9},{9,13},{13,1},{2,6},{6,10},{... | collective-permute-start | bytes 2359304 | tf_op jit(solution)/shard_map/ppermute | solution.py:366
  71.8 0.5 copy-start.11
  97.9 32.8 %collective-permute-start.1 = (bf16[6,128,512]{2,1,0:T(8,128)(2,1)}, bf16[6,128,512]{2,1,0:T(8,128)(2,1)S(1)}, u32[]{:S(2)}, u32[]{:S(2)}) collective-permute-start(bf16[6,128,512]{2,1,0:T(8,128)(2,1)} %gather.3), channel_id=1, source_target_pairs={{0,12},{4,0},{8,4},{12,8},{1,13},{5,1},{9,5},{13,9},{2,14},{6,2},{... | collective-permute-start | bytes 2359304 | tf_op jit(solution)/shard_map/ppermute | solution.py:366
  101.3 2.8 %copy-start = (bf16[16,2,6,128,128]{4,3,2,1,0:T(8,128)(2,1)S(1)}, bf16[16,2,6,128,128]{4,3,2,1,0:T(8,128)(2,1)}, u32[]{:S(2)}) copy-start(bf16[16,2,6,128,128]{4,3,2,1,0:T(8,128)(2,1)} %refs_4_.9) | copy-start | bytes 18874372
  104.1 1.6 copy-start.2
  105.7 1.1 copy-start.3
  106.9 23.9 %slice-start.1 = ((s8[6291456]{0:T(1024)(128)(4,1)}), s8[4194304]{0:T(1024)(128)(4,1)S(1)}, s32[]{:S(2)}) async-start(s8[6291456]{0:T(1024)(128)(4,1)} %bitcast.5), calls=%async_computation.1 | async-start | bytes 8388608
  106.9 23.9 %copy-start.1 = (bf16[2048,512]{1,0:T(8,128)(2,1)S(1)}, bf16[2048,512]{1,0:T(8,128)(2,1)}, u32[]{:S(2)}) copy-start(bf16[2048,512]{1,0:T(8,128)(2,1)} %param.8) | copy-start | bytes 6291460
  106.9 23.9 %copy-start.6 = (s32[192]{0:T(256)S(1)}, s32[192]{0:T(256)}, u32[]{:S(2)}) copy-start(s32[192]{0:T(256)} %get-tuple-element.11.loc_ref) | copy-start | bytes 2308
  139.8 95.3 %collective-permute-start.7 = (bf16[6,128,512]{2,1,0:T(8,128)(2,1)}, bf16[6,128,512]{2,1,0:T(8,128)(2,1)}, u32[]{:S(2)}, u32[]{:S(2)}) collective-permute-start(bf16[6,128,512]{2,1,0:T(8,128)(2,1)} %remote_terms.6.refs_8_), channel_id=1, source_target_pairs={{0,4},{4,8},{8,12},{12,0},{1,5},{5,9},{9,13},{13,1},{2,6},{6,10},{... | collective-permute-start | bytes 2359304 | tf_op jit(solution)/shard_map/ppermute | solution.py:366
  150.7 87.7 %collective-permute-start.6 = (bf16[6,128,512]{2,1,0:T(8,128)(2,1)}, bf16[6,128,512]{2,1,0:T(8,128)(2,1)}, u32[]{:S(2)}, u32[]{:S(2)}) collective-permute-start(bf16[6,128,512]{2,1,0:T(8,128)(2,1)} %remote_terms.7.refs_9_), channel_id=1, source_target_pairs={{0,12},{4,0},{8,4},{12,8},{1,13},{5,1},{9,5},{13,9},{2,14},{6,2},{... | collective-permute-start | bytes 2359304 | tf_op jit(solution)/shard_map/ppermute | solution.py:366
  152.5 6.7 %copy-start.14 = (s32[6]{0:T(128)S(1)}, s32[6]{0:T(128)}, u32[]{:S(2)}) copy-start(s32[6]{0:T(128)} %copy-done.13) | copy-start | bytes 76
  158.3 73.9 %collective-permute-start.8 = (bf16[4,128,512]{2,1,0:T(8,128)(2,1)S(1)}, bf16[4,128,512]{2,1,0:T(8,128)(2,1)}, u32[]{:S(2)}, u32[]{:S(2)}) collective-permute-start(bf16[4,128,512]{2,1,0:T(8,128)(2,1)S(1)} %remote_terms.5.refs_7_), channel_id=1, source_target_pairs={{0,8},{4,12},{8,0},{12,4},{1,9},{5,13},{9,1},{13,5},{2,10},{6,14},... | collective-permute-start | bytes 1572872 | tf_op jit(solution)/shard_map/ppermute | solution.py:366
  163.6 65.8 %collective-permute-start.9 = (bf16[2,128,512]{2,1,0:T(8,128)(2,1)}, bf16[2,128,512]{2,1,0:T(8,128)(2,1)}, u32[]{:S(2)}, u32[]{:S(2)}) collective-permute-start(bf16[2,128,512]{2,1,0:T(8,128)(2,1)} %remote_terms.4.refs_6_), channel_id=1, source_target_pairs={{0,8},{4,12},{8,0},{12,4},{1,9},{5,13},{9,1},{13,5},{2,10},{6,14},... | collective-permute-start | bytes 786440 | tf_op jit(solution)/shard_map/ppermute | solution.py:366
  232.2 3.0 %copy-start.12 = (s32[6]{0:T(128)S(1)}, s32[6]{0:T(128)}, u32[]{:S(2)}) copy-start(s32[6]{0:T(128)} %copy-done.11) | copy-start | bytes 76
  235.1 3.3 %copy-start.10 = (s32[6]{0:T(128)S(1)}, s32[6]{0:T(128)}, u32[]{:S(2)}) copy-start(s32[6]{0:T(128)} %copy-done.9) | copy-start | bytes 76

commit v2 on v1

v2 whole, which is shorter than its diff:
```python
import functools

import jax
import jax.numpy as jnp
from jax import lax
from jax.experimental import pallas as pl
from jax.experimental.pallas import tpu as pltpu
from jax.sharding import PartitionSpec as P

DISCOUNT = 0.95
VMEM_LIMIT = 40 * 1024 * 1024

SMEM_SPEC = pl.BlockSpec(memory_space=pltpu.SMEM)
ANY_SPEC = pl.BlockSpec(memory_space=pl.ANY)


def dot_f32(x, y, contract=(1, 0)):
    return lax.dot_general(
        x, y, (((contract[0],), (contract[1],)), ((), ())),
        precision=lax.Precision.HIGHEST, preferred_element_type=jnp.float32,
    )


def iota(shape, dim):
    return lax.broadcasted_iota(jnp.int32, shape, dim)


def plan_kernel(device_count, me_ref, dest_ref, counts_ref, *refs):
    request_refs = refs[: device_count - 1]
    source_refs = refs[device_count - 1 : 2 * (device_count - 1)]
    slot_ref, local_ref, mark_ref = refs[2 * (device_count - 1) :]
    entry_count, action_count, block_count = dest_ref.shape
    capacity = request_refs[0].shape[1]
    rows, places = slot_ref.shape[0], 8 * pl.cdiv(capacity, 8)
    me = me_ref[0]
    mark_ref[...] = jnp.zeros_like(mark_ref)
    local_ref[...] = jnp.zeros_like(local_ref)
    for n in range(entry_count):
        dest = dest_ref[n]
        owner = jnp.zeros_like(dest)
        for other in range(1, device_count):
            owner += (dest >= other * block_count).astype(jnp.int32)
        offset = owner - me
        offset = jnp.where(offset < 0, offset + device_count, offset)
        mark = jnp.where(n < counts_ref[...], offset, 0)
        mark_ref[n * action_count : (n + 1) * action_count, :] = mark
        local_ref[n * action_count : (n + 1) * action_count, :] = dest - owner * block_count
    mark, local = mark_ref[...], local_ref[...]
    row, lane = iota(mark.shape, 0), iota(mark.shape, 1)
    entry = row // action_count
    code = lane * 256 + (row - entry * action_count) * 16 + entry
    square = (block_count, block_count)
    before = (iota(square, 0) < iota(square, 1)).astype(jnp.float32)
    whole = jnp.ones(square, jnp.float32)
    tall = (mark.shape[0],) * 2
    above = (iota(tall, 1) < iota(tall, 0)).astype(jnp.float32)
    ones = jnp.ones((8, block_count), jnp.float32)
    slot = jnp.full(mark.shape, -1, jnp.int32)
    place_iota = iota((places, block_count), 0)
    for offset in range(1, device_count):
        hit = mark == offset
        hits = hit.astype(jnp.float32)
        place = (dot_f32(hits, before) + dot_f32(above, dot_f32(hits, whole))).astype(jnp.int32)
        slot = jnp.where(hit, (offset - 1) * capacity + place, slot)
        place = jnp.where(hit, place, -1)
        wants = jnp.zeros((places, block_count), jnp.int32)
        codes = jnp.zeros((places, block_count), jnp.int32)
        for r in range(entry_count * action_count):
            here = place[r : r + 1, :] == place_iota
            wants = jnp.where(here, local[r : r + 1, :] + 1, wants)
            codes = jnp.where(here, code[r : r + 1, :], codes)
        wants = dot_f32(ones, wants.astype(jnp.float32), (1, 1)).astype(jnp.int32) - 1
        codes = dot_f32(ones, codes.astype(jnp.float32), (1, 1)).astype(jnp.int32)
        request_refs[offset - 1][...] = wants[:1, :capacity]
        source_refs[offset - 1][...] = codes[:1, :capacity]
    slot_ref[...] = slot[:rows]


def make_plan(me, dest, counts, device_count, capacity):
    entry_count, action_count, block_count = dest.shape
    rows = entry_count * action_count
    padded = 8 * pl.cdiv(rows, 8)
    vmem = pl.BlockSpec(memory_space=pltpu.VMEM)
    outs = pl.pallas_call(
        functools.partial(plan_kernel, device_count),
        out_shape=[jax.ShapeDtypeStruct((1, capacity), jnp.int32)] * (2 * (device_count - 1))
        + [jax.ShapeDtypeStruct((rows, block_count), jnp.int32)],
        in_specs=[SMEM_SPEC, vmem, vmem],
        out_specs=[vmem] * (2 * device_count - 1),
        scratch_shapes=[pltpu.VMEM((padded, block_count), jnp.int32)] * 2,
        name="plan",
    )(me, dest, counts)
    return outs[: device_count - 1], outs[device_count - 1 : -1], outs[-1]


def gather_kernel(wanted_ref, value_ref, out_ref):
    del wanted_ref
    out_ref[...] = value_ref[...]


def gather_blocks(wanted, value_blocks):
    capacity = wanted.shape[1]
    block = (1,) + value_blocks.shape[1:]
    return pl.pallas_call(
        gather_kernel,
        out_shape=jax.ShapeDtypeStruct((capacity,) + value_blocks.shape[1:], value_blocks.dtype),
        grid_spec=pltpu.PrefetchScalarGridSpec(
            num_scalar_prefetch=1,
            grid=(capacity,),
            in_specs=[pl.BlockSpec(block, lambda k, wanted: (jnp.maximum(wanted[0, k], 0), 0, 0))],
            out_specs=pl.BlockSpec(block, lambda k, wanted: (k, 0, 0)),
        ),
        cost_estimate=pl.CostEstimate(flops=0, bytes_accessed=1 << 20, transcendentals=0),
        name="gather",
    )(wanted, value_blocks)


def local_forward_kernel(me_ref, dest_ref, counts_ref, value_ref, tiles_ref, util_ref, taste_ref, sent_ref, out_ref, acc_ref):
    del sent_ref
    block = pl.program_id(0)
    _, action_count, entry_count, tile_rows, _ = tiles_ref.shape
    block_count, _, width = value_ref.shape
    base = me_ref[0] * block_count
    for action in range(action_count):
        acc_ref[...] = jnp.zeros_like(acc_ref)
        for n in range(entry_count):
            rel = dest_ref[n, action, block] - base

            @pl.when((n < counts_ref[action, block]) & (rel >= 0) & (rel < block_count))
            def _():
                acc_ref[...] += jnp.dot(
                    tiles_ref[0, action, n], value_ref[rel], preferred_element_type=jnp.float32
                )

        util = jnp.broadcast_to(util_ref[action : action + 1, :], (tile_rows, tile_rows)).T
        taste = taste_ref[action : action + 1, :]
        for c in range(0, width, tile_rows):
            cols = slice(c, c + tile_rows)
            out_ref[0, action, :, cols] = (util + taste[:, cols]) + DISCOUNT * acc_ref[:, cols]


def local_forward(me, dest, counts, value_blocks, tiles, state_util, taste, sent):
    block_count, action_count, entry_count, tile_rows, _ = tiles.shape
    width = value_blocks.shape[2]
    return pl.pallas_call(
        local_forward_kernel,
        out_shape=jax.ShapeDtypeStruct((block_count, action_count, tile_rows, width), jnp.float32),
        grid_spec=pltpu.PrefetchScalarGridSpec(
            num_scalar_prefetch=3,
            grid=(block_count,),
            in_specs=[
                pl.BlockSpec(value_blocks.shape, lambda i, *_: (0, 0, 0)),
                pl.BlockSpec((1,) + tiles.shape[1:], lambda i, *_: (i, 0, 0, 0, 0)),
                pl.BlockSpec((action_count, tile_rows), lambda i, *_: (0, i)),
                pl.BlockSpec(taste.shape, lambda i, *_: (0, 0)),
                ANY_SPEC,
            ],
            out_specs=pl.BlockSpec((1, action_count, tile_rows, width), lambda i, *_: (i, 0, 0, 0)),
            scratch_shapes=[pltpu.VMEM((tile_rows, width), jnp.float32)],
        ),
        compiler_params=pltpu.CompilerParams(vmem_limit_bytes=VMEM_LIMIT),
        cost_estimate=pl.CostEstimate(flops=4 * 10**9, bytes_accessed=16 << 20, transcendentals=0),
        name="local_forward",
    )(me, dest, counts, value_blocks, tiles, state_util, taste, sent)


def add_remote(block, slot_ref, tiles_ref, incoming_refs, part_ref, scores_ref):
    _, action_count, entry_count, _, _ = tiles_ref.shape
    capacity = incoming_refs[0].shape[0]
    for action in range(action_count):
        scores_ref[action] = part_ref[0, action]
    for action in range(action_count):
        for n in range(entry_count):
            slot = slot_ref[n * action_count + action, block]

            @pl.when(slot >= 0)
            def _():
                for row, incoming_ref in enumerate(incoming_refs):
                    place = slot - row * capacity

                    @pl.when((place >= 0) & (place < capacity))
                    def _():
                        scores_ref[action] += DISCOUNT * jnp.dot(
                            tiles_ref[0, action, n], incoming_ref[place], preferred_element_type=jnp.float32
                        )


def transposed_dot(tile, rows):
    return lax.dot_general(tile, rows, (((0,), (0,)), ((), ())), preferred_element_type=jnp.float32)


def remote_terms_kernel(row_count, sent_count, src_ref, slot_ref, *refs):
    incoming_refs = refs[:row_count]
    part_ref, tiles_ref, cot_ref = refs[row_count : row_count + 3]
    out_ref, scores_ref, scaled_ref = refs[row_count + 3 + sent_count :]
    _, action_count, _, tile_rows, _ = tiles_ref.shape
    width = cot_ref.shape[2]
    code = src_ref[0, pl.program_id(0)]
    block, action, n = code >> 8, (code >> 4) & 15, code & 15
    add_remote(block, slot_ref, tiles_ref, incoming_refs, part_ref, scores_ref)
    for c in range(0, width, tile_rows):
        cols = slice(c, c + tile_rows)
        scores = [scores_ref[other, :, cols] for other in range(action_count)]
        largest = functools.reduce(jnp.maximum, scores)
        total = functools.reduce(jnp.add, [jnp.exp(x - largest) for x in scores])
        ratio = cot_ref[0, :, cols].astype(jnp.float32) / total
        grad = ratio * jnp.exp(scores_ref[action, :, cols] - largest)
        scaled_ref[:, cols] = (DISCOUNT * grad).astype(jnp.bfloat16)
    out_ref[0] = transposed_dot(tiles_ref[0, action, n], scaled_ref[...]).astype(jnp.bfloat16)


def remote_terms(src, slot, incoming, part, tiles, cot_blocks, sent):
    _, action_count, entry_count, tile_rows, _ = tiles.shape
    width = cot_blocks.shape[2]
    count = src.shape[1]
    return pl.pallas_call(
        functools.partial(remote_terms_kernel, len(incoming), len(sent)),
        out_shape=jax.ShapeDtypeStruct((count, tile_rows, width), jnp.bfloat16),
        grid_spec=pltpu.PrefetchScalarGridSpec(
            num_scalar_prefetch=2,
            grid=(count,),
            in_specs=[pl.BlockSpec(x.shape, lambda r, *_: (0, 0, 0)) for x in incoming]
            + [
                pl.BlockSpec((1,) + part.shape[1:], lambda r, src, *_: (src[0, r] >> 8, 0, 0, 0)),
                pl.BlockSpec((1,) + tiles.shape[1:], lambda r, src, *_: (src[0, r] >> 8, 0, 0, 0, 0)),
                pl.BlockSpec((1, tile_rows, width), lambda r, src, *_: (src[0, r] >> 8, 0, 0)),
            ]
            + [ANY_SPEC] * len(sent),
            out_specs=pl.BlockSpec((1, tile_rows, width), lambda r, *_: (r, 0, 0)),
            scratch_shapes=[
                pltpu.VMEM((action_count, tile_rows, width), jnp.float32),
                pltpu.VMEM((tile_rows, width), jnp.bfloat16),
            ],
        ),
        compiler_params=pltpu.CompilerParams(vmem_limit_bytes=VMEM_LIMIT),
        cost_estimate=pl.CostEstimate(flops=10**8, bytes_accessed=4 << 20, transcendentals=10**5),
        name="remote_terms",
    )(src, slot, *incoming, part, tiles, cot_blocks, *sent)


def finish_kernel(row_count, sent_count, util_scale, taste_scale, me_ref, dest_ref, slot_ref, counts_ref, *refs):
    incoming_refs = refs[:row_count]
    part_ref, tiles_ref, cot_ref = refs[row_count : row_count + 3]
    value_ref, adjoint_ref, util_ref, taste_ref, scores_ref, scaled_ref = refs[row_count + 3 + sent_count :]
    block = pl.program_id(0)
    _, action_count, entry_count, tile_rows, _ = tiles_ref.shape
    block_count = adjoint_ref.shape[0]
    width = value_ref.shape[1]
    base = me_ref[0] * block_count

    @pl.when(block == 0)
    def _():
        adjoint_ref[...] = jnp.zeros_like(adjoint_ref)
        taste_ref[...] = jnp.zeros_like(taste_ref)

    add_remote(block, slot_ref, tiles_ref, incoming_refs, part_ref, scores_ref)
    sums = [jnp.zeros((tile_rows, tile_rows), jnp.float32) for _ in range(action_count)]
    for c in range(0, width, tile_rows):
        cols = slice(c, c + tile_rows)
        scores = [scores_ref[action, :, cols] for action in range(action_count)]
        largest = functools.reduce(jnp.maximum, scores)
        powers = [jnp.exp(x - largest) for x in scores]
        total = functools.reduce(jnp.add, powers)
        value_ref[:, cols] = largest + jnp.log(total)
        ratio = cot_ref[0, :, cols].astype(jnp.float32) / total
        for action in range(action_count):
            grad = ratio * powers[action]
            scaled_ref[action, :, cols] = (DISCOUNT * grad).astype(jnp.bfloat16)
            sums[action] = sums[action] + grad
            taste_ref[action : action + 1, cols] += taste_scale * jnp.sum(grad, axis=0, keepdims=True)
    for action in range(action_count):
        util_ref[action : action + 1, :] = util_scale * jnp.sum(sums[action].T, axis=0, keepdims=True)
    for action in range(action_count):
        for n in range(entry_count):
            rel = dest_ref[n, action, block] - base

            @pl.when((n < counts_ref[action, block]) & (rel >= 0) & (rel < block_count))
            def _():
                adjoint_ref[rel] += transposed_dot(tiles_ref[0, action, n], scaled_ref[action])


def finish(me, dest, slot, counts, incoming, part, tiles, cot_blocks, sent, util_scale, taste_scale):
    block_count, action_count, entry_count, tile_rows, _ = tiles.shape
    width = cot_blocks.shape[2]
    states = block_count * tile_rows
    return pl.pallas_call(
        functools.partial(finish_kernel, len(incoming), len(sent), util_scale, taste_scale),
        out_shape=(
            jax.ShapeDtypeStruct((states, width), jnp.float32),
            jax.ShapeDtypeStruct((block_count, tile_rows, width), jnp.float32),
            jax.ShapeDtypeStruct((action_count, states), jnp.float32),
            jax.ShapeDtypeStruct((action_count, width), jnp.float32),
        ),
        grid_spec=pltpu.PrefetchScalarGridSpec(
            num_scalar_prefetch=4,
            grid=(block_count,),
            in_specs=[pl.BlockSpec(x.shape, lambda i, *_: (0, 0, 0)) for x in incoming]
            + [
                pl.BlockSpec((1,) + part.shape[1:], lambda i, *_: (i, 0, 0, 0)),
                pl.BlockSpec((1,) + tiles.shape[1:], lambda i, *_: (i, 0, 0, 0, 0)),
                pl.BlockSpec((1, tile_rows, width), lambda i, *_: (i, 0, 0)),
            ]
            + [ANY_SPEC] * len(sent),
            out_specs=(
                pl.BlockSpec((tile_rows, width), lambda i, *_: (i, 0)),
                pl.BlockSpec((block_count, tile_rows, width), lambda i, *_: (0, 0, 0)),
                pl.BlockSpec((action_count, tile_rows), lambda i, *_: (0, i)),
                pl.BlockSpec((action_count, width), lambda i, *_: (0, 0)),
            ),
            scratch_shapes=[
                pltpu.VMEM((action_count, tile_rows, width), jnp.float32),
                pltpu.VMEM((action_count, tile_rows, width), jnp.bfloat16),
            ],
        ),
        compiler_params=pltpu.CompilerParams(vmem_limit_bytes=VMEM_LIMIT),
        cost_estimate=pl.CostEstimate(flops=4 * 10**9, bytes_accessed=24 << 20, transcendentals=4 * 10**6),
        name="finish",
    )(me, dest, slot, counts, *incoming, part, tiles, cot_blocks, *sent)


def add_arrivals_kernel(wanted_ref, arrived_ref, base_ref, out_ref, held_ref, in_sems, out_sems):
    slots = arrived_ref.shape[0]
    target = [wanted_ref[0, k] for k in range(slots)]
    lead = []
    for k in range(slots):
        first = target[k] >= 0
        for other in range(k):
            first = first & (target[other] != target[k])
        lead.append(first)
    place = [jnp.maximum(t, 0) for t in target]
    fetch = [pltpu.make_async_copy(out_ref.at[place[k]], held_ref.at[k], in_sems.at[k]) for k in range(slots)]
    store = [pltpu.make_async_copy(held_ref.at[k], out_ref.at[place[k]], out_sems.at[k]) for k in range(slots)]
    for k in range(slots):

        @pl.when(lead[k])
        def _():
            fetch[k].start()

    for k in range(slots):

        @pl.when(lead[k])
        def _():
            fetch[k].wait()
            held_ref[k] += arrived_ref[k].astype(jnp.float32)
            for other in range(k + 1, slots):

                @pl.when(target[other] == target[k])
                def _():
                    held_ref[k] += arrived_ref[other].astype(jnp.float32)

            store[k].start()

    for k in range(slots):

        @pl.when(lead[k])
        def _():
            store[k].wait()


def add_arrivals(wanted, arrived, adjoint):
    slots = arrived.shape[0]
    return pl.pallas_call(
        add_arrivals_kernel,
        out_shape=jax.ShapeDtypeStruct(adjoint.shape, adjoint.dtype),
        in_specs=[SMEM_SPEC, pl.BlockSpec(memory_space=pltpu.VMEM), ANY_SPEC],
        out_specs=ANY_SPEC,
        scratch_shapes=[
            pltpu.VMEM(arrived.shape, jnp.float32),
            pltpu.SemaphoreType.DMA((slots,)),
            pltpu.SemaphoreType.DMA((slots,)),
        ],
        input_output_aliases={2: 0},
        compiler_params=pltpu.CompilerParams(vmem_limit_bytes=VMEM_LIMIT),
        cost_estimate=pl.CostEstimate(flops=10**6, bytes_accessed=4 << 20, transcendentals=0),
        name="add_arrivals",
    )(wanted, arrived, adjoint)


def local(value_in, cotangent, state_util, taste, tiles, dest_block, counts):
    block_count, action_count, entry_count, tile_rows, _ = tiles.shape
    width = value_in.shape[1]
    device_count = lax.axis_size("state")
    me = lax.axis_index("state").astype(jnp.int32).reshape(1)
    capacity = max(2, (block_count + device_count - 2) // (device_count - 1))
    value_blocks = value_in.reshape(block_count, tile_rows, width)
    cot_blocks = cotangent.reshape(block_count, tile_rows, width)
    offsets = range(1, device_count)
    order = sorted(offsets, key=lambda d: -min(d, device_count - d))

    def shift(x, offset):
        return lax.ppermute(x, "state", [(s, (s + offset) % device_count) for s in range(device_count)])

    def add_over(x, axis):
        size = lax.axis_size(axis)
        if size & (size - 1):
            return lax.psum(x, axis)
        step = 1
        while step < size:
            x = x + lax.ppermute(x, axis, [(s, s ^ step) for s in range(size)])
            step *= 2
        return x

    dest, counts = dest_block.transpose(2, 1, 0), counts.T
    request, source, slot = make_plan(me, dest, counts, device_count, capacity)
    wanted = {d: shift(request[d - 1], d) for d in order}
    outgoing = {d: gather_blocks(wanted[d], value_blocks) for d in order}
    incoming = {d: shift(outgoing[d], -d) for d in order}
    part = local_forward(me, dest, counts, value_blocks, tiles, state_util, taste, outgoing[order[-1]])
    held = [incoming[d] for d in offsets]

    returned = []
    sent = []
    for index, d in enumerate(order):
        cuts = [0, min(2, capacity), capacity] if index == 0 else [0, capacity]
        for lo, hi in zip(cuts[:-1], cuts[1:]):
            if lo < hi:
                terms = remote_terms(source[d - 1][:, lo:hi], slot, held, part, tiles, cot_blocks, sent[-1:])
                sent.append(terms)
                returned.append((wanted[d][:, lo:hi], shift(terms, d)))
    value_out, adjoint, util_part, taste_part = finish(
        me, dest, slot, counts, held, part, tiles, cot_blocks, sent,
        1.0 / (width * lax.axis_size("type")), 1.0 / (block_count * tile_rows * device_count),
    )
    util_total = add_over(util_part, "type")
    taste_total = add_over(taste_part, "state")
    for places, terms in returned:
        adjoint = add_arrivals(places, terms, adjoint)
    return value_out, adjoint.reshape(block_count * tile_rows, width), util_total, taste_total


def solution(mesh):
    return jax.shard_map(
        local,
        mesh=mesh,
        in_specs=(
            P(("groups", "state"), "type"),
            P(("groups", "state"), "type"),
            P(None, ("groups", "state")),
            P(None, ("groups", "type")),
            P(("groups", "state"), None, None, None, None),
            P(("groups", "state"), None, None),
            P(("groups", "state"), None),
        ),
        out_specs=(
            P(("groups", "state"), "type"),
            P(("groups", "state"), "type"),
            P(None, ("groups", "state")),
            P(None, ("groups", "type")),
        ),
        check_vma=False,
    )
```

time: 244 us -> 187 us (0.77)
  the two profiles are of different devices: /device:TPU:0 before, /device:TPU:30 now
where the time goes in v2:
time: 187 us; the launch traced here: 186 us
  Pallas kernels  107 us (57%)
  waiting for transfers between devices  37.8 us (20%)
  starting transfers between devices  31.2 us (17%)
  local copies, waits for them, and re-layouts  7.21 us (4%)
    pallas_call x1, Pallas kernels, finish(): pl.pallas_call(functools.partial(finish_kernel, len(incoming), len(sent),...  34.1 us
    pallas_call x4, Pallas kernels, remote_terms(): pl.pallas_call(functools.partial(remote_terms_kernel, len(incoming), len(...  24.7 us
    ppermute x10, starting transfers between devices, shift(): lax.ppermute(x, 'state', [(s, (s + offset) % device_count) for s in range...  22.2 us
    pallas_call x1, Pallas kernels, local_forward(): pl.pallas_call(local_forward_kernel, out_shape=jax.ShapeDtypeStruct((bloc...  21.4 us
    ppermute x4, waiting for transfers between devices, add_over(): x = x + lax.ppermute(x, axis, [(s, s ^ step) for s in range(size)])  19.2 us
    ppermute x10, waiting for transfers between devices, shift(): lax.ppermute(x, 'state', [(s, (s + offset) % device_count) for s in range...  18.6 us
    pallas_call x3, Pallas kernels, gather_blocks(): pl.pallas_call(gather_kernel, out_shape=jax.ShapeDtypeStruct((capacity,)...  14.5 us
    pallas_call x4, Pallas kernels, add_arrivals(): pl.pallas_call(add_arrivals_kernel, out_shape=jax.ShapeDtypeStruct(adjoin...  10.2 us
  transfers between devices with their start and end apart: 14, of which 7 were waited for; matrix products, arithmetic and copies ran while one was open for 1% of the time, Pallas kernels for 46%

profile of v2, /device:TPU:30, one launch (start us, length us, event | category | flops | bytes accessed | tf_op | source)
XLA Modules:
  0.0 185.6 jit_solution(15647257214332385324)
XLA Ops:
  0.6 2.2 %plan.1 = (s32[1,6]{1,0:T(1,128)}, s32[1,6]{1,0:T(1,128)}, s32[1,6]{1,0:T(1,128)}, s32[1,6]{1,0:T(1,128)}, s32[1,6]{1,0:T(1,128)}, /*index=5*/s32[1,6]{1,0:T(1,128)}, s32[12,16]{1,0:T(8,128)}) custom-call(s32[1]{0:T(128)} %bitcast.me_ref, s32[6,2,16]{2,1,0:T(2,128)} %bitcast.19, s32[2,16]{1,0:T(2,128)} %bitcast.22), custom_call_target="tpu_custom_call" | custom-call | tf_op jit(solution)/shard_map/plan/pallas_call | solution.py:84
  2.9 0.4 collective-permute-start.4
  3.3 0.3 collective-permute-start.2
  3.7 3.0 %collective-permute-start = (s32[1,6]{1,0:T(1,128)}, s32[1,6]{1,0:T(1,128)S(1)}, u32[]{:S(2)}, u32[]{:S(2)}) collective-permute-start(s32[1,6]{1,0:T(1,128)} %get-tuple-element.16), channel_id=1, source_target_pairs={{0,4},{4,8},{8,12},{12,0},{1,5},{5,9},{9,13},{13,1},{2,6},{6,10},{... | collective-permute-start | bytes 80 | tf_op jit(solution)/shard_map/ppermute | solution.py:391
  6.7 1.2 collective-permute-done.2.wanted_ref
  7.9 0.5 copy-done.13
  8.4 0.0 copy-start.8
  8.4 5.0 %gather.4 = bf16[6,128,512]{2,1,0:T(8,128)(2,1)} custom-call(s32[1,6]{1,0:T(1,128)} %copy-done.13, bf16[16,128,512]{2,1,0:T(8,128)(2,1)} %bitcast.15), custom_call_target="tpu_custom_call" | custom-call | bytes 1048576 | tf_op jit(solution)/shard_map/gather/pallas_call | solution.py:104
  13.4 0.9 collective-permute-start.3
  14.3 0.5 copy-done.9
  14.8 4.6 %gather.5.sent_ref = bf16[6,128,512]{2,1,0:T(8,128)(2,1)} custom-call(s32[1,6]{1,0:T(1,128)} %copy-done.9, bf16[16,128,512]{2,1,0:T(8,128)(2,1)} %bitcast.16), custom_call_target="tpu_custom_call" | custom-call | bytes 1048576 | tf_op jit(solution)/shard_map/gather/pallas_call | solution.py:104
  19.4 2.6 %collective-permute-start.5 = (bf16[6,128,512]{2,1,0:T(8,128)(2,1)}, bf16[6,128,512]{2,1,0:T(8,128)(2,1)}, u32[]{:S(2)}, u32[]{:S(2)}) collective-permute-start(bf16[6,128,512]{2,1,0:T(8,128)(2,1)} %gather.5.sent_ref), channel_id=1, source_target_pairs={{0,4},{4,8},{8,12},{12,0},{1,5},{5,9},{9,13},{13,1},{2,6},{6,10},{... | collective-permute-start | bytes 2359304 | tf_op jit(solution)/shard_map/ppermute | solution.py:391
  22.1 0.5 copy-done.11
  22.5 4.9 %gather.3 = bf16[6,128,512]{2,1,0:T(8,128)(2,1)} custom-call(s32[1,6]{1,0:T(1,128)} %copy-done.11, bf16[16,128,512]{2,1,0:T(8,128)(2,1)} %bitcast.17), custom_call_target="tpu_custom_call" | custom-call | bytes 1048576 | tf_op jit(solution)/shard_map/gather/pallas_call | solution.py:104
  27.4 0.1 collective-permute-start.1
  27.5 0.1 slice.13.src_ref
  27.6 0.0 copy-start
  27.6 2.8 %copy-done = bf16[16,2,6,128,128]{4,3,2,1,0:T(8,128)(2,1)S(1)} copy-done((bf16[16,2,6,128,128]{4,3,2,1,0:T(8,128)(2,1)S(1)}, bf16[16,2,6,128,128]{4,3,2,1,0:T(8,128)(2,1)}, u32[]{:S(2)}) %copy-start) | copy-done | bytes 6291480
  30.4 1.6 copy-done.2
  31.9 1.1 copy-done.3
  33.1 21.4 %local_forward.1.refs_3_ = f32[16,2,128,512]{3,2,1,0:T(8,128)} custom-call(s32[1]{0:T(128)} %bitcast.me_ref, s32[6,2,16]{2,1,0:T(2,128)S(1)} %bitcast.20, s32[2,16]{1,0:T(2,128)S(1)} %bitcast.23, bf16[16,128,512]{2,1,0:T(8,128)(2,1)S(1)} %bitcast.18, bf16[16,2,6,128,128]{4,3,2,1,0:T(8,128)(2,1)S(1)} %copy-done, f32[2,2048]{1,0:T(2,128)S(1)} %copy-done.6, ...), custom_call_target="tpu_custom_call" | custom-call | flops 4000000000 | bytes 16777216 | tf_op jit(solution)/shard_map/local_forward/pallas_call | solution.py:145
  54.5 12.2 %collective-permute-done.3.refs_1_ = bf16[6,128,512]{2,1,0:T(8,128)(2,1)S(1)} collective-permute-done((bf16[6,128,512]{2,1,0:T(8,128)(2,1)}, bf16[6,128,512]{2,1,0:T(8,128)(2,1)S(1)}, u32[]{:S(2)}, u32[]{:S(2)}) %collective-permute-start.3) | collective-permute-done | bytes 786464 | tf_op jit(solution)/shard_map/ppermute | solution.py:391
  66.7 5.2 %collective-permute-done.5.refs_2_ = bf16[6,128,512]{2,1,0:T(8,128)(2,1)} collective-permute-done((bf16[6,128,512]{2,1,0:T(8,128)(2,1)}, bf16[6,128,512]{2,1,0:T(8,128)(2,1)}, u32[]{:S(2)}, u32[]{:S(2)}) %collective-permute-start.5) | collective-permute-done | bytes 786464 | tf_op jit(solution)/shard_map/ppermute | solution.py:391
  71.9 3.7 %remote_terms.4.refs_6_ = bf16[2,128,512]{2,1,0:T(8,128)(2,1)S(1)} custom-call(s32[1,2]{1,0:T(1,128)S(1)} %bitcast.26, s32[12,16]{1,0:T(8,128)S(1)} %copy-done.4, bf16[6,128,512]{2,1,0:T(8,128)(2,1)S(1)} %collective-permute-done.1.refs_0_, bf16[6,128,512]{2,1,0:T(8,128)(2,1)S(1)} %collective-permute-done.3.refs_1_, ...), custom_call_target="tpu_custom_call" | custom-call | flops 100000000 | bytes 4194304 | tf_op jit(solution)/shard_map/remote_terms/pallas_call | solution.py:216
  75.7 5.6 %remote_terms.5.refs_6_.refs_7_ = bf16[4,128,512]{2,1,0:T(8,128)(2,1)S(1)} custom-call(s32[1,4]{1,0:T(1,128)S(1)} %slice.13.src_ref, s32[12,16]{1,0:T(8,128)S(1)} %copy-done.4, bf16[6,128,512]{2,1,0:T(8,128)(2,1)S(1)} %collective-permute-done.1.refs_0_, bf16[6,128,512]{2,1,0:T(8,128)(2,1)S(1)} %collective-permute-done.3.refs_1_, ...), custom_call_target="tpu_custom_call" | custom-call | flops 100000000 | bytes 4194304 | tf_op jit(solution)/shard_map/remote_terms/pallas_call | solution.py:216
  81.4 7.6 %remote_terms.6.refs_6_.refs_8_ = bf16[6,128,512]{2,1,0:T(8,128)(2,1)S(1)} custom-call(s32[1,6]{1,0:T(1,128)S(1)} %copy-done.16, s32[12,16]{1,0:T(8,128)S(1)} %copy-done.4, bf16[6,128,512]{2,1,0:T(8,128)(2,1)S(1)} %collective-permute-done.1.refs_0_, bf16[6,128,512]{2,1,0:T(8,128)(2,1)S(1)} %collective-permute-done.3.refs_1_, ...), custom_call_target="tpu_custom_call" | custom-call | flops 100000000 | bytes 4194304 | tf_op jit(solution)/shard_map/remote_terms/pallas_call | solution.py:216
  89.0 8.1 %collective-permute-start.7 = (bf16[6,128,512]{2,1,0:T(8,128)(2,1)S(1)}, bf16[6,128,512]{2,1,0:T(8,128)(2,1)S(1)}, u32[]{:S(2)}, u32[]{:S(2)}) collective-permute-start(bf16[6,128,512]{2,1,0:T(8,128)(2,1)S(1)} %remote_terms.6.refs_6_.refs_8_), channel_id=1, source_target_pairs={{0,4},{4,8},{8,12},{12,0},{1,5},{5,9},{9,13},{13,1},{2,6},{6,10},{... | collective-permute-start | bytes 2359304 | tf_op jit(solution)/shard_map/ppermute | solution.py:391
  97.1 7.6 %remote_terms.7.refs_9_ = bf16[6,128,512]{2,1,0:T(8,128)(2,1)S(1)} custom-call(s32[1,6]{1,0:T(1,128)S(1)} %copy-done.15, s32[12,16]{1,0:T(8,128)S(1)} %copy-done.4, bf16[6,128,512]{2,1,0:T(8,128)(2,1)S(1)} %collective-permute-done.1.refs_0_, bf16[6,128,512]{2,1,0:T(8,128)(2,1)S(1)} %collective-permute-done.3.refs_1_, ...), custom_call_target="tpu_custom_call" | custom-call | flops 100000000 | bytes 4194304 | tf_op jit(solution)/shard_map/remote_terms/pallas_call | solution.py:216
  104.7 3.3 %collective-permute-start.6 = (bf16[6,128,512]{2,1,0:T(8,128)(2,1)S(1)}, bf16[6,128,512]{2,1,0:T(8,128)(2,1)S(1)}, u32[]{:S(2)}, u32[]{:S(2)}) collective-permute-start(bf16[6,128,512]{2,1,0:T(8,128)(2,1)S(1)} %remote_terms.7.refs_9_), channel_id=1, source_target_pairs={{0,12},{4,0},{8,4},{12,8},{1,13},{5,1},{9,5},{13,9},{2,14},{6,2},{... | collective-permute-start | bytes 2359304 | tf_op jit(solution)/shard_map/ppermute | solution.py:391
  108.0 3.4 %collective-permute-start.8 = (bf16[4,128,512]{2,1,0:T(8,128)(2,1)S(1)}, bf16[4,128,512]{2,1,0:T(8,128)(2,1)S(1)}, u32[]{:S(2)}, u32[]{:S(2)}) collective-permute-start(bf16[4,128,512]{2,1,0:T(8,128)(2,1)S(1)} %remote_terms.5.refs_6_.refs_7_), channel_id=1, source_target_pairs={{0,8},{4,12},{8,0},{12,4},{1,9},{5,13},{9,1},{13,5},{2,10},{6,14},... | collective-permute-start | bytes 1572872 | tf_op jit(solution)/shard_map/ppermute | solution.py:391
  111.5 0.0 collective-permute-start.9
  111.5 34.1 %finish.1 = (f32[2048,512]{1,0:T(8,128)}, f32[16,128,512]{2,1,0:T(8,128)}, f32[2,2048]{1,0:T(2,128)S(1)}, f32[2,512]{1,0:T(2,128)S(1)}) custom-call(s32[1]{0:T(128)} %bitcast.me_ref, s32[6,2,16]{2,1,0:T(2,128)S(1)} %bitcast.21, s32[12,16]{1,0:T(8,128)S(1)} %copy-done.4, s32[2,16]{1,0:T(2,128)S(1)} %bitcast.24, ...), custom_call_target="tpu_custom_call" | custom-call | flops 4000000000 | bytes 25165824 | tf_op jit(solution)/shard_map/finish/pallas_call | solution.py:286
  145.6 5.1 %collective-permute-start.12 = (f32[2,512]{1,0:T(2,128)S(1)}, f32[2,512]{1,0:T(2,128)S(1)}, u32[]{:S(2)}, u32[]{:S(2)}) collective-permute-start(f32[2,512]{1,0:T(2,128)S(1)} %get-tuple-element.25), channel_id=1, source_target_pairs={{0,4},{4,0},{8,12},{12,8},{1,5},{5,1},{9,13},{13,9},{2,6},{6,2},{1... | collective-permute-start | bytes 12296 | tf_op jit(solution)/shard_map/ppermute | solution.py:399
  150.7 1.6 collective-permute-done.12
  152.3 1.2 collective-permute-done.10
  153.5 3.3 %collective-permute-start.13 = (f32[2,512]{1,0:T(2,128)S(1)}, f32[2,512]{1,0:T(2,128)S(1)}, u32[]{:S(2)}, u32[]{:S(2)}) collective-permute-start(f32[2,512]{1,0:T(2,128)S(1)} %add.14), channel_id=1, source_target_pairs={{0,8},{4,12},{8,0},{12,4},{1,9},{5,13},{9,1},{13,5},{2,10},{6,14},... | collective-permute-start | bytes 12296 | tf_op jit(solution)/shard_map/ppermute | solution.py:399
  156.8 14.0 %collective-permute-done.13 = f32[2,512]{1,0:T(2,128)S(1)} collective-permute-done((f32[2,512]{1,0:T(2,128)S(1)}, f32[2,512]{1,0:T(2,128)S(1)}, u32[]{:S(2)}, u32[]{:S(2)}) %collective-permute-start.13) | collective-permute-done | bytes 4128 | tf_op jit(solution)/shard_map/ppermute | solution.py:399
  170.8 0.5 collective-permute-start.11
  171.3 0.1 slice.14.wanted_ref
  171.4 0.6 add.15
  172.0 2.5 %collective-permute-done.11 = f32[2,2048]{1,0:T(2,128)S(1)} collective-permute-done((f32[2,2048]{1,0:T(2,128)S(1)}, f32[2,2048]{1,0:T(2,128)S(1)}, u32[]{:S(2)}, u32[]{:S(2)}) %collective-permute-start.11) | collective-permute-done | bytes 16416 | tf_op jit(solution)/shard_map/ppermute | solution.py:399
  174.5 0.6 add.13
  175.2 0.0 collective-permute-done.9.arrived_ref
  175.2 2.3 %add_arrivals.4.base_ref = f32[16,128,512]{2,1,0:T(8,128)} custom-call(s32[1,2]{1,0:T(1,128)S(1)} %bitcast.25, bf16[2,128,512]{2,1,0:T(8,128)(2,1)S(1)} %collective-permute-done.9.arrived_ref, f32[16,128,512]{2,1,0:T(8,128)} %get-tuple-element.23.base_ref), custom_call_target="tpu_custom_call", output_to_operand_aliasing={{}: (2, {})} | custom-call | flops 1000000 | bytes 4194304 | tf_op jit(solution)/shard_map/add_arrivals/pallas_call | solution.py:362
  177.5 0.0 collective-permute-done.8.arrived_ref
  177.5 2.6 %add_arrivals.5.base_ref = f32[16,128,512]{2,1,0:T(8,128)} custom-call(s32[1,4]{1,0:T(1,128)S(1)} %slice.14.wanted_ref, bf16[4,128,512]{2,1,0:T(8,128)(2,1)S(1)} %collective-permute-done.8.arrived_ref, f32[16,128,512]{2,1,0:T(8,128)} %add_arrivals.4.base_ref), custom_call_target="tpu_custom_call", output_to_operand_aliasing={{}: (2, {})} | custom-call | flops 1000000 | bytes 4194304 | tf_op jit(solution)/shard_map/add_arrivals/pallas_call | solution.py:362
  180.1 2.7 %add_arrivals.6.base_ref = f32[16,128,512]{2,1,0:T(8,128)} custom-call(s32[1,6]{1,0:T(1,128)S(1)} %copy-done.12, bf16[6,128,512]{2,1,0:T(8,128)(2,1)S(1)} %collective-permute-done.7.arrived_ref, f32[16,128,512]{2,1,0:T(8,128)} %add_arrivals.5.base_ref), custom_call_target="tpu_custom_call", output_to_operand_aliasing={{}: (2, {})} | custom-call | flops 1000000 | bytes 4194304 | tf_op jit(solution)/shard_map/add_arrivals/pallas_call | solution.py:362
  182.9 2.5 %add_arrivals.7 = f32[16,128,512]{2,1,0:T(8,128)} custom-call(s32[1,6]{1,0:T(1,128)S(1)} %copy-done.10, bf16[6,128,512]{2,1,0:T(8,128)(2,1)S(1)} %collective-permute-done.6.arrived_ref, f32[16,128,512]{2,1,0:T(8,128)} %add_arrivals.6.base_ref), custom_call_target="tpu_custom_call", output_to_operand_aliasing={{}: (2, {})} | custom-call | flops 1000000 | bytes 4194304 | tf_op jit(solution)/shard_map/add_arrivals/pallas_call | solution.py:362
  (41 shorter events, 0.1 us)
Async XLA Ops:
  2.9 11.4 %collective-permute-start.4 = (s32[1,6]{1,0:T(1,128)}, s32[1,6]{1,0:T(1,128)S(1)}, u32[]{:S(2)}, u32[]{:S(2)}) collective-permute-start(s32[1,6]{1,0:T(1,128)} %get-tuple-element.18), channel_id=1, source_target_pairs={{0,12},{4,0},{8,4},{12,8},{1,13},{5,1},{9,5},{13,9},{2,14},{6,2},{... | collective-permute-start | bytes 80 | tf_op jit(solution)/shard_map/ppermute | solution.py:391
  3.3 4.6 %collective-permute-start.2 = (s32[1,6]{1,0:T(1,128)}, s32[1,6]{1,0:T(1,128)S(1)}, u32[]{:S(2)}, u32[]{:S(2)}) collective-permute-start(s32[1,6]{1,0:T(1,128)} %get-tuple-element.17), channel_id=1, source_target_pairs={{0,8},{4,12},{8,0},{12,4},{1,9},{5,13},{9,1},{13,5},{2,10},{6,14},... | collective-permute-start | bytes 80 | tf_op jit(solution)/shard_map/ppermute | solution.py:391
  3.7 18.4 %collective-permute-start = (s32[1,6]{1,0:T(1,128)}, s32[1,6]{1,0:T(1,128)S(1)}, u32[]{:S(2)}, u32[]{:S(2)}) collective-permute-start(s32[1,6]{1,0:T(1,128)} %get-tuple-element.16), channel_id=1, source_target_pairs={{0,4},{4,8},{8,12},{12,0},{1,5},{5,9},{9,13},{13,1},{2,6},{6,10},{... | collective-permute-start | bytes 80 | tf_op jit(solution)/shard_map/ppermute | solution.py:391
  7.9 0.5 copy-start.13
  8.4 19.1 %copy-start.17 = (s32[1,6]{1,0:T(1,128)S(1)}, s32[1,6]{1,0:T(1,128)}, u32[]{:S(2)}) copy-start(s32[1,6]{1,0:T(1,128)} %get-tuple-element.19) | copy-start | bytes 76
  8.4 19.1 %copy-start.5 = (s32[16,2,6]{0,1,2:T(2,128)S(1)}, s32[16,2,6]{0,1,2:T(2,128)}, u32[]{:S(2)}) copy-start(s32[16,2,6]{0,1,2:T(2,128)} %param.12) | copy-start | bytes 2308
  8.4 19.1 %copy-start.6 = (f32[2,2048]{1,0:T(2,128)S(1)}, f32[2,2048]{1,0:T(2,128)}, u32[]{:S(2)}) copy-start(f32[2,2048]{1,0:T(2,128)} %util_ref.1) | copy-start | bytes 49156
  8.4 19.1 %copy-start.7 = (s32[16,2]{0,1:T(2,128)S(1)}, s32[16,2]{0,1:T(2,128)}, u32[]{:S(2)}) copy-start(s32[16,2]{0,1:T(2,128)} %param.13) | copy-start | bytes 388
  8.4 19.1 %copy-start.8 = (f32[2,512]{1,0:T(2,128)S(1)}, f32[2,512]{1,0:T(2,128)}, u32[]{:S(2)}) copy-start(f32[2,512]{1,0:T(2,128)} %taste_ref.1) | copy-start | bytes 12292
  13.4 53.3 %collective-permute-start.3 = (bf16[6,128,512]{2,1,0:T(8,128)(2,1)}, bf16[6,128,512]{2,1,0:T(8,128)(2,1)S(1)}, u32[]{:S(2)}, u32[]{:S(2)}) collective-permute-start(bf16[6,128,512]{2,1,0:T(8,128)(2,1)} %gather.4), channel_id=1, source_target_pairs={{0,8},{4,12},{8,0},{12,4},{1,9},{5,13},{9,1},{13,5},{2,10},{6,14},... | collective-permute-start | bytes 2359304 | tf_op jit(solution)/shard_map/ppermute | solution.py:391
  14.3 0.5 copy-start.9
  14.8 57.1 %slice-start = ((s8[6291456]{0:T(1024)(128)(4,1)}), s8[2097152]{0:T(1024)(128)(4,1)S(1)}, s32[]{:S(2)}) async-start(s8[6291456]{0:T(1024)(128)(4,1)} %bitcast.8), calls=%async_computation | async-start | bytes 4194304
  19.4 52.5 %collective-permute-start.5 = (bf16[6,128,512]{2,1,0:T(8,128)(2,1)}, bf16[6,128,512]{2,1,0:T(8,128)(2,1)}, u32[]{:S(2)}, u32[]{:S(2)}) collective-permute-start(bf16[6,128,512]{2,1,0:T(8,128)(2,1)} %gather.5.sent_ref), channel_id=1, source_target_pairs={{0,4},{4,8},{8,12},{12,0},{1,5},{5,9},{9,13},{13,1},{2,6},{6,10},{... | collective-permute-start | bytes 2359304 | tf_op jit(solution)/shard_map/ppermute | solution.py:391
  22.1 0.5 copy-start.11
  27.4 44.5 %collective-permute-start.1 = (bf16[6,128,512]{2,1,0:T(8,128)(2,1)}, bf16[6,128,512]{2,1,0:T(8,128)(2,1)S(1)}, u32[]{:S(2)}, u32[]{:S(2)}) collective-permute-start(bf16[6,128,512]{2,1,0:T(8,128)(2,1)} %gather.3), channel_id=1, source_target_pairs={{0,12},{4,0},{8,4},{12,8},{1,13},{5,1},{9,5},{13,9},{2,14},{6,2},{... | collective-permute-start | bytes 2359304 | tf_op jit(solution)/shard_map/ppermute | solution.py:391
  27.6 2.8 %copy-start = (bf16[16,2,6,128,128]{4,3,2,1,0:T(8,128)(2,1)S(1)}, bf16[16,2,6,128,128]{4,3,2,1,0:T(8,128)(2,1)}, u32[]{:S(2)}) copy-start(bf16[16,2,6,128,128]{4,3,2,1,0:T(8,128)(2,1)} %refs_4_.9) | copy-start | bytes 18874372
  30.4 1.6 copy-start.2
  31.9 1.1 copy-start.3
  33.1 38.8 %slice-start.1 = ((s8[6291456]{0:T(1024)(128)(4,1)}), s8[4194304]{0:T(1024)(128)(4,1)S(1)}, s32[]{:S(2)}) async-start(s8[6291456]{0:T(1024)(128)(4,1)} %bitcast.8), calls=%async_computation.1 | async-start | bytes 8388608
  33.1 38.8 %copy-start.1 = (bf16[2048,512]{1,0:T(8,128)(2,1)S(1)}, bf16[2048,512]{1,0:T(8,128)(2,1)}, u32[]{:S(2)}) copy-start(bf16[2048,512]{1,0:T(8,128)(2,1)} %param.8) | copy-start | bytes 6291460
  33.1 38.8 %copy-start.4 = (s32[12,16]{1,0:T(8,128)S(1)}, s32[12,16]{1,0:T(8,128)}, u32[]{:S(2)}) copy-start(s32[12,16]{1,0:T(8,128)} %get-tuple-element.15.slot_ref) | copy-start | bytes 2308
  75.7 5.7 %copy-start.16 = (s32[1,6]{1,0:T(1,128)S(1)}, s32[1,6]{1,0:T(1,128)}, u32[]{:S(2)}) copy-start(s32[1,6]{1,0:T(1,128)} %get-tuple-element.20.src_ref) | copy-start | bytes 76
  81.3 15.7 %copy-start.15 = (s32[1,6]{1,0:T(1,128)S(1)}, s32[1,6]{1,0:T(1,128)}, u32[]{:S(2)}) copy-start(s32[1,6]{1,0:T(1,128)} %get-tuple-element.21.src_ref) | copy-start | bytes 76
  89.0 91.1 %collective-permute-start.7 = (bf16[6,128,512]{2,1,0:T(8,128)(2,1)S(1)}, bf16[6,128,512]{2,1,0:T(8,128)(2,1)S(1)}, u32[]{:S(2)}, u32[]{:S(2)}) collective-permute-start(bf16[6,128,512]{2,1,0:T(8,128)(2,1)S(1)} %remote_terms.6.refs_6_.refs_8_), channel_id=1, source_target_pairs={{0,4},{4,8},{8,12},{12,0},{1,5},{5,9},{9,13},{13,1},{2,6},{6,10},{... | collective-permute-start | bytes 2359304 | tf_op jit(solution)/shard_map/ppermute | solution.py:391
  104.7 66.6 %copy-start.14 = (s32[1,6]{1,0:T(1,128)S(1)}, s32[1,6]{1,0:T(1,128)}, u32[]{:S(2)}) copy-start(s32[1,6]{1,0:T(1,128)} %copy-done.13) | copy-start | bytes 76
  104.7 78.1 %collective-permute-start.6 = (bf16[6,128,512]{2,1,0:T(8,128)(2,1)S(1)}, bf16[6,128,512]{2,1,0:T(8,128)(2,1)S(1)}, u32[]{:S(2)}, u32[]{:S(2)}) collective-permute-start(bf16[6,128,512]{2,1,0:T(8,128)(2,1)S(1)} %remote_terms.7.refs_9_), channel_id=1, source_target_pairs={{0,12},{4,0},{8,4},{12,8},{1,13},{5,1},{9,5},{13,9},{2,14},{6,2},{... | collective-permute-start | bytes 2359304 | tf_op jit(solution)/shard_map/ppermute | solution.py:391
  108.0 69.5 %collective-permute-start.8 = (bf16[4,128,512]{2,1,0:T(8,128)(2,1)S(1)}, bf16[4,128,512]{2,1,0:T(8,128)(2,1)S(1)}, u32[]{:S(2)}, u32[]{:S(2)}) collective-permute-start(bf16[4,128,512]{2,1,0:T(8,128)(2,1)S(1)} %remote_terms.5.refs_6_.refs_7_), channel_id=1, source_target_pairs={{0,8},{4,12},{8,0},{12,4},{1,9},{5,13},{9,1},{13,5},{2,10},{6,14},... | collective-permute-start | bytes 1572872 | tf_op jit(solution)/shard_map/ppermute | solution.py:391
  111.5 63.7 %collective-permute-start.9 = (bf16[2,128,512]{2,1,0:T(8,128)(2,1)S(1)}, bf16[2,128,512]{2,1,0:T(8,128)(2,1)S(1)}, u32[]{:S(2)}, u32[]{:S(2)}) collective-permute-start(bf16[2,128,512]{2,1,0:T(8,128)(2,1)S(1)} %remote_terms.4.refs_6_), channel_id=1, source_target_pairs={{0,8},{4,12},{8,0},{12,4},{1,9},{5,13},{9,1},{13,5},{2,10},{6,14},... | collective-permute-start | bytes 786440 | tf_op jit(solution)/shard_map/ppermute | solution.py:391
  145.6 6.7 %collective-permute-start.12 = (f32[2,512]{1,0:T(2,128)S(1)}, f32[2,512]{1,0:T(2,128)S(1)}, u32[]{:S(2)}, u32[]{:S(2)}) collective-permute-start(f32[2,512]{1,0:T(2,128)S(1)} %get-tuple-element.25), channel_id=1, source_target_pairs={{0,4},{4,0},{8,12},{12,8},{1,5},{5,1},{9,13},{13,9},{2,6},{6,2},{1... | collective-permute-start | bytes 12296 | tf_op jit(solution)/shard_map/ppermute | solution.py:399
  152.3 1.2 collective-permute-start.10
  153.5 17.3 %collective-permute-start.13 = (f32[2,512]{1,0:T(2,128)S(1)}, f32[2,512]{1,0:T(2,128)S(1)}, u32[]{:S(2)}, u32[]{:S(2)}) collective-permute-start(f32[2,512]{1,0:T(2,128)S(1)} %add.14), channel_id=1, source_target_pairs={{0,8},{4,12},{8,0},{12,4},{1,9},{5,13},{9,1},{13,5},{2,10},{6,14},... | collective-permute-start | bytes 12296 | tf_op jit(solution)/shard_map/ppermute | solution.py:399
  170.8 3.7 %collective-permute-start.11 = (f32[2,2048]{1,0:T(2,128)S(1)}, f32[2,2048]{1,0:T(2,128)S(1)}, u32[]{:S(2)}, u32[]{:S(2)}) collective-permute-start(f32[2,2048]{1,0:T(2,128)S(1)} %add.12), channel_id=1, source_target_pairs={{0,2},{1,3},{2,0},{3,1},{4,6},{5,7},{6,4},{7,5},{8,10},{9,11},{10,... | collective-permute-start | bytes 49160 | tf_op jit(solution)/shard_map/ppermute | solution.py:399
  177.5 2.6 %copy-start.12 = (s32[1,6]{1,0:T(1,128)S(1)}, s32[1,6]{1,0:T(1,128)}, u32[]{:S(2)}) copy-start(s32[1,6]{1,0:T(1,128)} %copy-done.11) | copy-start | bytes 76
  180.1 2.8 %copy-start.10 = (s32[1,6]{1,0:T(1,128)S(1)}, s32[1,6]{1,0:T(1,128)}, u32[]{:S(2)}) copy-start(s32[1,6]{1,0:T(1,128)} %copy-done.9) | copy-start | bytes 76

commit v3 on v0

v3 whole, which is shorter than its diff:
```python
import functools

import jax
import jax.numpy as jnp
from jax import lax
from jax.experimental import pallas as pl
from jax.experimental.pallas import tpu as pltpu
from jax.sharding import PartitionSpec as P

DISCOUNT = 0.95
VMEM_LIMIT = 12 * 1024 * 1024

SMEM_SPEC = pl.BlockSpec(memory_space=pltpu.SMEM)
ANY_SPEC = pl.BlockSpec(memory_space=pl.ANY)
HBM_SPEC = pl.BlockSpec(memory_space=pltpu.HBM)
VMEM_SPEC = pl.BlockSpec(memory_space=pltpu.VMEM)
PARAMS = pltpu.CompilerParams(vmem_limit_bytes=VMEM_LIMIT)
SMALL_COST = pl.CostEstimate(flops=1000, bytes_accessed=1000, transcendentals=0)


def dot_counts(x, y, contract=(1, 0)):
    return lax.dot_general(
        x.astype(jnp.float32).astype(jnp.bfloat16), y.astype(jnp.float32).astype(jnp.bfloat16),
        (((contract[0],), (contract[1],)), ((), ())), preferred_element_type=jnp.float32,
    )


def iota(shape, dim):
    return lax.broadcasted_iota(jnp.int32, shape, dim)


def plan_kernel(device_count, me_ref, dest_hbm_ref, counts_hbm_ref, *refs):
    request_refs = refs[: device_count - 1]
    source_refs = refs[device_count - 1 : 2 * (device_count - 1)]
    dest_ref, counts_ref, mark_ref, local_ref, sems = refs[2 * (device_count - 1) :]
    copies = [
        pltpu.make_async_copy(dest_hbm_ref, dest_ref, sems.at[0]),
        pltpu.make_async_copy(counts_hbm_ref, counts_ref, sems.at[1]),
    ]
    for copy in copies:
        copy.start()
    entry_count, action_count, block_count = dest_ref.shape
    capacity = request_refs[0].shape[1]
    places = 8 * pl.cdiv(capacity, 8)
    me = me_ref[0]
    mark_ref[...] = jnp.zeros_like(mark_ref)
    local_ref[...] = jnp.zeros_like(local_ref)
    for copy in copies:
        copy.wait()
    for n in range(entry_count):
        dest = dest_ref[n]
        owner = jnp.zeros_like(dest)
        for other in range(1, device_count):
            owner += (dest >= other * block_count).astype(jnp.int32)
        offset = owner - me
        offset = jnp.where(offset < 0, offset + device_count, offset)
        mark = jnp.where(n < counts_ref[...], offset, 0)
        mark_ref[n * action_count : (n + 1) * action_count, :] = mark
        local_ref[n * action_count : (n + 1) * action_count, :] = dest - owner * block_count
    mark, local = mark_ref[...], local_ref[...]
    row, lane = iota(mark.shape, 0), iota(mark.shape, 1)
    square = (block_count, block_count)
    before = iota(square, 0) < iota(square, 1)
    whole = jnp.ones(square, jnp.int32)
    tall = (mark.shape[0],) * 2
    above = iota(tall, 1) < iota(tall, 0)
    ones = jnp.ones((8, block_count), jnp.int32)
    place_iota = iota((places, block_count), 0)
    for offset in range(1, device_count):
        hit = mark == offset
        place = (dot_counts(hit, before) + dot_counts(above, dot_counts(hit, whole))).astype(jnp.int32)
        place = jnp.where(hit, place, -1)
        wants = jnp.zeros((places, block_count), jnp.int32)
        blocks = jnp.zeros((places, block_count), jnp.int32)
        lists = jnp.zeros((places, block_count), jnp.int32)
        for r in range(entry_count * action_count):
            here = place[r : r + 1, :] == place_iota
            wants = jnp.where(here, local[r : r + 1, :] + 1, wants)
            blocks = jnp.where(here, lane[r : r + 1, :], blocks)
            lists = jnp.where(here, row[r : r + 1, :], lists)
        wants, blocks, lists = (dot_counts(ones, x, (1, 1)).astype(jnp.int32) for x in (wants, blocks, lists))
        entry = lists // action_count
        codes = jnp.where(wants > 0, blocks * 256 + (lists - entry * action_count) * 16 + entry, -1)
        request_refs[offset - 1][...] = (wants - 1)[:1, :capacity]
        source_refs[offset - 1][...] = codes[:1, :capacity]


def make_plan(me, dest, counts, device_count, capacity):
    entry_count, action_count, block_count = dest.shape
    padded = 8 * pl.cdiv(entry_count * action_count, 8)
    outs = pl.pallas_call(
        functools.partial(plan_kernel, device_count),
        out_shape=[jax.ShapeDtypeStruct((1, capacity), jnp.int32)] * (2 * (device_count - 1)),
        in_specs=[SMEM_SPEC, HBM_SPEC, HBM_SPEC],
        out_specs=[VMEM_SPEC] * (2 * (device_count - 1)),
        scratch_shapes=[pltpu.VMEM(dest.shape, jnp.int32), pltpu.VMEM(counts.shape, jnp.int32)]
        + [pltpu.VMEM((padded, block_count), jnp.int32)] * 2
        + [pltpu.SemaphoreType.DMA((2,))],
        compiler_params=PARAMS,
        cost_estimate=SMALL_COST,
        name="plan",
    )(me, dest, counts)
    return outs[: device_count - 1], outs[device_count - 1 :]


def stage_kernel(value_ref, plan_ref, out_ref):
    del plan_ref
    for block in range(out_ref.shape[0]):
        out_ref[block] = value_ref[block]


def stage(value_blocks, plan):
    return pl.pallas_call(
        stage_kernel,
        out_shape=jax.ShapeDtypeStruct(value_blocks.shape, value_blocks.dtype),
        in_specs=[VMEM_SPEC, ANY_SPEC],
        out_specs=VMEM_SPEC,
        compiler_params=PARAMS,
        cost_estimate=SMALL_COST,
        name="stage",
    )(value_blocks, plan)


def gather_kernel(wanted_ref, value_ref, out_ref):
    for k in range(out_ref.shape[0]):
        out_ref[k] = value_ref[jnp.maximum(wanted_ref[0, k], 0)]


def gather_blocks(wanted, value_blocks):
    return pl.pallas_call(
        gather_kernel,
        out_shape=jax.ShapeDtypeStruct(wanted.shape[1:] + value_blocks.shape[1:], value_blocks.dtype),
        in_specs=[SMEM_SPEC, VMEM_SPEC],
        out_specs=VMEM_SPEC,
        compiler_params=PARAMS,
        cost_estimate=SMALL_COST,
        name="gather",
    )(wanted, value_blocks)


def local_forward_kernel(me_ref, dest_ref, counts_ref, value_ref, tiles_ref, util_ref, taste_ref, sent_ref, out_ref):
    del sent_ref
    block_count, action_count, entry_count, tile_rows, _ = tiles_ref.shape
    width = value_ref.shape[2]
    base = me_ref[0] * block_count

    def one_block(block, carry):
        states = pl.ds(pl.multiple_of(block * tile_rows, tile_rows), tile_rows)
        for action in range(action_count):
            left, right = [], []
            for n in range(entry_count):
                rel = dest_ref[n, action, block] - base
                here = (n < counts_ref[action, block]) & (rel >= 0) & (rel < block_count)
                tile = tiles_ref[block, action, n]
                left.append(jnp.where(here, tile, jnp.zeros_like(tile)))
                right.append(value_ref[jnp.where(here, rel, 0)])
            cont = jnp.dot(
                jnp.concatenate(left, axis=1), jnp.concatenate(right, axis=0), preferred_element_type=jnp.float32
            )
            util = jnp.broadcast_to(util_ref[action : action + 1, states], (tile_rows, tile_rows)).T
            taste = taste_ref[action : action + 1, :]
            for c in range(0, width, tile_rows):
                cols = slice(c, c + tile_rows)
                out_ref[block, action, :, cols] = (util + taste[:, cols]) + DISCOUNT * cont[:, cols]
        return carry

    lax.fori_loop(0, block_count, one_block, 0)


def local_forward(me, dest, counts, value_blocks, tiles, state_util, taste, sent):
    block_count, action_count, _, tile_rows, _ = tiles.shape
    return pl.pallas_call(
        local_forward_kernel,
        out_shape=jax.ShapeDtypeStruct((block_count, action_count, tile_rows, value_blocks.shape[2]), jnp.float32),
        in_specs=[SMEM_SPEC] * 3 + [VMEM_SPEC] * 4 + [ANY_SPEC],
        out_specs=VMEM_SPEC,
        compiler_params=PARAMS,
        cost_estimate=SMALL_COST,
        name="local_forward",
    )(me, dest, counts, value_blocks, tiles, state_util, taste, sent)


def unpack(code):
    return code >> 8, (code >> 4) & 15, code & 15


def add_rows(source_ref, incoming_ref, tiles_ref, scores_ref):
    for k in range(incoming_ref.shape[0]):
        code = source_ref[0, k]
        block, action, n = unpack(jnp.maximum(code, 0))
        tile = tiles_ref[block, action, n]
        tile = jnp.where(code >= 0, tile, jnp.zeros_like(tile))
        scores_ref[block, action] += DISCOUNT * jnp.dot(tile, incoming_ref[k], preferred_element_type=jnp.float32)


def add_incoming_kernel(source_ref, incoming_ref, tiles_ref, scores_in_ref, scores_ref):
    del scores_in_ref
    add_rows(source_ref, incoming_ref, tiles_ref, scores_ref)


def add_incoming(source, incoming, tiles, scores):
    return pl.pallas_call(
        add_incoming_kernel,
        out_shape=jax.ShapeDtypeStruct(scores.shape, scores.dtype),
        in_specs=[SMEM_SPEC] + [VMEM_SPEC] * 3,
        out_specs=VMEM_SPEC,
        input_output_aliases={3: 0},
        compiler_params=PARAMS,
        cost_estimate=SMALL_COST,
        name="add_incoming",
    )(source, incoming, tiles, scores)


def soft_max(scores):
    largest = functools.reduce(jnp.maximum, scores)
    if len(scores) == 2:
        ahead = scores[0] >= scores[1]
        power = jnp.exp(-jnp.abs(scores[0] - scores[1]))
        return largest, [jnp.where(ahead, 1.0, power), jnp.where(ahead, power, 1.0)], 1.0 + power
    powers = [jnp.exp(x - largest) for x in scores]
    return largest, powers, functools.reduce(jnp.add, powers)


def transposed_dot(tile, rows):
    return lax.dot_general(tile, rows, (((0,), (0,)), ((), ())), preferred_element_type=jnp.float32)


def lead_terms_kernel(row_count, *refs):
    last_refs, incoming_refs = refs[:row_count], refs[row_count : 2 * row_count]
    source_ref, tiles_ref, cot_ref, _, scores_ref, out_ref, scaled_ref = refs[2 * row_count :]
    for last_ref, incoming_ref in zip(last_refs, incoming_refs):
        add_rows(last_ref, incoming_ref, tiles_ref, scores_ref)
    _, action_count, _, tile_rows, _ = tiles_ref.shape
    capacity = source_ref.shape[1]
    width = cot_ref.shape[2]

    def one_term(k, carry):
        code = source_ref[0, k]

        @pl.when(code >= 0)
        def _():
            block, action, n = unpack(code)
            for c in range(0, width, tile_rows):
                cols = slice(c, c + tile_rows)
                _, powers, total = soft_max([scores_ref[block, other, :, cols] for other in range(action_count)])
                power = powers[0]
                for other in range(1, action_count):
                    power = jnp.where(action == other, powers[other], power)
                grad = cot_ref[block, :, cols].astype(jnp.float32) / total * power
                scaled_ref[:, cols] = (DISCOUNT * grad).astype(jnp.bfloat16)
            rows = pl.ds(pl.multiple_of(k * tile_rows, tile_rows), tile_rows)
            out_ref[rows, :] = transposed_dot(tiles_ref[block, action, n], scaled_ref[...]).astype(jnp.bfloat16)

        return carry

    lax.fori_loop(0, capacity, one_term, 0)


def lead_terms(last, incoming, source, scores, tiles, cot_blocks, rows):
    tile_rows, width = tiles.shape[3], cot_blocks.shape[2]
    count = len(last)
    return pl.pallas_call(
        functools.partial(lead_terms_kernel, count),
        out_shape=(
            jax.ShapeDtypeStruct(scores.shape, scores.dtype),
            jax.ShapeDtypeStruct((rows, width), jnp.bfloat16),
        ),
        in_specs=[SMEM_SPEC] * count + [VMEM_SPEC] * count + [SMEM_SPEC] + [VMEM_SPEC] * 3,
        out_specs=(VMEM_SPEC, VMEM_SPEC),
        scratch_shapes=[pltpu.VMEM((tile_rows, width), jnp.bfloat16)],
        input_output_aliases={2 * count + 3: 0},
        compiler_params=PARAMS,
        cost_estimate=SMALL_COST,
        name="lead_terms",
    )(*last, *incoming, source, tiles, cot_blocks, scores)


def split_rows(x):
    high = x.astype(jnp.bfloat16)
    rest = x - high.astype(jnp.float32)
    middle = rest.astype(jnp.bfloat16)
    return high, middle, (rest - middle.astype(jnp.float32)).astype(jnp.bfloat16)


def join_rows(parts):
    high, middle, low = (x.astype(jnp.float32) for x in parts)
    return (high + middle) + low


def score_kernel(row_count, scales, *refs):
    source_refs = refs[:row_count]
    scores_ref, tiles_ref, cot_ref, _, value_ref, scaled_ref, util_ref, taste_ref = refs[row_count : row_count + 8]
    out_refs = refs[row_count + 8 :]
    util_scale, taste_scale = scales
    block = pl.program_id(0)
    _, action_count, tile_rows, width = scores_ref.shape
    states = pl.ds(pl.multiple_of(block * tile_rows, tile_rows), tile_rows)

    @pl.when(block == 0)
    def _():
        taste_ref[...] = jnp.zeros_like(taste_ref)

    sums = [jnp.zeros((tile_rows, tile_rows), jnp.float32) for _ in range(action_count)]
    for c in range(0, width, tile_rows):
        cols = slice(c, c + tile_rows)
        largest, powers, total = soft_max([scores_ref[block, action, :, cols] for action in range(action_count)])
        value_ref[:, cols] = largest + jnp.log(total)
        ratio = cot_ref[block, :, cols].astype(jnp.float32) / total
        for action in range(action_count):
            grad = ratio * powers[action]
            scaled_ref[block, action, :, cols] = (DISCOUNT * grad).astype(jnp.bfloat16)
            sums[action] = sums[action] + grad
            taste_ref[action : action + 1, cols] += taste_scale * jnp.sum(grad, axis=0, keepdims=True)
    for action in range(action_count):
        util_ref[action : action + 1, states] = util_scale * jnp.sum(sums[action].T, axis=0, keepdims=True)

    @pl.when(block == pl.num_programs(0) - 1)
    def _():
        for source_ref, out_ref in zip(source_refs, out_refs):
            capacity = source_ref.shape[1]

            def one_term(k, carry):
                code = source_ref[0, k]

                @pl.when(code >= 0)
                def _():
                    block, action, n = unpack(code)
                    rows = pl.ds(pl.multiple_of(k * tile_rows, tile_rows), tile_rows)
                    out_ref[rows, :] = transposed_dot(tiles_ref[block, action, n], scaled_ref[block, action]).astype(
                        jnp.bfloat16
                    )

                return carry

            lax.fori_loop(0, capacity, one_term, 0)
            rows = list(split_rows(taste_ref[...]))
            spare = out_ref.shape[0] - capacity * tile_rows - sum(x.shape[0] for x in rows)
            rows.append(jnp.zeros((spare, width), jnp.bfloat16))
            out_ref[capacity * tile_rows :, :] = jnp.concatenate(rows, axis=0)


def score(sources, scores, tiles, cot_blocks, sent, scales, rows):
    block_count, action_count, tile_rows, width = scores.shape
    states = block_count * tile_rows
    return pl.pallas_call(
        functools.partial(score_kernel, len(sources), scales),
        out_shape=[
            jax.ShapeDtypeStruct((states, width), jnp.float32),
            jax.ShapeDtypeStruct(scores.shape, jnp.bfloat16),
            jax.ShapeDtypeStruct((action_count, states), jnp.float32),
            jax.ShapeDtypeStruct((action_count, width), jnp.float32),
        ]
        + [jax.ShapeDtypeStruct((rows, width), jnp.bfloat16)] * len(sources),
        grid=(block_count,),
        in_specs=[SMEM_SPEC] * len(sources) + [VMEM_SPEC] * 3 + [ANY_SPEC],
        out_specs=[pl.BlockSpec((tile_rows, width), lambda i: (i, 0))] + [VMEM_SPEC] * (3 + len(sources)),
        compiler_params=PARAMS,
        cost_estimate=SMALL_COST,
        name="score",
    )(*sources, scores, tiles, cot_blocks, sent)


def local_adjoint_kernel(me_ref, dest_ref, counts_ref, tiles_ref, scaled_ref, sent_ref, held_ref, written_ref, sem):
    del sent_ref
    block_count, action_count, entry_count, _, _ = tiles_ref.shape
    base = me_ref[0] * block_count

    def clear(block, carry):
        held_ref[block] = jnp.zeros_like(held_ref[block])
        return carry

    lax.fori_loop(0, block_count, clear, 0)

    def one_block(block, carry):
        for action in range(action_count):
            for n in range(entry_count):
                rel = dest_ref[n, action, block] - base
                here = (n < counts_ref[action, block]) & (rel >= 0) & (rel < block_count)
                tile = tiles_ref[block, action, n]
                tile = jnp.where(here, tile, jnp.zeros_like(tile))
                held_ref[jnp.where(here, rel, 0)] += transposed_dot(tile, scaled_ref[block, action])
        return carry

    lax.fori_loop(0, block_count, one_block, 0)
    copy = pltpu.make_async_copy(held_ref, written_ref, sem)
    copy.start()
    copy.wait()


def local_adjoint(me, dest, counts, tiles, scaled, sent):
    block_count, _, _, tile_rows, _ = tiles.shape
    shape = jax.ShapeDtypeStruct((block_count, tile_rows, scaled.shape[3]), jnp.float32)
    return pl.pallas_call(
        local_adjoint_kernel,
        out_shape=(shape, shape),
        in_specs=[SMEM_SPEC] * 3 + [VMEM_SPEC] * 2 + [ANY_SPEC],
        out_specs=(VMEM_SPEC, HBM_SPEC),
        scratch_shapes=[pltpu.SemaphoreType.DMA],
        compiler_params=PARAMS,
        cost_estimate=SMALL_COST,
        name="local_adjoint",
    )(me, dest, counts, tiles, scaled, sent)


def add_arrivals_kernel(count, taste_offsets, *refs):
    wanted_refs, arrived_refs = refs[:count], refs[count : 2 * count]
    rest = refs[2 * count + 2 :]
    if taste_offsets:
        me_ref, lead_ref, own_ref, held_ref, written_ref, taste_ref, sems, part_ref = rest
    else:
        held_ref, written_ref, sems = rest
    slots = wanted_refs[0].shape[1]
    tile_rows = held_ref.shape[1]
    target = [ref[0, k] for ref in wanted_refs for k in range(slots)]
    total = len(target)
    place = [jnp.maximum(t, 0) for t in target]
    store = [pltpu.make_async_copy(held_ref.at[place[k]], written_ref.at[place[k]], sems.at[k]) for k in range(total)]
    last = []
    for k in range(total):
        final = target[k] >= 0
        for other in range(k + 1, total):
            final = final & (target[other] != target[k])
        last.append(final)
    for k in range(total):

        @pl.when(target[k] >= 0)
        def _():
            first = k % slots * tile_rows
            held_ref[place[k]] += arrived_refs[k // slots][first : first + tile_rows, :].astype(jnp.float32)

        @pl.when(last[k])
        def _():
            store[k].start()

    if taste_offsets:
        devices, action_count = part_ref.shape[:2]
        me = me_ref[0]

        def sender(offset):
            return lax.rem(me - offset + devices, devices)

        part_ref[me] = own_ref[...]
        part_ref[sender(taste_offsets[0])] = lead_ref[...]
        for offset, arrived_ref in zip(taste_offsets[1:], arrived_refs):
            first = [slots * tile_rows + p * action_count for p in range(3)]
            part_ref[sender(offset)] = join_rows([arrived_ref[f : f + action_count, :] for f in first])
        taste = part_ref[0]
        for device in range(1, devices):
            taste = taste + part_ref[device]
        taste_ref[...] = taste

    for k in range(total):

        @pl.when(last[k])
        def _():
            store[k].wait()


def add_arrivals(wanted, arrived, held, written, taste=()):
    count = len(wanted)
    shape = jax.ShapeDtypeStruct(held.shape, held.dtype)
    out_shape, out_specs = [shape, shape], [VMEM_SPEC, HBM_SPEC]
    in_specs = [SMEM_SPEC] * count + [VMEM_SPEC] * (count + 1) + [HBM_SPEC]
    scratch = [pltpu.SemaphoreType.DMA((count * wanted[0].shape[1],))]
    offsets, extra = (), ()
    if taste:
        offsets, extra = tuple(taste[0]), taste[1:]
        own = extra[-1]
        out_shape.append(jax.ShapeDtypeStruct(own.shape, own.dtype))
        out_specs.append(VMEM_SPEC)
        in_specs += [SMEM_SPEC] + [VMEM_SPEC] * 2
        scratch.append(pltpu.VMEM((len(offsets) + 1,) + own.shape, own.dtype))
    return pl.pallas_call(
        functools.partial(add_arrivals_kernel, count, offsets),
        out_shape=out_shape,
        in_specs=in_specs,
        out_specs=out_specs,
        scratch_shapes=scratch,
        input_output_aliases={2 * count: 0, 2 * count + 1: 1},
        compiler_params=PARAMS,
        cost_estimate=SMALL_COST,
        name="add_arrivals",
    )(*wanted, *arrived, held, written, *extra)


def local(value_in, cotangent, state_util, taste, tiles, dest_block, counts):
    block_count, action_count, _, tile_rows, _ = tiles.shape
    states, width = value_in.shape
    device_count = lax.axis_size("state")
    me = lax.axis_index("state").astype(jnp.int32).reshape(1)
    capacity = max(2, (block_count + device_count - 2) // (device_count - 1))
    value_blocks = value_in.reshape(block_count, tile_rows, width)
    cot_blocks = cotangent.reshape(block_count, tile_rows, width)
    offsets = range(1, device_count)
    order = sorted(offsets, key=lambda d: -min(d, device_count - d))

    def shift(x, offset):
        return lax.ppermute(x, "state", [(s, (s + offset) % device_count) for s in range(device_count)])

    def add_over(x, axis):
        size = lax.axis_size(axis)
        if size & (size - 1):
            return lax.psum(x, axis)
        step = 1
        while step < size:
            x = x + lax.ppermute(x, axis, [(s, s ^ step) for s in range(size)])
            step *= 2
        return x

    dest, counts = dest_block.transpose(2, 1, 0), counts.T
    request, source = make_plan(me, dest, counts, device_count, capacity)
    wanted = {d: shift(request[d - 1], d) for d in order}
    staged = stage(value_blocks, request[0])
    outgoing = {d: gather_blocks(wanted[d], staged) for d in order}
    incoming = {d: shift(outgoing[d], -d) for d in order}
    scores = local_forward(me, dest, counts, staged, tiles, state_util, taste, outgoing[order[-1]])
    early, late = order[:1], order[1:]
    for d in early:
        scores = add_incoming(source[d - 1], incoming[d], tiles, scores)

    rows = capacity * tile_rows + 16 * pl.cdiv(3 * action_count, 16)
    scores, lead = lead_terms(
        [source[d - 1] for d in late], [incoming[d] for d in late], source[order[0] - 1], scores, tiles, cot_blocks, rows
    )
    scales = (1.0 / (width * lax.axis_size("type")), 1.0 / (states * device_count))
    value_out, scaled, util_part, taste_part, *rest = score(
        [source[d - 1] for d in late], scores, tiles, cot_blocks, lead, scales, rows
    )
    terms = [lead, *rest]
    returned = [shift(x, d) for d, x in zip(order, terms)]
    lead_taste = shift(taste_part, order[0])
    held, written = local_adjoint(me, dest, counts, tiles, scaled, terms[-1])
    util_total = add_over(util_part, "type")
    held, written = add_arrivals([wanted[order[0]]], returned[:1], held, written)
    held, written, taste_total = add_arrivals(
        [wanted[d] for d in late], returned[1:], held, written, (order, me, lead_taste, taste_part)
    )
    return value_out, written.reshape(states, width), util_total, taste_total


def solution(mesh):
    return jax.shard_map(
        local,
        mesh=mesh,
        in_specs=(
            P(("groups", "state"), "type"),
            P(("groups", "state"), "type"),
            P(None, ("groups", "state")),
            P(None, ("groups", "type")),
            P(("groups", "state"), None, None, None, None),
            P(("groups", "state"), None, None),
            P(("groups", "state"), None),
        ),
        out_specs=(
            P(("groups", "state"), "type"),
            P(("groups", "state"), "type"),
            P(None, ("groups", "state")),
            P(None, ("groups", "type")),
        ),
        check_vma=False,
    )
```

time: 340 us -> 160 us (0.47)
  local copies, waits for them, and re-layouts: 125 us -> 3.65 us
  matrix products: 67.8 us -> 0 us
  Pallas kernels: 0 us -> 42.3 us
  other arithmetic: 38.5 us -> 0.63 us
  blocking collectives: 33.9 us -> 0 us
  starting transfers between devices: 8.47 us -> 31.6 us
  waiting for transfers between devices: 63.7 us -> 80.7 us
    ppermute x0 -> x12, waiting for transfers between devices: none -> 80.7 us  [the longest x10 79.5 us: shift(): lax.ppermute(x, 'state', [(s, (s + offset) % device_count) for s in range...]
    dot_general x4 -> x0, matrix products: 67.8 us -> none  [the longest x1 24.5 us: local(): jnp.einsum('bamij,baik->bamjk', tiles, scaled, preferred_element_type=jnp...]
    all_to_all x2 -> x0, waiting for transfers between devices: 63.7 us -> none  [the longest x1 63.7 us: local(): lax.all_to_all(outgoing.reshape(device_count, capacity, tile_rows, type_w...]
    gather x5 -> x0, local copies, waits for them, and re-layouts: 55.6 us -> none  [the longest x2 46.1 us: local(): picked = jnp.take(table, lookup, axis=0)]
    reshape x4 -> x0, local copies, waits for them, and re-layouts: 49.5 us -> none  [the longest x1 49.2 us: local(): contrib = jnp.einsum('bamij,baik->bamjk', tiles, scaled, preferred_elemen...]
    pallas_call x0 -> x12, Pallas kernels: none -> 42.3 us  [the longest x1 12.8 us: local_adjoint(): pl.pallas_call(local_adjoint_kernel, out_shape=(shape, shape), in_specs=[...]
    ppermute x0 -> x12, starting transfers between devices: none -> 31.6 us  [the longest x10 30 us: shift(): lax.ppermute(x, 'state', [(s, (s + offset) % device_count) for s in range...]
    psum x2 -> x0, blocking collectives: 22.3 us -> none  [the longest x1 12.2 us: local(): lax.psum(jnp.sum(grad_q, axis=(0, 2)), 'state')]
  transfers between devices with their start and end apart: 2 -> 12, of which waited for: 1 -> 5; matrix products, arithmetic and copies ran while one was open for 27% -> 0% of each run, Pallas kernels for 0% -> 22%
where the time goes in v3:
time: 160 us
  waiting for transfers between devices  80.7 us (50%)
  Pallas kernels  42.3 us (26%)
  starting transfers between devices  31.6 us (20%)
  local copies, waits for them, and re-layouts  3.65 us (2%)
    ppermute x10, waiting for transfers between devices, shift(): lax.ppermute(x, 'state', [(s, (s + offset) % device_count) for s in range...  79.5 us
    ppermute x10, starting transfers between devices, shift(): lax.ppermute(x, 'state', [(s, (s + offset) % device_count) for s in range...  30 us
    pallas_call x1, Pallas kernels, local_adjoint(): pl.pallas_call(local_adjoint_kernel, out_shape=(shape, shape), in_specs=[...  12.8 us
    pallas_call x1, Pallas kernels, score(): pl.pallas_call(functools.partial(score_kernel, len(sources), scales), out...  11.5 us
    pallas_call x1, Pallas kernels, local_forward(): pl.pallas_call(local_forward_kernel, out_shape=jax.ShapeDtypeStruct((bloc...  7.01 us
    pallas_call x2, Pallas kernels, add_arrivals(): pl.pallas_call(functools.partial(add_arrivals_kernel, count, offsets), ou...  4.36 us
    unnamed x20, local copies, waits for them, and re-layouts  3.65 us
  transfers between devices with their start and end apart: 12, of which 5 were waited for; matrix products, arithmetic and copies ran while one was open for 0% of the time, Pallas kernels for 22%

profile of v3, /device:TPU:0, one launch (start us, length us, event | category | flops | bytes accessed | tf_op | source)
XLA Modules:
  0.0 159.7 jit_solution(7889503788250999081)
XLA Ops:
  0.6 0.0 copy-start.2
  0.6 0.7 copy-done.2
  1.3 0.7 copy-done.5
  2.0 1.0 plan.1
  3.0 5.1 %collective-permute-start.2 = (s32[1,6]{1,0:T(1,128)S(1)}, s32[1,6]{1,0:T(1,128)S(1)}, u32[]{:S(2)}, u32[]{:S(2)}) collective-permute-start(s32[1,6]{1,0:T(1,128)S(1)} %get-tuple-element.27), channel_id=1, source_target_pairs={{0,12},{4,0},{8,4},{12,8},{1,13},{5,1},{9,5},{13,9},{2,14},{6,2},{... | collective-permute-start | bytes 80 | tf_op jit(solution)/shard_map/ppermute | solution.py:498
  8.1 0.0 collective-permute-start.4
  8.1 1.0 collective-permute-start
  9.1 1.6 copy-done.1
  10.7 0.1 stage.1.value_ref
  10.8 0.0 slice-start.1
  10.8 0.0 copy-start.3
  10.8 0.0 copy-start.4
  10.9 0.0 copy-start.6
  10.9 0.0 copy-start.7
  10.9 1.6 %collective-permute-done.4.wanted_ref.refs_0_ = s32[1,6]{1,0:T(1,128)S(1)} collective-permute-done((s32[1,6]{1,0:T(1,128)S(1)}, s32[1,6]{1,0:T(1,128)S(1)}, u32[]{:S(2)}, u32[]{:S(2)}) %collective-permute-start.4) | collective-permute-done | bytes 56 | tf_op jit(solution)/shard_map/ppermute | solution.py:498
  12.5 0.6 gather.5
  13.1 0.4 collective-permute-start.5
  13.5 0.0 collective-permute-done.2.wanted_ref.refs_1_
  13.5 0.6 gather.4.sent_ref
  14.1 1.5 collective-permute-start.3
  15.6 0.0 collective-permute-done.wanted_ref.refs_0_
  15.6 0.6 gather.3
  16.2 2.4 %collective-permute-start.1 = (bf16[6,128,512]{2,1,0:T(8,128)(2,1)S(1)}, bf16[6,128,512]{2,1,0:T(8,128)(2,1)S(1)}, u32[]{:S(2)}, u32[]{:S(2)}) collective-permute-start(bf16[6,128,512]{2,1,0:T(8,128)(2,1)S(1)} %gather.3), channel_id=1, source_target_pairs={{0,12},{4,0},{8,4},{12,8},{1,13},{5,1},{9,5},{13,9},{2,14},{6,2},{... | collective-permute-start | bytes 2359304 | tf_op jit(solution)/shard_map/ppermute | solution.py:498
  18.6 0.0 copy-done.4
  18.7 7.0 %local_forward.1.scores_in_ref = f32[16,2,128,512]{3,2,1,0:T(8,128)S(1)} custom-call(s32[1]{0:T(128)} %bitcast.me_ref.refs_6_, s32[6,2,16]{2,1,0:T(2,128)S(1)} %bitcast.12, s32[2,16]{1,0:T(2,128)S(1)} %bitcast.15, bf16[16,128,512]{2,1,0:T(8,128)(2,1)S(1)} %stage.1.value_ref, bf16[16,2,6,128,128]{4,3,2,1,0:T(8,128)(2,1)S(1)} %bitcast.7, ...), custom_call_target="tpu_custom_call" | custom-call | flops 1000 | bytes 1000 | tf_op jit(solution)/shard_map/local_forward/pallas_call | solution.py:172
  25.7 41.0 %collective-permute-done.5.incoming_ref = bf16[6,128,512]{2,1,0:T(8,128)(2,1)S(1)} collective-permute-done((bf16[6,128,512]{2,1,0:T(8,128)(2,1)S(1)}, bf16[6,128,512]{2,1,0:T(8,128)(2,1)S(1)}, u32[]{:S(2)}, u32[]{:S(2)}) %collective-permute-start.5) | collective-permute-done | bytes 786464 | tf_op jit(solution)/shard_map/ppermute | solution.py:498
  66.7 0.9 add_incoming.1.refs_7_
  67.6 0.0 collective-permute-done.3.refs_3_
  67.7 0.0 collective-permute-done.1.refs_2_
  67.7 0.7 copy-done
  68.3 2.9 %lead_terms.1 = (f32[16,2,128,512]{3,2,1,0:T(8,128)S(1)}, bf16[784,512]{1,0:T(8,128)(2,1)S(1)}) custom-call(s32[1,6]{1,0:T(1,128)S(1)} %get-tuple-element.24.refs_0_, s32[1,6]{1,0:T(1,128)S(1)} %get-tuple-element.25.refs_1_, bf16[6,128,512]{2,1,0:T(8,128)(2,1)S(1)} %collective-permute-done.1.refs_2_, ...), custom_call_target="tpu_custom_call", output_to_operand_aliasing={{0}: (7, {})} | custom-call | flops 1000 | bytes 1000 | tf_op jit(solution)/shard_map/lead_terms/pallas_call | solution.py:262
  71.2 15.8 %collective-permute-start.8 = (bf16[784,512]{1,0:T(8,128)(2,1)S(1)}, bf16[784,512]{1,0:T(8,128)(2,1)S(1)}, u32[]{:S(2)}, u32[]{:S(2)}) collective-permute-start(bf16[784,512]{1,0:T(8,128)(2,1)S(1)} %get-tuple-element.31.refs_5_), channel_id=1, source_target_pairs={{0,8},{4,12},{8,0},{12,4},{1,9},{5,13},{9,1},{13,5},{2,10},{6,14},... | collective-permute-start | bytes 2408456 | tf_op jit(solution)/shard_map/ppermute | solution.py:498
  87.0 11.5 %score.1 = (f32[2048,512]{1,0:T(8,128)}, bf16[16,2,128,512]{3,2,1,0:T(8,128)(2,1)S(1)}, f32[2,2048]{1,0:T(2,128)S(1)}, f32[2,512]{1,0:T(2,128)S(1)}, bf16[784,51...) custom-call(s32[1,6]{1,0:T(1,128)S(1)} %get-tuple-element.24.refs_0_, s32[1,6]{1,0:T(1,128)S(1)} %get-tuple-element.25.refs_1_, ...), custom_call_target="tpu_custom_call" | custom-call | flops 1000 | bytes 1000 | tf_op jit(solution)/shard_map/score/pallas_call | solution.py:345
  98.5 0.0 collective-permute-start.6
  98.5 3.8 %collective-permute-start.7 = (bf16[784,512]{1,0:T(8,128)(2,1)S(1)}, bf16[784,512]{1,0:T(8,128)(2,1)S(1)}, u32[]{:S(2)}, u32[]{:S(2)}) collective-permute-start(bf16[784,512]{1,0:T(8,128)(2,1)S(1)} %get-tuple-element.34.sent_ref), channel_id=1, source_target_pairs={{0,12},{4,0},{8,4},{12,8},{1,13},{5,1},{9,5},{13,9},{2,14},{6,2},{... | collective-permute-start | bytes 2408456 | tf_op jit(solution)/shard_map/ppermute | solution.py:498
  102.3 0.0 collective-permute-start.10
  102.3 1.2 collective-permute-done.10
  103.5 1.6 collective-permute-start.11
  105.1 0.0 collective-permute-start.9
  105.1 12.8 %local_adjoint.1 = (f32[16,128,512]{2,1,0:T(8,128)S(1)}, f32[16,128,512]{2,1,0:T(8,128)}) custom-call(s32[1]{0:T(128)} %bitcast.me_ref.refs_6_, s32[6,2,16]{2,1,0:T(2,128)S(1)} %bitcast.13, s32[2,16]{1,0:T(2,128)S(1)} %bitcast.16, bf16[16,2,6,128,128]{4,3,2,1,0:T(8,128)(2,1)S(1)} %bitcast.7, bf16[16,2,128,512]{3,2,1,0:T(8,128)(2,1)S(1)} %get-tuple-element.35.scaled_ref, ...), custom_call_target="tpu_custom_call" | custom-call | flops 1000 | bytes 1000 | tf_op jit(solution)/shard_map/local_adjoint/pallas_call | solution.py:393
  117.8 0.0 collective-permute-done.11
  117.8 0.6 add.7
  118.5 21.7 %collective-permute-done.8.refs_1_ = bf16[784,512]{1,0:T(8,128)(2,1)S(1)} collective-permute-done((bf16[784,512]{1,0:T(8,128)(2,1)S(1)}, bf16[784,512]{1,0:T(8,128)(2,1)S(1)}, u32[]{:S(2)}, u32[]{:S(2)}) %collective-permute-start.8) | collective-permute-done | bytes 802848 | tf_op jit(solution)/shard_map/ppermute | solution.py:498
  140.2 1.6 %add_arrivals.2 = (f32[16,128,512]{2,1,0:T(8,128)S(1)}, f32[16,128,512]{2,1,0:T(8,128)}) custom-call(s32[1,6]{1,0:T(1,128)S(1)} %collective-permute-done.4.wanted_ref.refs_0_, bf16[784,512]{1,0:T(8,128)(2,1)S(1)} %collective-permute-done.8.refs_1_, f32[16,128,512]{2,1,0:T(8,128)S(1)} %get-tuple-element.36.refs_2_, ...), custom_call_target="tpu_custom_call", output_to_operand_aliasing={{0}: (2, {}), {1}: (3, {})} | custom-call | flops 1000 | bytes 1000 | tf_op jit(solution)/shard_map/add_arrivals/pallas_call | solution.py:473
  141.8 15.1 %collective-permute-done.9.refs_7_ = f32[2,512]{1,0:T(2,128)S(1)} collective-permute-done((f32[2,512]{1,0:T(2,128)S(1)}, f32[2,512]{1,0:T(2,128)S(1)}, u32[]{:S(2)}, u32[]{:S(2)}) %collective-permute-start.9) | collective-permute-done | bytes 4128 | tf_op jit(solution)/shard_map/ppermute | solution.py:498
  156.9 0.0 collective-permute-done.6.refs_2_
  156.9 0.0 collective-permute-done.7.refs_3_
  156.9 2.7 %add_arrivals.3 = (f32[16,128,512]{2,1,0:T(8,128)S(1)}, f32[16,128,512]{2,1,0:T(8,128)}, f32[2,512]{1,0:T(2,128)}) custom-call(s32[1,6]{1,0:T(1,128)S(1)} %collective-permute-done.wanted_ref.refs_0_, s32[1,6]{1,0:T(1,128)S(1)} %collective-permute-done.2.wanted_ref.refs_1_, ...), custom_call_target="tpu_custom_call", output_to_operand_aliasing={{0}: (4, {}), {1}: (5, {})} | custom-call | flops 1000 | bytes 1000 | tf_op jit(solution)/shard_map/add_arrivals/pallas_call | solution.py:473
  (11 shorter events, 0.0 us)
Async XLA Ops:
  0.6 0.7 copy-start.2
  1.3 0.7 copy-start.5
  3.0 10.5 %collective-permute-start.2 = (s32[1,6]{1,0:T(1,128)S(1)}, s32[1,6]{1,0:T(1,128)S(1)}, u32[]{:S(2)}, u32[]{:S(2)}) collective-permute-start(s32[1,6]{1,0:T(1,128)S(1)} %get-tuple-element.27), channel_id=1, source_target_pairs={{0,12},{4,0},{8,4},{12,8},{1,13},{5,1},{9,5},{13,9},{2,14},{6,2},{... | collective-permute-start | bytes 80 | tf_op jit(solution)/shard_map/ppermute | solution.py:498
  8.1 4.4 %collective-permute-start.4 = (s32[1,6]{1,0:T(1,128)S(1)}, s32[1,6]{1,0:T(1,128)S(1)}, u32[]{:S(2)}, u32[]{:S(2)}) collective-permute-start(s32[1,6]{1,0:T(1,128)S(1)} %get-tuple-element.29), channel_id=1, source_target_pairs={{0,8},{4,12},{8,0},{12,4},{1,9},{5,13},{9,1},{13,5},{2,10},{6,14},... | collective-permute-start | bytes 80 | tf_op jit(solution)/shard_map/ppermute | solution.py:498
  8.1 7.5 %collective-permute-start = (s32[1,6]{1,0:T(1,128)S(1)}, s32[1,6]{1,0:T(1,128)S(1)}, u32[]{:S(2)}, u32[]{:S(2)}) collective-permute-start(s32[1,6]{1,0:T(1,128)S(1)} %get-tuple-element.26.plan_ref), channel_id=1, source_target_pairs={{0,4},{4,8},{8,12},{12,0},{1,5},{5,9},{9,13},{13,1},{2,6},{6,10},{... | collective-permute-start | bytes 80 | tf_op jit(solution)/shard_map/ppermute | solution.py:498
  9.1 1.6 copy-start.1
  10.7 7.9 %slice-start = ((s8[6291456]{0:T(1024)(128)(4,1)}), s8[4194304]{0:T(1024)(128)(4,1)S(1)}, s32[]{:S(2)}) async-start(s8[6291456]{0:T(1024)(128)(4,1)} %bitcast.6), calls=%async_computation | async-start | bytes 8388608
  10.8 7.8 %slice-start.1 = ((s8[6291456]{0:T(1024)(128)(4,1)}), s8[2097152]{0:T(1024)(128)(4,1)S(1)}, s32[]{:S(2)}) async-start(s8[6291456]{0:T(1024)(128)(4,1)} %bitcast.6), calls=%async_computation.1 | async-start | bytes 4194304
  10.8 7.8 %copy-start.3 = (s32[16,2,6]{0,1,2:T(2,128)S(1)}, s32[16,2,6]{0,1,2:T(2,128)}, u32[]{:S(2)}) copy-start(s32[16,2,6]{0,1,2:T(2,128)} %param.12) | copy-start | bytes 2308
  10.8 7.8 %copy-start.4 = (f32[2,2048]{1,0:T(2,128)S(1)}, f32[2,2048]{1,0:T(2,128)}, u32[]{:S(2)}) copy-start(f32[2,2048]{1,0:T(2,128)} %util_ref.1) | copy-start | bytes 49156
  10.9 7.8 %copy-start.6 = (s32[16,2]{0,1:T(2,128)S(1)}, s32[16,2]{0,1:T(2,128)}, u32[]{:S(2)}) copy-start(s32[16,2]{0,1:T(2,128)} %param.13) | copy-start | bytes 388
  10.9 7.8 %copy-start.7 = (f32[2,512]{1,0:T(2,128)S(1)}, f32[2,512]{1,0:T(2,128)}, u32[]{:S(2)}) copy-start(f32[2,512]{1,0:T(2,128)} %taste_ref.1) | copy-start | bytes 12292
  13.1 53.6 %collective-permute-start.5 = (bf16[6,128,512]{2,1,0:T(8,128)(2,1)S(1)}, bf16[6,128,512]{2,1,0:T(8,128)(2,1)S(1)}, u32[]{:S(2)}, u32[]{:S(2)}) collective-permute-start(bf16[6,128,512]{2,1,0:T(8,128)(2,1)S(1)} %gather.5), channel_id=1, source_target_pairs={{0,8},{4,12},{8,0},{12,4},{1,9},{5,13},{9,1},{13,5},{2,10},{6,14},... | collective-permute-start | bytes 2359304 | tf_op jit(solution)/shard_map/ppermute | solution.py:498
  14.1 53.6 %collective-permute-start.3 = (bf16[6,128,512]{2,1,0:T(8,128)(2,1)S(1)}, bf16[6,128,512]{2,1,0:T(8,128)(2,1)S(1)}, u32[]{:S(2)}, u32[]{:S(2)}) collective-permute-start(bf16[6,128,512]{2,1,0:T(8,128)(2,1)S(1)} %gather.4.sent_ref), channel_id=1, source_target_pairs={{0,4},{4,8},{8,12},{12,0},{1,5},{5,9},{9,13},{13,1},{2,6},{6,10},{... | collective-permute-start | bytes 2359304 | tf_op jit(solution)/shard_map/ppermute | solution.py:498
  16.2 51.4 %collective-permute-start.1 = (bf16[6,128,512]{2,1,0:T(8,128)(2,1)S(1)}, bf16[6,128,512]{2,1,0:T(8,128)(2,1)S(1)}, u32[]{:S(2)}, u32[]{:S(2)}) collective-permute-start(bf16[6,128,512]{2,1,0:T(8,128)(2,1)S(1)} %gather.3), channel_id=1, source_target_pairs={{0,12},{4,0},{8,4},{12,8},{1,13},{5,1},{9,5},{13,9},{2,14},{6,2},{... | collective-permute-start | bytes 2359304 | tf_op jit(solution)/shard_map/ppermute | solution.py:498
  66.7 1.6 copy-start
  71.2 68.9 %collective-permute-start.8 = (bf16[784,512]{1,0:T(8,128)(2,1)S(1)}, bf16[784,512]{1,0:T(8,128)(2,1)S(1)}, u32[]{:S(2)}, u32[]{:S(2)}) collective-permute-start(bf16[784,512]{1,0:T(8,128)(2,1)S(1)} %get-tuple-element.31.refs_5_), channel_id=1, source_target_pairs={{0,8},{4,12},{8,0},{12,4},{1,9},{5,13},{9,1},{13,5},{2,10},{6,14},... | collective-permute-start | bytes 2408456 | tf_op jit(solution)/shard_map/ppermute | solution.py:498
  98.5 58.4 %collective-permute-start.6 = (bf16[784,512]{1,0:T(8,128)(2,1)S(1)}, bf16[784,512]{1,0:T(8,128)(2,1)S(1)}, u32[]{:S(2)}, u32[]{:S(2)}) collective-permute-start(bf16[784,512]{1,0:T(8,128)(2,1)S(1)} %get-tuple-element.33), channel_id=1, source_target_pairs={{0,4},{4,8},{8,12},{12,0},{1,5},{5,9},{9,13},{13,1},{2,6},{6,10},{... | collective-permute-start | bytes 2408456 | tf_op jit(solution)/shard_map/ppermute | solution.py:498
  98.5 58.4 %collective-permute-start.7 = (bf16[784,512]{1,0:T(8,128)(2,1)S(1)}, bf16[784,512]{1,0:T(8,128)(2,1)S(1)}, u32[]{:S(2)}, u32[]{:S(2)}) collective-permute-start(bf16[784,512]{1,0:T(8,128)(2,1)S(1)} %get-tuple-element.34.sent_ref), channel_id=1, source_target_pairs={{0,12},{4,0},{8,4},{12,8},{1,13},{5,1},{9,5},{13,9},{2,14},{6,2},{... | collective-permute-start | bytes 2408456 | tf_op jit(solution)/shard_map/ppermute | solution.py:498
  102.3 1.2 collective-permute-start.10
  103.5 14.3 %collective-permute-start.11 = (f32[2,2048]{1,0:T(2,128)S(1)}, f32[2,2048]{1,0:T(2,128)S(1)}, u32[]{:S(2)}, u32[]{:S(2)}) collective-permute-start(f32[2,2048]{1,0:T(2,128)S(1)} %add.6), channel_id=1, source_target_pairs={{0,2},{1,3},{2,0},{3,1},{4,6},{5,7},{6,4},{7,5},{8,10},{9,11},{10,... | collective-permute-start | bytes 49160 | tf_op jit(solution)/shard_map/ppermute | solution.py:506
  105.1 51.9 %collective-permute-start.9 = (f32[2,512]{1,0:T(2,128)S(1)}, f32[2,512]{1,0:T(2,128)S(1)}, u32[]{:S(2)}, u32[]{:S(2)}) collective-permute-start(f32[2,512]{1,0:T(2,128)S(1)} %get-tuple-element.40.refs_8_), channel_id=1, source_target_pairs={{0,8},{4,12},{8,0},{12,4},{1,9},{5,13},{9,1},{13,5},{2,10},{6,14},... | collective-permute-start | bytes 12296 | tf_op jit(solution)/shard_map/ppermute | solution.py:498

commit v4 on v3

--- a/solution.py
+++ b/solution.py
@@ -15,6 +15,7 @@
 HBM_SPEC = pl.BlockSpec(memory_space=pltpu.HBM)
 VMEM_SPEC = pl.BlockSpec(memory_space=pltpu.VMEM)
 PARAMS = pltpu.CompilerParams(vmem_limit_bytes=VMEM_LIMIT)
+PLAN_COST = pl.CostEstimate(flops=2 * 10**10, bytes_accessed=1000, transcendentals=0)
 SMALL_COST = pl.CostEstimate(flops=1000, bytes_accessed=1000, transcendentals=0)
 
 
@@ -29,24 +30,16 @@
     return lax.broadcasted_iota(jnp.int32, shape, dim)
 
 
-def plan_kernel(device_count, me_ref, dest_hbm_ref, counts_hbm_ref, *refs):
+def plan_kernel(device_count, me_ref, dest_ref, *refs):
     request_refs = refs[: device_count - 1]
     source_refs = refs[device_count - 1 : 2 * (device_count - 1)]
-    dest_ref, counts_ref, mark_ref, local_ref, sems = refs[2 * (device_count - 1) :]
-    copies = [
-        pltpu.make_async_copy(dest_hbm_ref, dest_ref, sems.at[0]),
-        pltpu.make_async_copy(counts_hbm_ref, counts_ref, sems.at[1]),
-    ]
-    for copy in copies:
-        copy.start()
+    mark_ref, local_ref = refs[2 * (device_count - 1) :]
     entry_count, action_count, block_count = dest_ref.shape
     capacity = request_refs[0].shape[1]
     places = 8 * pl.cdiv(capacity, 8)
     me = me_ref[0]
     mark_ref[...] = jnp.zeros_like(mark_ref)
     local_ref[...] = jnp.zeros_like(local_ref)
-    for copy in copies:
-        copy.wait()
     for n in range(entry_count):
         dest = dest_ref[n]
         owner = jnp.zeros_like(dest)
@@ -54,8 +47,7 @@
             owner += (dest >= other * block_count).astype(jnp.int32)
         offset = owner - me
         offset = jnp.where(offset < 0, offset + device_count, offset)
-        mark = jnp.where(n < counts_ref[...], offset, 0)
-        mark_ref[n * action_count : (n + 1) * action_count, :] = mark
+        mark_ref[n * action_count : (n + 1) * action_count, :] = offset
         local_ref[n * action_count : (n + 1) * action_count, :] = dest - owner * block_count
     mark, local = mark_ref[...], local_ref[...]
     row, lane = iota(mark.shape, 0), iota(mark.shape, 1)
@@ -85,21 +77,19 @@
         source_refs[offset - 1][...] = codes[:1, :capacity]
 
 
-def make_plan(me, dest, counts, device_count, capacity):
+def make_plan(me, dest, device_count, capacity):
     entry_count, action_count, block_count = dest.shape
     padded = 8 * pl.cdiv(entry_count * action_count, 8)
     outs = pl.pallas_call(
         functools.partial(plan_kernel, device_count),
         out_shape=[jax.ShapeDtypeStruct((1, capacity), jnp.int32)] * (2 * (device_count - 1)),
-        in_specs=[SMEM_SPEC, HBM_SPEC, HBM_SPEC],
+        in_specs=[SMEM_SPEC, VMEM_SPEC],
         out_specs=[VMEM_SPEC] * (2 * (device_count - 1)),
-        scratch_shapes=[pltpu.VMEM(dest.shape, jnp.int32), pltpu.VMEM(counts.shape, jnp.int32)]
-        + [pltpu.VMEM((padded, block_count), jnp.int32)] * 2
-        + [pltpu.SemaphoreType.DMA((2,))],
-        compiler_params=PARAMS,
-        cost_estimate=SMALL_COST,
+        scratch_shapes=[pltpu.VMEM((padded, block_count), jnp.int32)] * 2,
+        compiler_params=PARAMS,
+        cost_estimate=PLAN_COST,
         name="plan",
-    )(me, dest, counts)
+    )(me, dest)
     return outs[: device_count - 1], outs[device_count - 1 :]
 
 
@@ -211,6 +201,11 @@
     )(source, incoming, tiles, scores)
 
 
+def reciprocal(x):
+    guess = pl.reciprocal(x, approx=True)
+    return guess * (2.0 - x * guess)
+
+
 def soft_max(scores):
     largest = functools.reduce(jnp.maximum, scores)
     if len(scores) == 2:
@@ -235,22 +230,22 @@
     width = cot_ref.shape[2]
 
     def one_term(k, carry):
-        code = source_ref[0, k]
-
-        @pl.when(code >= 0)
-        def _():
-            block, action, n = unpack(code)
-            for c in range(0, width, tile_rows):
-                cols = slice(c, c + tile_rows)
+        block, action, n = unpack(jnp.maximum(source_ref[0, k], 0))
+        for c in range(0, width, tile_rows):
+            cols = slice(c, c + tile_rows)
+            if action_count == 2:
+                behind = scores_ref[block, 1 - action, :, cols] - scores_ref[block, action, :, cols]
+                power = jnp.exp(-jnp.abs(behind))
+                total, power = 1.0 + power, jnp.where(behind > 0, power, 1.0)
+            else:
                 _, powers, total = soft_max([scores_ref[block, other, :, cols] for other in range(action_count)])
                 power = powers[0]
                 for other in range(1, action_count):
                     power = jnp.where(action == other, powers[other], power)
-                grad = cot_ref[block, :, cols].astype(jnp.float32) / total * power
-                scaled_ref[:, cols] = (DISCOUNT * grad).astype(jnp.bfloat16)
-            rows = pl.ds(pl.multiple_of(k * tile_rows, tile_rows), tile_rows)
-            out_ref[rows, :] = transposed_dot(tiles_ref[block, action, n], scaled_ref[...]).astype(jnp.bfloat16)
-
+            grad = cot_ref[block, :, cols].astype(jnp.float32) * reciprocal(total) * power
+            scaled_ref[:, cols] = (DISCOUNT * grad).astype(jnp.bfloat16)
+        rows = pl.ds(pl.multiple_of(k * tile_rows, tile_rows), tile_rows)
+        out_ref[rows, :] = transposed_dot(tiles_ref[block, action, n], scaled_ref[...]).astype(jnp.bfloat16)
         return carry
 
     lax.fori_loop(0, capacity, one_term, 0)
@@ -290,53 +285,48 @@
 def score_kernel(row_count, scales, *refs):
     source_refs = refs[:row_count]
     scores_ref, tiles_ref, cot_ref, _, value_ref, scaled_ref, util_ref, taste_ref = refs[row_count : row_count + 8]
-    out_refs = refs[row_count + 8 :]
+    out_refs, (held_ref, sems) = refs[row_count + 8 : -2], refs[-2:]
     util_scale, taste_scale = scales
-    block = pl.program_id(0)
-    _, action_count, tile_rows, width = scores_ref.shape
-    states = pl.ds(pl.multiple_of(block * tile_rows, tile_rows), tile_rows)
-
-    @pl.when(block == 0)
-    def _():
-        taste_ref[...] = jnp.zeros_like(taste_ref)
-
-    sums = [jnp.zeros((tile_rows, tile_rows), jnp.float32) for _ in range(action_count)]
-    for c in range(0, width, tile_rows):
-        cols = slice(c, c + tile_rows)
-        largest, powers, total = soft_max([scores_ref[block, action, :, cols] for action in range(action_count)])
-        value_ref[:, cols] = largest + jnp.log(total)
-        ratio = cot_ref[block, :, cols].astype(jnp.float32) / total
+    block_count, action_count, tile_rows, width = scores_ref.shape
+    taste_ref[...] = jnp.zeros_like(taste_ref)
+
+    def states(block):
+        return pl.ds(pl.multiple_of(block * tile_rows, tile_rows), tile_rows)
+
+    def store(block):
+        return pltpu.make_async_copy(held_ref.at[block], value_ref.at[states(block), :], sems.at[block])
+
+    def one_block(block, carry):
+        sums = [jnp.zeros((tile_rows, tile_rows), jnp.float32) for _ in range(action_count)]
+        for c in range(0, width, tile_rows):
+            cols = slice(c, c + tile_rows)
+            largest, powers, total = soft_max([scores_ref[block, action, :, cols] for action in range(action_count)])
+            held_ref[block, :, cols] = largest + jnp.log(total)
+            ratio = cot_ref[block, :, cols].astype(jnp.float32) * reciprocal(total)
+            for action in range(action_count):
+                grad = ratio * powers[action]
+                scaled_ref[block, action, :, cols] = (DISCOUNT * grad).astype(jnp.bfloat16)
+                sums[action] = sums[action] + grad
+                taste_ref[action : action + 1, cols] += taste_scale * jnp.sum(grad, axis=0, keepdims=True)
+        store(block).start()
         for action in range(action_count):
-            grad = ratio * powers[action]
-            scaled_ref[block, action, :, cols] = (DISCOUNT * grad).astype(jnp.bfloat16)
-            sums[action] = sums[action] + grad
-            taste_ref[action : action + 1, cols] += taste_scale * jnp.sum(grad, axis=0, keepdims=True)
-    for action in range(action_count):
-        util_ref[action : action + 1, states] = util_scale * jnp.sum(sums[action].T, axis=0, keepdims=True)
-
-    @pl.when(block == pl.num_programs(0) - 1)
-    def _():
-        for source_ref, out_ref in zip(source_refs, out_refs):
-            capacity = source_ref.shape[1]
-
-            def one_term(k, carry):
-                code = source_ref[0, k]
-
-                @pl.when(code >= 0)
-                def _():
-                    block, action, n = unpack(code)
-                    rows = pl.ds(pl.multiple_of(k * tile_rows, tile_rows), tile_rows)
-                    out_ref[rows, :] = transposed_dot(tiles_ref[block, action, n], scaled_ref[block, action]).astype(
-                        jnp.bfloat16
-                    )
-
-                return carry
-
-            lax.fori_loop(0, capacity, one_term, 0)
-            rows = list(split_rows(taste_ref[...]))
-            spare = out_ref.shape[0] - capacity * tile_rows - sum(x.shape[0] for x in rows)
-            rows.append(jnp.zeros((spare, width), jnp.bfloat16))
-            out_ref[capacity * tile_rows :, :] = jnp.concatenate(rows, axis=0)
+            util_ref[action : action + 1, states(block)] = util_scale * jnp.sum(sums[action].T, axis=0, keepdims=True)
+        return carry
+
+    lax.fori_loop(0, block_count, one_block, 0)
+    for source_ref, out_ref in zip(source_refs, out_refs):
+        capacity = source_ref.shape[1]
+        for k in range(capacity):
+            block, action, n = unpack(jnp.maximum(source_ref[0, k], 0))
+            out_ref[k * tile_rows : (k + 1) * tile_rows, :] = transposed_dot(
+                tiles_ref[block, action, n], scaled_ref[block, action]
+            ).astype(jnp.bfloat16)
+        rows = list(split_rows(taste_ref[...]))
+        spare = out_ref.shape[0] - capacity * tile_rows - sum(x.shape[0] for x in rows)
+        rows.append(jnp.zeros((spare, width), jnp.bfloat16))
+        out_ref[capacity * tile_rows :, :] = jnp.concatenate(rows, axis=0)
+    for block in range(block_count):
+        store(block).wait()
 
 
 def score(sources, scores, tiles, cot_blocks, sent, scales, rows):
@@ -351,9 +341,12 @@
             jax.ShapeDtypeStruct((action_count, width), jnp.float32),
         ]
         + [jax.ShapeDtypeStruct((rows, width), jnp.bfloat16)] * len(sources),
-        grid=(block_count,),
         in_specs=[SMEM_SPEC] * len(sources) + [VMEM_SPEC] * 3 + [ANY_SPEC],
-        out_specs=[pl.BlockSpec((tile_rows, width), lambda i: (i, 0))] + [VMEM_SPEC] * (3 + len(sources)),
+        out_specs=[HBM_SPEC] + [VMEM_SPEC] * (3 + len(sources)),
+        scratch_shapes=[
+            pltpu.VMEM((block_count, tile_rows, width), jnp.float32),
+            pltpu.SemaphoreType.DMA((block_count,)),
+        ],
         compiler_params=PARAMS,
         cost_estimate=SMALL_COST,
         name="score",
@@ -508,7 +501,7 @@
         return x
 
     dest, counts = dest_block.transpose(2, 1, 0), counts.T
-    request, source = make_plan(me, dest, counts, device_count, capacity)
+    request, source = make_plan(me, dest, device_count, capacity)
     wanted = {d: shift(request[d - 1], d) for d in order}
     staged = stage(value_blocks, request[0])
     outgoing = {d: gather_blocks(wanted[d], staged) for d in order}

time: 160 us -> 157 us (0.981)
  waiting for transfers between devices: 80.7 us -> 85.9 us
  Pallas kernels: 42.3 us -> 38 us
  local copies, waits for them, and re-layouts: 3.65 us -> 0.73 us
    ppermute x10, waiting for transfers between devices: 79.5 us -> 84.7 us  [shift(): lax.ppermute(x, 'state', [(s, (s + offset) % device_count) for s in range...]
    pallas_call x1, Pallas kernels: 11.5 us -> 6.67 us  [score(): pl.pallas_call(functools.partial(score_kernel, len(sources), scales), out...]
    unnamed x20 -> x18, local copies, waits for them, and re-layouts: 3.65 us -> 0.73 us
  transfers between devices with their start and end apart: 12 -> 12, of which waited for: 5 -> 6; matrix products, arithmetic and copies ran while one was open for 0% -> 0% of each run, Pallas kernels for 22% -> 20%
where the time goes in v4:
time: 157 us
  waiting for transfers between devices  85.9 us (55%)
  Pallas kernels  38 us (24%)
  starting transfers between devices  30.6 us (19%)
    ppermute x10, waiting for transfers between devices, shift(): lax.ppermute(x, 'state', [(s, (s + offset) % device_count) for s in range...  84.7 us
    ppermute x10, starting transfers between devices, shift(): lax.ppermute(x, 'state', [(s, (s + offset) % device_count) for s in range...  29 us
    pallas_call x1, Pallas kernels, local_adjoint(): pl.pallas_call(local_adjoint_kernel, out_shape=(shape, shape), in_specs=[...  12.8 us
    pallas_call x1, Pallas kernels, local_forward(): pl.pallas_call(local_forward_kernel, out_shape=jax.ShapeDtypeStruct((bloc...  7.01 us
    pallas_call x1, Pallas kernels, score(): pl.pallas_call(functools.partial(score_kernel, len(sources), scales), out...  6.67 us
    pallas_call x2, Pallas kernels, add_arrivals(): pl.pallas_call(functools.partial(add_arrivals_kernel, count, offsets), ou...  4.53 us
    pallas_call x1, Pallas kernels, lead_terms(): pl.pallas_call(functools.partial(lead_terms_kernel, count), out_shape=(ja...  3.27 us
  transfers between devices with their start and end apart: 12, of which 6 were waited for; matrix products, arithmetic and copies ran while one was open for 0% of the time, Pallas kernels for 20%

profile of v4, /device:TPU:0, one launch (start us, length us, event | category | flops | bytes accessed | tf_op | source)
XLA Modules:
  0.0 156.7 jit_solution(8288191142439138428)
XLA Ops:
  0.6 0.0 copy-start.2
  0.6 0.7 copy-done.2
  1.3 0.9 plan.1
  2.3 5.1 %collective-permute-start.2 = (s32[1,6]{1,0:T(1,128)S(1)}, s32[1,6]{1,0:T(1,128)S(1)}, u32[]{:S(2)}, u32[]{:S(2)}) collective-permute-start(s32[1,6]{1,0:T(1,128)S(1)} %get-tuple-element.27), channel_id=1, source_target_pairs={{0,12},{4,0},{8,4},{12,8},{1,13},{5,1},{9,5},{13,9},{2,14},{6,2},{... | collective-permute-start | bytes 80 | tf_op jit(solution)/shard_map/ppermute | solution.py:491
  7.4 0.0 collective-permute-start.4
  7.4 1.0 collective-permute-start
  8.4 0.0 copy-done.1
  8.4 0.1 stage.1.value_ref
  8.5 0.0 slice-start.1
  8.5 0.0 copy-start.4
  8.5 0.0 copy-start.5
  8.6 0.0 copy-start.6
  8.6 3.2 %collective-permute-done.4.wanted_ref.refs_0_ = s32[1,6]{1,0:T(1,128)S(1)} collective-permute-done((s32[1,6]{1,0:T(1,128)S(1)}, s32[1,6]{1,0:T(1,128)S(1)}, u32[]{:S(2)}, u32[]{:S(2)}) %collective-permute-start.4) | collective-permute-done | bytes 56 | tf_op jit(solution)/shard_map/ppermute | solution.py:491
  11.8 0.6 gather.5
  12.4 0.1 collective-permute-start.5
  12.5 0.0 collective-permute-done.2.wanted_ref.refs_1_
  12.5 0.6 gather.4.sent_ref
  13.1 1.0 collective-permute-start.3
  14.1 0.0 collective-permute-done.wanted_ref.refs_0_
  14.2 0.6 gather.3
  14.8 2.9 %collective-permute-start.1 = (bf16[6,128,512]{2,1,0:T(8,128)(2,1)S(1)}, bf16[6,128,512]{2,1,0:T(8,128)(2,1)S(1)}, u32[]{:S(2)}, u32[]{:S(2)}) collective-permute-start(bf16[6,128,512]{2,1,0:T(8,128)(2,1)S(1)} %gather.3), channel_id=1, source_target_pairs={{0,12},{4,0},{8,4},{12,8},{1,13},{5,1},{9,5},{13,9},{2,14},{6,2},{... | collective-permute-start | bytes 2359304 | tf_op jit(solution)/shard_map/ppermute | solution.py:491
  17.6 0.0 slice-done
  17.6 0.0 slice-done.1
  17.6 0.0 copy-done.4
  17.7 0.0 copy-done.6
  17.7 7.0 %local_forward.1.scores_in_ref = f32[16,2,128,512]{3,2,1,0:T(8,128)S(1)} custom-call(s32[1]{0:T(128)} %bitcast.me_ref.refs_6_, s32[6,2,16]{2,1,0:T(2,128)S(1)} %bitcast.12, s32[2,16]{1,0:T(2,128)S(1)} %bitcast.14, bf16[16,128,512]{2,1,0:T(8,128)(2,1)S(1)} %stage.1.value_ref, bf16[16,2,6,128,128]{4,3,2,1,0:T(8,128)(2,1)S(1)} %bitcast.7, ...), custom_call_target="tpu_custom_call" | custom-call | flops 1000 | bytes 1000 | tf_op jit(solution)/shard_map/local_forward/pallas_call | solution.py:162
  24.7 39.7 %collective-permute-done.5.incoming_ref = bf16[6,128,512]{2,1,0:T(8,128)(2,1)S(1)} collective-permute-done((bf16[6,128,512]{2,1,0:T(8,128)(2,1)S(1)}, bf16[6,128,512]{2,1,0:T(8,128)(2,1)S(1)}, u32[]{:S(2)}, u32[]{:S(2)}) %collective-permute-start.5) | collective-permute-done | bytes 786464 | tf_op jit(solution)/shard_map/ppermute | solution.py:491
  64.4 0.9 add_incoming.1.refs_7_
  65.3 0.0 collective-permute-done.3.refs_3_
  65.3 1.2 collective-permute-done.1.refs_2_
  66.4 3.3 %lead_terms.1 = (f32[16,2,128,512]{3,2,1,0:T(8,128)S(1)}, bf16[784,512]{1,0:T(8,128)(2,1)S(1)}) custom-call(s32[1,6]{1,0:T(1,128)S(1)} %get-tuple-element.24.refs_0_, s32[1,6]{1,0:T(1,128)S(1)} %get-tuple-element.25.refs_1_, bf16[6,128,512]{2,1,0:T(8,128)(2,1)S(1)} %collective-permute-done.1.refs_2_, ...), custom_call_target="tpu_custom_call", output_to_operand_aliasing={{0}: (7, {})} | custom-call | flops 1000 | bytes 1000 | tf_op jit(solution)/shard_map/lead_terms/pallas_call | solution.py:257
  69.7 15.0 %collective-permute-start.8 = (bf16[784,512]{1,0:T(8,128)(2,1)S(1)}, bf16[784,512]{1,0:T(8,128)(2,1)S(1)}, u32[]{:S(2)}, u32[]{:S(2)}) collective-permute-start(bf16[784,512]{1,0:T(8,128)(2,1)S(1)} %get-tuple-element.31.refs_5_), channel_id=1, source_target_pairs={{0,8},{4,12},{8,0},{12,4},{1,9},{5,13},{9,1},{13,5},{2,10},{6,14},... | collective-permute-start | bytes 2408456 | tf_op jit(solution)/shard_map/ppermute | solution.py:491
  84.8 6.7 %score.1 = (f32[2048,512]{1,0:T(8,128)}, bf16[16,2,128,512]{3,2,1,0:T(8,128)(2,1)S(1)}, f32[2,2048]{1,0:T(2,128)S(1)}, f32[2,512]{1,0:T(2,128)S(1)}, bf16[784,51...) custom-call(s32[1,6]{1,0:T(1,128)S(1)} %get-tuple-element.24.refs_0_, s32[1,6]{1,0:T(1,128)S(1)} %get-tuple-element.25.refs_1_, ...), custom_call_target="tpu_custom_call" | custom-call | flops 1000 | bytes 1000 | tf_op jit(solution)/shard_map/score/pallas_call | solution.py:335
  91.4 0.3 collective-permute-start.6
  91.8 3.5 %collective-permute-start.7 = (bf16[784,512]{1,0:T(8,128)(2,1)S(1)}, bf16[784,512]{1,0:T(8,128)(2,1)S(1)}, u32[]{:S(2)}, u32[]{:S(2)}) collective-permute-start(bf16[784,512]{1,0:T(8,128)(2,1)S(1)} %get-tuple-element.34.sent_ref), channel_id=1, source_target_pairs={{0,12},{4,0},{8,4},{12,8},{1,13},{5,1},{9,5},{13,9},{2,14},{6,2},{... | collective-permute-start | bytes 2408456 | tf_op jit(solution)/shard_map/ppermute | solution.py:491
  95.3 0.0 collective-permute-start.10
  95.3 1.2 collective-permute-done.10
  96.5 1.6 collective-permute-start.11
  98.1 0.0 collective-permute-start.9
  98.1 12.8 %local_adjoint.1 = (f32[16,128,512]{2,1,0:T(8,128)S(1)}, f32[16,128,512]{2,1,0:T(8,128)}) custom-call(s32[1]{0:T(128)} %bitcast.me_ref.refs_6_, s32[6,2,16]{2,1,0:T(2,128)S(1)} %bitcast.13, s32[2,16]{1,0:T(2,128)S(1)} %bitcast.15, bf16[16,2,6,128,128]{4,3,2,1,0:T(8,128)(2,1)S(1)} %bitcast.7, bf16[16,2,128,512]{3,2,1,0:T(8,128)(2,1)S(1)} %get-tuple-element.35.scaled_ref, ...), custom_call_target="tpu_custom_call" | custom-call | flops 1000 | bytes 1000 | tf_op jit(solution)/shard_map/local_adjoint/pallas_call | solution.py:386
  110.8 0.0 collective-permute-done.11
  110.9 0.6 add.7
  111.5 26.5 %collective-permute-done.8.refs_1_ = bf16[784,512]{1,0:T(8,128)(2,1)S(1)} collective-permute-done((bf16[784,512]{1,0:T(8,128)(2,1)S(1)}, bf16[784,512]{1,0:T(8,128)(2,1)S(1)}, u32[]{:S(2)}, u32[]{:S(2)}) %collective-permute-start.8) | collective-permute-done | bytes 802848 | tf_op jit(solution)/shard_map/ppermute | solution.py:491
  138.0 1.8 %add_arrivals.2 = (f32[16,128,512]{2,1,0:T(8,128)S(1)}, f32[16,128,512]{2,1,0:T(8,128)}) custom-call(s32[1,6]{1,0:T(1,128)S(1)} %collective-permute-done.4.wanted_ref.refs_0_, bf16[784,512]{1,0:T(8,128)(2,1)S(1)} %collective-permute-done.8.refs_1_, f32[16,128,512]{2,1,0:T(8,128)S(1)} %get-tuple-element.36.refs_2_, ...), custom_call_target="tpu_custom_call", output_to_operand_aliasing={{0}: (2, {}), {1}: (3, {})} | custom-call | flops 1000 | bytes 1000 | tf_op jit(solution)/shard_map/add_arrivals/pallas_call | solution.py:466
  139.8 14.1 %collective-permute-done.9.refs_7_ = f32[2,512]{1,0:T(2,128)S(1)} collective-permute-done((f32[2,512]{1,0:T(2,128)S(1)}, f32[2,512]{1,0:T(2,128)S(1)}, u32[]{:S(2)}, u32[]{:S(2)}) %collective-permute-start.9) | collective-permute-done | bytes 4128 | tf_op jit(solution)/shard_map/ppermute | solution.py:491
  153.9 0.0 collective-permute-done.6.refs_2_
  153.9 0.0 collective-permute-done.7.refs_3_
  153.9 2.8 %add_arrivals.3 = (f32[16,128,512]{2,1,0:T(8,128)S(1)}, f32[16,128,512]{2,1,0:T(8,128)}, f32[2,512]{1,0:T(2,128)}) custom-call(s32[1,6]{1,0:T(1,128)S(1)} %collective-permute-done.wanted_ref.refs_0_, s32[1,6]{1,0:T(1,128)S(1)} %collective-permute-done.2.wanted_ref.refs_1_, ...), custom_call_target="tpu_custom_call", output_to_operand_aliasing={{0}: (4, {}), {1}: (5, {})} | custom-call | flops 1000 | bytes 1000 | tf_op jit(solution)/shard_map/add_arrivals/pallas_call | solution.py:466
  (9 shorter events, 0.0 us)
Async XLA Ops:
  0.6 0.7 copy-start.2
  1.3 7.1 %copy-start.1 = (bf16[2048,512]{1,0:T(8,128)(2,1)S(1)}, bf16[2048,512]{1,0:T(8,128)(2,1)}, u32[]{:S(2)}) copy-start(bf16[2048,512]{1,0:T(8,128)(2,1)} %param.7) | copy-start | bytes 6291460
  2.3 10.2 %collective-permute-start.2 = (s32[1,6]{1,0:T(1,128)S(1)}, s32[1,6]{1,0:T(1,128)S(1)}, u32[]{:S(2)}, u32[]{:S(2)}) collective-permute-start(s32[1,6]{1,0:T(1,128)S(1)} %get-tuple-element.27), channel_id=1, source_target_pairs={{0,12},{4,0},{8,4},{12,8},{1,13},{5,1},{9,5},{13,9},{2,14},{6,2},{... | collective-permute-start | bytes 80 | tf_op jit(solution)/shard_map/ppermute | solution.py:491
  7.4 4.4 %collective-permute-start.4 = (s32[1,6]{1,0:T(1,128)S(1)}, s32[1,6]{1,0:T(1,128)S(1)}, u32[]{:S(2)}, u32[]{:S(2)}) collective-permute-start(s32[1,6]{1,0:T(1,128)S(1)} %get-tuple-element.29), channel_id=1, source_target_pairs={{0,8},{4,12},{8,0},{12,4},{1,9},{5,13},{9,1},{13,5},{2,10},{6,14},... | collective-permute-start | bytes 80 | tf_op jit(solution)/shard_map/ppermute | solution.py:491
  7.4 6.8 %collective-permute-start = (s32[1,6]{1,0:T(1,128)S(1)}, s32[1,6]{1,0:T(1,128)S(1)}, u32[]{:S(2)}, u32[]{:S(2)}) collective-permute-start(s32[1,6]{1,0:T(1,128)S(1)} %get-tuple-element.26.plan_ref), channel_id=1, source_target_pairs={{0,4},{4,8},{8,12},{12,0},{1,5},{5,9},{9,13},{13,1},{2,6},{6,10},{... | collective-permute-start | bytes 80 | tf_op jit(solution)/shard_map/ppermute | solution.py:491
  8.4 9.3 %slice-start = ((s8[6291456]{0:T(1024)(128)(4,1)}), s8[4194304]{0:T(1024)(128)(4,1)S(1)}, s32[]{:S(2)}) async-start(s8[6291456]{0:T(1024)(128)(4,1)} %bitcast.6), calls=%async_computation | async-start | bytes 8388608
  8.5 9.1 %slice-start.1 = ((s8[6291456]{0:T(1024)(128)(4,1)}), s8[2097152]{0:T(1024)(128)(4,1)S(1)}, s32[]{:S(2)}) async-start(s8[6291456]{0:T(1024)(128)(4,1)} %bitcast.6), calls=%async_computation.1 | async-start | bytes 4194304
  8.5 9.1 %copy-start.4 = (f32[2,2048]{1,0:T(2,128)S(1)}, f32[2,2048]{1,0:T(2,128)}, u32[]{:S(2)}) copy-start(f32[2,2048]{1,0:T(2,128)} %util_ref.1) | copy-start | bytes 49156
  8.5 9.1 %copy-start.5 = (f32[2,512]{1,0:T(2,128)S(1)}, f32[2,512]{1,0:T(2,128)}, u32[]{:S(2)}) copy-start(f32[2,512]{1,0:T(2,128)} %taste_ref.1) | copy-start | bytes 12292
  8.6 9.1 %copy-start.6 = (s32[16,2]{0,1:T(2,128)S(1)}, s32[16,2]{0,1:T(2,128)}, u32[]{:S(2)}) copy-start(s32[16,2]{0,1:T(2,128)} %param.13) | copy-start | bytes 388
  12.4 51.9 %collective-permute-start.5 = (bf16[6,128,512]{2,1,0:T(8,128)(2,1)S(1)}, bf16[6,128,512]{2,1,0:T(8,128)(2,1)S(1)}, u32[]{:S(2)}, u32[]{:S(2)}) collective-permute-start(bf16[6,128,512]{2,1,0:T(8,128)(2,1)S(1)} %gather.5), channel_id=1, source_target_pairs={{0,8},{4,12},{8,0},{12,4},{1,9},{5,13},{9,1},{13,5},{2,10},{6,14},... | collective-permute-start | bytes 2359304 | tf_op jit(solution)/shard_map/ppermute | solution.py:491
  13.1 52.2 %collective-permute-start.3 = (bf16[6,128,512]{2,1,0:T(8,128)(2,1)S(1)}, bf16[6,128,512]{2,1,0:T(8,128)(2,1)S(1)}, u32[]{:S(2)}, u32[]{:S(2)}) collective-permute-start(bf16[6,128,512]{2,1,0:T(8,128)(2,1)S(1)} %gather.4.sent_ref), channel_id=1, source_target_pairs={{0,4},{4,8},{8,12},{12,0},{1,5},{5,9},{9,13},{13,1},{2,6},{6,10},{... | collective-permute-start | bytes 2359304 | tf_op jit(solution)/shard_map/ppermute | solution.py:491
  14.8 51.7 %collective-permute-start.1 = (bf16[6,128,512]{2,1,0:T(8,128)(2,1)S(1)}, bf16[6,128,512]{2,1,0:T(8,128)(2,1)S(1)}, u32[]{:S(2)}, u32[]{:S(2)}) collective-permute-start(bf16[6,128,512]{2,1,0:T(8,128)(2,1)S(1)} %gather.3), channel_id=1, source_target_pairs={{0,12},{4,0},{8,4},{12,8},{1,13},{5,1},{9,5},{13,9},{2,14},{6,2},{... | collective-permute-start | bytes 2359304 | tf_op jit(solution)/shard_map/ppermute | solution.py:491
  64.4 2.1 %copy-start = (bf16[2048,512]{1,0:T(8,128)(2,1)S(1)}, bf16[2048,512]{1,0:T(8,128)(2,1)}, u32[]{:S(2)}) copy-start(bf16[2048,512]{1,0:T(8,128)(2,1)} %param.8) | copy-start | bytes 6291460
  69.7 68.3 %collective-permute-start.8 = (bf16[784,512]{1,0:T(8,128)(2,1)S(1)}, bf16[784,512]{1,0:T(8,128)(2,1)S(1)}, u32[]{:S(2)}, u32[]{:S(2)}) collective-permute-start(bf16[784,512]{1,0:T(8,128)(2,1)S(1)} %get-tuple-element.31.refs_5_), channel_id=1, source_target_pairs={{0,8},{4,12},{8,0},{12,4},{1,9},{5,13},{9,1},{13,5},{2,10},{6,14},... | collective-permute-start | bytes 2408456 | tf_op jit(solution)/shard_map/ppermute | solution.py:491
  84.8 13.3 %copy-start.3 = (s32[16,2,6]{0,1,2:T(2,128)S(1)}, s32[16,2,6]{0,1,2:T(2,128)}, u32[]{:S(2)}) copy-start(s32[16,2,6]{0,1,2:T(2,128)} %param.12) | copy-start | bytes 2308
  91.4 62.5 %collective-permute-start.6 = (bf16[784,512]{1,0:T(8,128)(2,1)S(1)}, bf16[784,512]{1,0:T(8,128)(2,1)S(1)}, u32[]{:S(2)}, u32[]{:S(2)}) collective-permute-start(bf16[784,512]{1,0:T(8,128)(2,1)S(1)} %get-tuple-element.33), channel_id=1, source_target_pairs={{0,4},{4,8},{8,12},{12,0},{1,5},{5,9},{9,13},{13,1},{2,6},{6,10},{... | collective-permute-start | bytes 2408456 | tf_op jit(solution)/shard_map/ppermute | solution.py:491
  91.8 62.1 %collective-permute-start.7 = (bf16[784,512]{1,0:T(8,128)(2,1)S(1)}, bf16[784,512]{1,0:T(8,128)(2,1)S(1)}, u32[]{:S(2)}, u32[]{:S(2)}) collective-permute-start(bf16[784,512]{1,0:T(8,128)(2,1)S(1)} %get-tuple-element.34.sent_ref), channel_id=1, source_target_pairs={{0,12},{4,0},{8,4},{12,8},{1,13},{5,1},{9,5},{13,9},{2,14},{6,2},{... | collective-permute-start | bytes 2408456 | tf_op jit(solution)/shard_map/ppermute | solution.py:491
  95.3 1.2 collective-permute-start.10
  96.5 14.3 %collective-permute-start.11 = (f32[2,2048]{1,0:T(2,128)S(1)}, f32[2,2048]{1,0:T(2,128)S(1)}, u32[]{:S(2)}, u32[]{:S(2)}) collective-permute-start(f32[2,2048]{1,0:T(2,128)S(1)} %add.6), channel_id=1, source_target_pairs={{0,2},{1,3},{2,0},{3,1},{4,6},{5,7},{6,4},{7,5},{8,10},{9,11},{10,... | collective-permute-start | bytes 49160 | tf_op jit(solution)/shard_map/ppermute | solution.py:499
  98.1 55.9 %collective-permute-start.9 = (f32[2,512]{1,0:T(2,128)S(1)}, f32[2,512]{1,0:T(2,128)S(1)}, u32[]{:S(2)}, u32[]{:S(2)}) collective-permute-start(f32[2,512]{1,0:T(2,128)S(1)} %get-tuple-element.40.refs_8_), channel_id=1, source_target_pairs={{0,8},{4,12},{8,0},{12,4},{1,9},{5,13},{9,1},{13,5},{2,10},{6,14},... | collective-permute-start | bytes 12296 | tf_op jit(solution)/shard_map/ppermute | solution.py:491
